TPU v7x, 32 devices: a whole 2x2x4 slice. The times are simulated.
32 devices in a mesh: parts: 2 (over x), node: 4 (over z), expert: 4 (over y, core).
Axes of the slice: x: 2, y: 2, z: 4, core: 2. Of those that a mesh axis runs over, the one named last changes fastest.
Arguments:
- hidden_in: bfloat16 [1024, 3584], P(('parts', 'node'), 'expert'), parts along dimension 0, may hold values from -6 to 6
- out_grad: bfloat16 [1024, 3584], P(('parts', 'node'), 'expert'), parts along dimension 0, may hold values from -0.59765625 to 0.59765625
- expert_ids: int32 [1024, 2], P(('parts', 'node')), parts along dimension 0, may hold values from 0 to 3, all different within a row; in each aligned block of 128 rows (0 to 127, 128 to 255, ...) at most 64 rows name the same one
- gate_weights: bfloat16 [1024, 2], P(('parts', 'node')), parts along dimension 0, may hold values from 0.099609375 to 1
- w_gate: bfloat16 [4, 2432, 3584], P('node', 'expert'), may hold values from -0.09375 to 0.09375
- w_up: bfloat16 [4, 2432, 3584], P('node', 'expert'), may hold values from -0.09375 to 0.09375
- w_down: bfloat16 [4, 2432, 3584], P('node', 'expert'), may hold values from -0.125 to 0.125
Outputs:
- grad_in: bfloat16 [1024, 3584], P(('parts', 'node'), 'expert'), parts along dimension 0
- grad_gates: float32 [1024, 2], P(('parts', 'node')), parts along dimension 0
- grad_gate: bfloat16 [8, 2432, 3584], P(('parts', 'node'), 'expert'), parts along dimension 0
- grad_up: bfloat16 [8, 2432, 3584], P(('parts', 'node'), 'expert'), parts along dimension 0
- grad_down: bfloat16 [8, 2432, 3584], P(('parts', 'node'), 'expert'), parts along dimension 0
There are 2 independent parts, one for each index of `parts`. A program takes and returns all parts, laid end to end along the dimension named above; an argument that names none is the same for every part. Nothing has to cross between parts.
Inputs may be any that keep to these rules, and one draw needn't show every extreme that they name: `expert_ids`: each row names two different experts. Among the 128 tokens of one node group no expert is named more than 64 times, a bound that some block reaches.
All inputs are finite; a program needn't handle non-finite values.
Results may differ from a plain program's by a relative error of at most 0.0051.
Values may be sent and summed in bfloat16 or wider, within the bound.
No kernel may reach another device: no remote copies, remote signals or barrier semaphores. Data moves between devices by JAX's collectives and lax.ppermute only.
A program may use at most 128 MiB of HBM per device.

v0:
```python
import jax
import jax.numpy as jnp
from jax import lax
from jax.sharding import PartitionSpec as P


def contract_rows(left, right):
    return lax.dot_general(
        left, right, (((0,), (0,)), ((), ())), preferred_element_type=jnp.float32
    )


def contract_cols(left, right):
    return lax.dot_general(
        left, right, (((1,), (1,)), ((), ())), preferred_element_type=jnp.float32
    )


def expert_backward(rows_in, rows_grad, row_weight, gate_mat, up_mat, down_mat):
    gate_pre = contract_cols(rows_in, gate_mat)
    up_pre = contract_cols(rows_in, up_mat)
    sigmoid_gate = jax.nn.sigmoid(gate_pre)
    silu_gate = gate_pre * sigmoid_gate
    hidden = silu_gate * up_pre
    back_hidden = contract_cols(rows_grad, down_mat)
    statistic = jnp.sum(hidden * back_hidden, axis=1)
    scaled = row_weight[:, None] * back_hidden
    grad_gate_pre = (
        scaled * up_pre * sigmoid_gate * (1.0 + gate_pre * (1.0 - sigmoid_gate))
    ).astype(jnp.bfloat16)
    grad_up_pre = (scaled * silu_gate).astype(jnp.bfloat16)
    weighted_hidden = (row_weight[:, None] * hidden).astype(jnp.bfloat16)
    grad_down = contract_rows(weighted_hidden, rows_grad).astype(jnp.bfloat16)
    grad_gate = contract_rows(grad_gate_pre, rows_in).astype(jnp.bfloat16)
    grad_up = contract_rows(grad_up_pre, rows_in).astype(jnp.bfloat16)
    return (grad_gate, grad_up, grad_down, grad_gate_pre, grad_up_pre, statistic)


def local(hidden_in, out_grad, expert_ids, gate_weights, w_gate, w_up, w_down):
    groups = lax.axis_size("node")
    count_tok = hidden_in.shape[0]
    capacity = count_tok // 2
    group_ids = jnp.arange(groups, dtype=jnp.int32)
    member = expert_ids[:, :, None] == group_ids[None, None, :]
    routed = jnp.any(member, axis=1)
    routed_int = routed.astype(jnp.int32)
    position = jnp.cumsum(routed_int, axis=0) - routed_int
    weight_of = jnp.sum(
        jnp.where(member, gate_weights[:, :, None].astype(jnp.float32), jnp.float32(0.0)), axis=1
    )
    slot_ids = jnp.arange(capacity, dtype=jnp.int32)
    landing = routed[:, :, None] & (position[:, :, None] == slot_ids[None, None, :])
    token_of = jnp.sum(
        jnp.where(landing, jnp.arange(count_tok, dtype=jnp.int32)[:, None, None], 0), axis=0
    )
    filled = jnp.any(landing, axis=0)
    send_weight = jnp.where(
        filled, weight_of[token_of, group_ids[:, None]], jnp.float32(0.0)
    ).astype(jnp.bfloat16)

    def pack_rows(source):
        return jnp.where(filled[:, :, None], source[token_of], jnp.zeros((), source.dtype))

    slice_in, slice_grad, recv_weight = (
        lax.all_to_all(pack_rows(hidden_in), "node", split_axis=0, concat_axis=0, tiled=True),
        lax.all_to_all(pack_rows(out_grad), "node", split_axis=0, concat_axis=0, tiled=True),
        lax.all_to_all(send_weight, "node", split_axis=0, concat_axis=0, tiled=True),
    )
    rows_in, rows_grad = (
        lax.all_gather(slice_in, "expert", axis=2, tiled=True),
        lax.all_gather(slice_grad, "expert", axis=2, tiled=True),
    )
    total_rows = groups * capacity
    features = rows_in.shape[2]
    row_weight = recv_weight.reshape(total_rows).astype(jnp.float32)
    gate_mat = w_gate[0]
    up_mat = w_up[0]
    grad_gate, grad_up, grad_down, grad_gate_pre, grad_up_pre, statistic = expert_backward(
        rows_in.reshape(total_rows, features),
        rows_grad.reshape(total_rows, features),
        row_weight,
        gate_mat,
        up_mat,
        w_down[0],
    )
    input_part = jnp.dot(grad_gate_pre, gate_mat, preferred_element_type=jnp.float32) + jnp.dot(
        grad_up_pre, up_mat, preferred_element_type=jnp.float32
    )
    input_slice = lax.psum_scatter(input_part, "expert", scatter_dimension=1, tiled=True)
    stat_total = lax.psum(statistic, "expert")
    slice_width = input_slice.shape[1]
    back_input, back_stat = (
        lax.all_to_all(
            input_slice.reshape(groups, capacity, slice_width),
            "node",
            split_axis=0,
            concat_axis=0,
            tiled=True,
        ),
        lax.all_to_all(
            stat_total.reshape(groups, capacity), "node", split_axis=0, concat_axis=0, tiled=True
        ),
    )
    flat_input = back_input.reshape(total_rows, slice_width)
    flat_stat = back_stat.reshape(total_rows)
    flat_index = expert_ids * capacity + jnp.take_along_axis(position, expert_ids, axis=1)
    grad_in = (flat_input[flat_index[:, 0]] + flat_input[flat_index[:, 1]]).astype(jnp.bfloat16)
    grad_gates = flat_stat[flat_index]
    return (grad_in, grad_gates, grad_gate[None], grad_up[None], grad_down[None])


def solution(mesh):
    return jax.shard_map(
        local,
        mesh=mesh,
        in_specs=(
            P(("parts", "node"), "expert"),
            P(("parts", "node"), "expert"),
            P(("parts", "node"), None),
            P(("parts", "node"), None),
            P("node", "expert", None),
            P("node", "expert", None),
            P("node", "expert", None),
        ),
        out_specs=(
            P(("parts", "node"), "expert"),
            P(("parts", "node"), None),
            P(("parts", "node"), "expert", None),
            P(("parts", "node"), "expert", None),
            P(("parts", "node"), "expert", None),
        ),
        check_vma=False,
    )
```

profile of v0, /device:TPU:0, one launch (start us, length us, event | category | flops | bytes accessed | tf_op | source)
XLA Modules:
  0.0 165.9 jit_solution(12337213814300599144)
XLA Ops:
  8.8 1.2 gather_fusion.2
  10.1 1.2 gather_fusion.1
  11.4 19.3 %all_to_all.30 = bf16[4,64,896]{2,1,0:T(8,128)(2,1)} all-to-all(bf16[4,64,896]{2,1,0:T(8,128)(2,1)S(1)} %get-tuple-element.50), channel_id=1, replica_groups=mesh['parts'=2,'node'=4,'expert'=4] {'node'}, dimensions={0} | all-to-all | bytes 917504 | tf_op jit(solution)/shard_map/all_to_all | solution.py:65
  30.8 15.6 %all_to_all.31 = bf16[4,64,896]{2,1,0:T(8,128)(2,1)} all-to-all(bf16[4,64,896]{2,1,0:T(8,128)(2,1)S(1)} %get-tuple-element.49), channel_id=1, replica_groups=mesh['parts'=2,'node'=4,'expert'=4] {'node'}, dimensions={0} | all-to-all | bytes 917504 | tf_op jit(solution)/shard_map/all_to_all | solution.py:66
  46.6 2.4 %gather_fusion = bf16[256]{0:T(256)(128)(2,1)S(1)} fusion(bf16[128,4]{0,1:T(4,128)(2,1)S(1)} %select_reduce_fusion.1, s32[256]{0:T(256)S(1)} %reshape.100), kind=kCustom, calls=%fused_computation | custom fusion | bytes 3072 | tf_op jit(solution)/shard_map/gather | solution.py:58
  49.1 8.1 %all_to_all.32 = bf16[4,1,64]{2,1,0:T(2,128)(2,1)S(1)} all-to-all(bf16[4,1,64]{2,1,0:T(2,128)(2,1)S(1)} %copy.83), channel_id=1, replica_groups=mesh['parts'=2,'node'=4,'expert'=4] {'node'}, dimensions={0} | all-to-all | bytes 1024 | tf_op jit(solution)/shard_map/all_to_all | solution.py:67
  57.3 4.5 %fusion.5 = f32[256,608]{0,1:T(8,128)S(1)} fusion(bf16[256,3584]{1,0:T(8,128)(2,1)} %bitcast.57, bf16[1,608,3584]{2,1,0:T(8,128)(2,1)} %param.11), kind=kOutput, calls=%fused_computation.16 | convolution fusion | flops 1115684864 | bytes 6815744 | tf_op jit(solution)/shard_map/dot_general | solution.py:14
  61.8 4.6 %fusion.8 = f32[256,608]{0,1:T(8,128)} fusion(bf16[256,3584]{1,0:T(8,128)(2,1)S(1)} %bitcast.58, bf16[1,608,3584]{2,1,0:T(8,128)(2,1)} %param.12), kind=kOutput, calls=%fused_computation.19 | convolution fusion | flops 1115684864 | bytes 6815744 | tf_op jit(solution)/shard_map/dot_general | solution.py:14
  66.5 7.4 %all-gather.3.cloned.1.call-done = bf16[4,64,3584]{2,1,0:T(8,128)(2,1)} async-done(((bf16[4,64,896]{2,1,0:T(8,128)(2,1)}), bf16[4,64,3584]{2,1,0:T(8,128)(2,1)}) %all-gather.3.cloned.1.call-update) | async-done | bytes 1835024 | tf_op jit(solution)/shard_map/all_gather | solution.py:71
  73.9 4.4 %multiply_reduce_fusion = (f32[256]{0:T(256)S(1)}, bf16[256,608]{0,1:T(8,128)(2,1)S(1)}, bf16[256,608]{0,1:T(8,128)(2,1)S(1)}) fusion(f32[256,608]{0,1:T(8,128)} %fusion.8, f32[256,608]{0,1:T(8,128)S(1)} %fusion.5, f32[256]{0:T(256)S(1)} %reshape.99, bf16[256,3584]{1,0:T(8,128)(2,1)} %bitcast.63, bf16[1,608,3584]{2,1,0:T(8,128)(2,1)} %param.13), kind=kOutput, calls=%fused_computation.24 | convolution fusion | flops 1118330624 | bytes 8062976 | tf_op jit(solution)/shard_map/dot_general | solution.py:14
  78.3 4.0 %fusion.3 = f32[256,3584]{1,0:T(8,128)S(1)} fusion(bf16[256,608]{0,1:T(8,128)(2,1)S(1)} %get-tuple-element.43, bf16[1,608,3584]{2,1,0:T(8,128)(2,1)} %param.11), kind=kOutput, calls=%fused_computation.14 | convolution fusion | flops 1115684864 | bytes 8339456 | tf_op jit(solution)/shard_map/dot_general | solution.py:86
  82.3 5.8 %convolution_add_fusion = f32[256,3584]{1,0:T(8,128)} fusion(f32[256,3584]{1,0:T(8,128)S(1)} %fusion.3, bf16[256,608]{0,1:T(8,128)(2,1)S(1)} %get-tuple-element.44, bf16[1,608,3584]{2,1,0:T(8,128)(2,1)} %param.12), kind=kOutput, calls=%fused_computation.13 | convolution fusion | flops 1116602368 | bytes 12009472 | tf_op jit(solution)/shard_map/dot_general | solution.py:86
  88.2 6.4 %psum.7 = f32[4,1,64]{2,1,0:T(1,128)} all-reduce(f32[4,1,64]{2,1,0:T(1,128)S(1)} %all_to_all.23), channel_id=1, replica_groups=mesh['parts'=2,'node'=4,'expert'=4] {'expert'}, use_global_device_ids=true, to_apply=%region_7.8 | all-reduce | flops 256 | bytes 2048 | tf_op jit(solution)/shard_map/psum | solution.py:90
  94.6 4.8 %all-to-all-start.4 = ((f32[4,1,64]{2,1,0:T(1,128)}), f32[4,1,64]{2,1,0:T(1,128)S(1)}, u32[]{:S(2)}, u32[]{:S(2)}) async-start(f32[4,1,64]{2,1,0:T(1,128)} %psum.7), calls=%async_computation.5 | async-start | bytes 4096 | tf_op jit(solution)/shard_map/all_to_all | solution.py:100
  99.7 1.9 %gather_fusion.6 = s32[256]{0:T(256)S(1)} fusion(s32[128,4]{1,0:T(8,128)S(1)} %sub.10, s32[256]{0:T(256)S(1)} %reshape.146), kind=kCustom, calls=%fused_computation.6 | custom fusion | bytes 4096 | tf_op jit(solution)/shard_map/jit(take_along_axis)/gather | solution.py:106
  101.8 3.0 %all-to-all-done.4 = f32[4,1,64]{2,1,0:T(1,128)S(1)} async-done(((f32[4,1,64]{2,1,0:T(1,128)}), f32[4,1,64]{2,1,0:T(1,128)S(1)}, u32[]{:S(2)}, u32[]{:S(2)}) %all-to-all-start.4) | async-done | bytes 1056 | tf_op jit(solution)/shard_map/all_to_all | solution.py:100
  104.9 24.7 %reduce-scatter.2.cloned.1.call-done = f32[256,896]{1,0:T(8,128)} async-done(((f32[256,3584]{1,0:T(8,128)}), f32[256,896]{1,0:T(8,128)}) %reduce-scatter.2.cloned.1.call-update) | async-done | bytes 917520 | tf_op jit(solution)/shard_map/reduce_scatter | solution.py:89
  129.5 4.6 %all-to-all-start.3 = ((f32[4,64,896]{2,1,0:T(8,128)}), f32[4,64,896]{2,1,0:T(8,128)S(1)}, u32[]{:S(2)}, u32[]{:S(2)}) async-start(f32[4,64,896]{2,1,0:T(8,128)} %bitcast.65), calls=%async_computation.4 | async-start | bytes 1835008 | tf_op jit(solution)/shard_map/all_to_all | solution.py:93
  134.4 4.3 %fusion.1 = bf16[1,608,3584]{2,1,0:T(8,128)(2,1)} fusion(bf16[256,608]{0,1:T(8,128)(2,1)} %copy-done.3, bf16[256,3584]{1,0:T(8,128)(2,1)S(1)} %bitcast.59), kind=kOutput, calls=%fused_computation.11 | convolution fusion | flops 1117863936 | bytes 6504448 | tf_op jit(solution)/shard_map/dot_general | solution.py:8
  138.8 3.4 %fusion = bf16[1,608,3584]{2,1,0:T(8,128)(2,1)} fusion(bf16[256,608]{0,1:T(8,128)(2,1)S(1)} %get-tuple-element.43, bf16[256,3584]{1,0:T(8,128)(2,1)S(1)} %bitcast.60), kind=kOutput, calls=%fused_computation.10 | convolution fusion | flops 1117863936 | bytes 6504448 | tf_op jit(solution)/shard_map/dot_general | solution.py:8
  142.1 3.4 %fusion.2 = bf16[1,608,3584]{2,1,0:T(8,128)(2,1)} fusion(bf16[256,3584]{1,0:T(8,128)(2,1)S(1)} %bitcast.64, f32[256]{0:T(256)S(1)} %reshape.99, f32[256,608]{0,1:T(8,128)S(1)} %copy-done.7, f32[256,608]{0,1:T(8,128)S(1)} %copy-done.6), kind=kOutput, calls=%fused_computation.12 | convolution fusion | flops 1118953472 | bytes 7439360 | tf_op jit(solution)/shard_map/dot_general | solution.py:8
  146.8 1.9 %gather_fusion.5 = f32[256]{0:T(256)S(1)} fusion(f32[256]{0:T(256)S(1)} %reshape.98, s32[1024]{0:T(1024)S(1)} %pad_clamp_fusion), kind=kCustom, calls=%fused_computation.5 | custom fusion | bytes 3072 | tf_op jit(solution)/shard_map/gather | solution.py:108
  149.5 7.5 %all-to-all-done.3 = f32[4,64,896]{2,1,0:T(8,128)S(1)} async-done(((f32[4,64,896]{2,1,0:T(8,128)}), f32[4,64,896]{2,1,0:T(8,128)S(1)}, u32[]{:S(2)}, u32[]{:S(2)}) %all-to-all-start.3) | async-done | bytes 917536 | tf_op jit(solution)/shard_map/all_to_all | solution.py:93
  157.8 0.8 gather_fusion.3
  (66 shorter events, 6.7 us)
Async XLA Ops:
  7.2 1.7 copy-start
  7.2 2.8 %copy-start.1 = (bf16[128,896]{1,0:T(8,128)(2,1)S(1)}, bf16[128,896]{1,0:T(8,128)(2,1)}, u32[]{:S(2)}) copy-start(bf16[128,896]{1,0:T(8,128)(2,1)} %param.8) | copy-start | bytes 688132
  7.2 50.1 %all-gather.5.cloned.1.call-start = ((), (), s32[]{:S(2)}) async-start(), calls=%async_computation.7 | async-start | bytes 2293760 | tf_op jit(solution)/shard_map/all_gather | solution.py:70
  10.0 36.5 %copy-start.9 = (bf16[128,2]{0,1:T(2,128)(2,1)S(1)}, bf16[128,2]{0,1:T(2,128)(2,1)}, u32[]{:S(2)}) copy-start(bf16[128,2]{0,1:T(2,128)(2,1)} %param.10) | copy-start | bytes 1540
  10.0 36.6 %copy-start.8 = (s32[128,2]{0,1:T(2,128)S(1)}, s32[128,2]{0,1:T(2,128)}, u32[]{:S(2)}) copy-start(s32[128,2]{0,1:T(2,128)} %param.9) | copy-start | bytes 3076
  30.8 43.1 %all-gather.3.cloned.1.call-start = ((), (), s32[]{:S(2)}) async-start(), calls=%async_computation.6 | async-start | bytes 2293760 | tf_op jit(solution)/shard_map/all_gather | solution.py:71
  46.4 83.1 %reduce-scatter.2.cloned.1.call-start = ((), (), s32[]{:S(2)}) async-start(), calls=%async_computation.8 | async-start | bytes 4587520 | tf_op jit(solution)/shard_map/reduce_scatter | solution.py:89
  57.3 4.5 %copy-start.2 = (bf16[4,64,3584]{2,1,0:T(8,128)(2,1)S(1)}, bf16[4,64,3584]{2,1,0:T(8,128)(2,1)}, u32[]{:S(2)}) copy-start(bf16[4,64,3584]{2,1,0:T(8,128)(2,1)} %all-gather.5.cloned.1.call-done) | copy-start | bytes 5505028
  61.8 16.5 %copy-start.5 = (f32[256,608]{0,1:T(8,128)}, f32[256,608]{0,1:T(8,128)S(1)}, u32[]{:S(2)}) copy-start(f32[256,608]{0,1:T(8,128)S(1)} %fusion.5) | copy-start | bytes 1867780
  78.3 4.0 %copy-start.3 = (bf16[256,608]{0,1:T(8,128)(2,1)}, bf16[256,608]{0,1:T(8,128)(2,1)S(1)}, u32[]{:S(2)}) copy-start(bf16[256,608]{0,1:T(8,128)(2,1)S(1)} %get-tuple-element.44) | copy-start | bytes 933892
  94.6 10.2 %all-to-all-start.4 = ((f32[4,1,64]{2,1,0:T(1,128)}), f32[4,1,64]{2,1,0:T(1,128)S(1)}, u32[]{:S(2)}, u32[]{:S(2)}) async-start(f32[4,1,64]{2,1,0:T(1,128)} %psum.7), calls=%async_computation.5 | async-start | bytes 4096 | tf_op jit(solution)/shard_map/all_to_all | solution.py:100
  129.5 27.5 %all-to-all-start.3 = ((f32[4,64,896]{2,1,0:T(8,128)}), f32[4,64,896]{2,1,0:T(8,128)S(1)}, u32[]{:S(2)}, u32[]{:S(2)}) async-start(f32[4,64,896]{2,1,0:T(8,128)} %bitcast.65), calls=%async_computation.4 | async-start | bytes 1835008 | tf_op jit(solution)/shard_map/all_to_all | solution.py:93
  138.8 3.4 %copy-start.4 = (bf16[4,64,3584]{2,1,0:T(8,128)(2,1)S(1)}, bf16[4,64,3584]{2,1,0:T(8,128)(2,1)}, u32[]{:S(2)}) copy-start(bf16[4,64,3584]{2,1,0:T(8,128)(2,1)} %all-gather.3.cloned.1.call-done) | copy-start | bytes 5505028
  138.8 3.4 %copy-start.6 = (f32[256,608]{0,1:T(8,128)S(1)}, f32[256,608]{0,1:T(8,128)}, u32[]{:S(2)}) copy-start(f32[256,608]{0,1:T(8,128)} %copy-done.5) | copy-start | bytes 1867780
  138.8 3.4 %copy-start.7 = (f32[256,608]{0,1:T(8,128)S(1)}, f32[256,608]{0,1:T(8,128)}, u32[]{:S(2)}) copy-start(f32[256,608]{0,1:T(8,128)} %fusion.8) | copy-start | bytes 1867780
Sparse Core Ops, SparseCore 0:
  30.9 20.2 all-gather.4
  52.7 21.1 all-gather.2
  88.2 41.2 reduce-scatter.1
where the time goes:
time: 166 us
  blocking collectives  49.4 us (30%)
  waiting for transfers between devices  42.6 us (26%)
  matrix products  34.5 us (21%)
  between operations  14 us (8%)
  local copies, waits for them, and re-layouts  13 us (8%)
  starting transfers between devices  9.48 us (6%)
  other arithmetic  2.95 us (2%)
    reduce_scatter x1, waiting for transfers between devices, local(): lax.psum_scatter(input_part, 'expert', scatter_dimension=1, tiled=True)  24.7 us
    all_to_all x1, blocking collectives, local(): lax.all_to_all(pack_rows(hidden_in), 'node', split_axis=0, concat_axis=0,...  19.3 us
    all_to_all x1, blocking collectives, local(): lax.all_to_all(pack_rows(out_grad), 'node', split_axis=0, concat_axis=0,...  15.6 us
    dot_general x3, matrix products, contract_cols(): lax.dot_general(left, right, (((1,), (1,)), ((), ())), preferred_element_...  13.6 us
    dot_general x3, matrix products, contract_rows(): lax.dot_general(left, right, (((0,), (0,)), ((), ())), preferred_element_...  11.1 us
    all_to_all x1, blocking collectives, local(): lax.all_to_all(send_weight, 'node', split_axis=0, concat_axis=0, tiled=True)  8.07 us
    all_to_all x1, waiting for transfers between devices, local(): lax.all_to_all(input_slice.reshape(groups, capacity, slice_width), 'node'...  7.47 us
    all_gather x1, waiting for transfers between devices, local(): lax.all_gather(slice_grad, 'expert', axis=2, tiled=True)  7.41 us
  transfers between devices with their start and end apart: 5, of which 4 were waited for; matrix products, arithmetic and copies ran while one was open for 18% of the time, Pallas kernels for 0%

commit v1 on v0

--- a/solution.py
+++ b/solution.py
@@ -1,7 +1,245 @@
+import functools
+
 import jax
 import jax.numpy as jnp
 from jax import lax
+from jax.experimental import pallas as pl
+from jax.experimental.pallas import tpu as pltpu
 from jax.sharding import PartitionSpec as P
+
+BF16 = jnp.bfloat16
+F32 = jnp.float32
+
+
+def dot_nt(left, right):
+    return lax.dot_general(left, right, (((1,), (1,)), ((), ())), preferred_element_type=F32)
+
+
+def dot_tn(left, right):
+    return lax.dot_general(left, right, (((0,), (0,)), ((), ())), preferred_element_type=F32)
+
+
+def dot_nn(left, right):
+    return lax.dot_general(left, right, (((1,), (0,)), ((), ())), preferred_element_type=F32)
+
+
+def call(kernel, outs, *args, flops=0, nbytes=0, vmem=24 << 20, scratch=(), fast=()):
+    args = [
+        pltpu.with_memory_space_constraint(a, pltpu.VMEM) if i in fast else a
+        for i, a in enumerate(args)
+    ]
+    return pl.pallas_call(
+        kernel,
+        out_shape=outs,
+        in_specs=[pl.BlockSpec(memory_space=pltpu.VMEM)] * len(args),
+        out_specs=[pl.BlockSpec(memory_space=pltpu.VMEM)] * len(outs),
+        scratch_shapes=list(scratch),
+        compiler_params=pltpu.CompilerParams(vmem_limit_bytes=vmem),
+        cost_estimate=pl.CostEstimate(flops=flops, bytes_accessed=nbytes, transcendentals=0),
+    )(*args)
+
+
+def slots_of(ids, expert, capacity):
+    tokens = ids.shape[1]
+    routed = jnp.max((ids == expert).astype(F32), axis=0, keepdims=True)
+    before = (
+        lax.broadcasted_iota(jnp.int32, (tokens, tokens), 0)
+        < lax.broadcasted_iota(jnp.int32, (tokens, tokens), 1)
+    ).astype(BF16)
+    position = dot_nn(jnp.broadcast_to(routed, (8, tokens)).astype(BF16), before)[0:1]
+    slot = lax.broadcasted_iota(jnp.int32, (capacity, tokens), 0).astype(F32)
+    return jnp.where((slot == position) & (routed > 0.0), 1.0, 0.0)
+
+
+def pack_kernel(groups, ids_ref, gates_ref, hidden_ref, grad_ref, *outs):
+    me = lax.axis_index("node")
+    ids = ids_ref[...]
+    gates = gates_ref[...].astype(F32)
+    capacity = ids.shape[1] // 2
+    for shift in range(groups):
+        expert = me ^ shift
+        chosen = slots_of(ids, expert, capacity)
+        one_hot = chosen.astype(BF16)
+        in_ref, grad_out, weight_ref = outs[3 * shift : 3 * shift + 3]
+        in_ref[...] = dot_nn(one_hot, hidden_ref[...]).astype(BF16)
+        grad_out[...] = dot_nn(one_hot, grad_ref[...]).astype(BF16)
+        weight = jnp.sum(jnp.where(ids == expert, gates, 0.0), axis=0, keepdims=True)
+        weight_ref[...] = dot_nt(jnp.broadcast_to(weight, (16, ids.shape[1])).astype(BF16), one_hot).astype(BF16)
+
+
+def assemble(parts, groups, rows_ref):
+    me = lax.axis_index("expert")
+    capacity, width = parts[0].shape
+    for index, part in enumerate(parts):
+        relative, shift = divmod(index, groups)
+        start = pl.multiple_of((me ^ relative) * width, width)
+        rows_ref[shift * capacity : (shift + 1) * capacity, pl.ds(start, width)] = part[...]
+
+
+def front_kernel(groups, *refs):
+    parts = refs[: 4 * groups]
+    gate_w, up_w, rows_ref, gate_ref, up_ref = refs[4 * groups :]
+    assemble(parts, groups, rows_ref)
+    rows = rows_ref[...]
+    gate_ref[...] = dot_nt(gate_w[0], rows)
+    up_ref[...] = dot_nt(up_w[0], rows)
+
+
+def middle_kernel(groups, *refs):
+    parts = refs[: 4 * groups]
+    weights = refs[4 * groups : 5 * groups]
+    down_w, gate_ref, up_ref, rows_ref, dgate_ref, dup_ref, hid_ref, stat_ref = refs[5 * groups :]
+    assemble(parts, groups, rows_ref)
+    back = dot_nt(down_w[0], rows_ref[...])
+    weight = jnp.concatenate([w[0:1, :] for w in weights], axis=1).astype(F32)
+    gate = gate_ref[...]
+    up = up_ref[...]
+    sig = 1.0 / (1.0 + jnp.exp(-gate))
+    silu = gate * sig
+    hidden = silu * up
+    stat_ref[...] = jnp.broadcast_to(jnp.sum(hidden * back, axis=0, keepdims=True), stat_ref.shape)
+    scaled = weight * back
+    dgate_ref[...] = (scaled * up * sig * (1.0 + gate * (1.0 - sig))).astype(BF16)
+    dup_ref[...] = (scaled * silu).astype(BF16)
+    hid_ref[...] = (weight * hidden).astype(BF16)
+
+
+def input_kernel(far, dgate_ref, dup_ref, gate_w, up_w, keep_ref, give_ref):
+    me = lax.axis_index("expert")
+    width = keep_ref.shape[1]
+    dgate = dgate_ref[...].T
+    dup = dup_ref[...].T
+    for ref, relative in ((give_ref, far + 1), (keep_ref, far)):
+        columns = pl.ds(pl.multiple_of((me ^ relative) * width, width), width)
+        total = dot_nn(dgate, gate_w[0, :, columns]) + dot_nn(dup, up_w[0, :, columns])
+        ref[...] = total.astype(ref.dtype)
+
+
+def add_kernel(groups, left, right, *outs):
+    capacity = outs[0].shape[0]
+    for shift in range(groups):
+        rows = slice(shift * capacity, (shift + 1) * capacity)
+        outs[shift][...] = (left[rows].astype(F32) + right[rows].astype(F32)).astype(BF16)
+
+
+def join_kernel(left, right, third, out):
+    out[...] = (left[...].astype(F32) + right[...].astype(F32) + third[...].astype(F32)).astype(BF16)
+
+
+def grad_kernel(left_ref, rows_ref, out_ref):
+    tile = 512
+    def step(i, _):
+        columns = pl.ds(pl.multiple_of(i * tile, tile), tile)
+        out_ref[0, :, columns] = dot_nn(left_ref[...], rows_ref[:, columns]).astype(BF16)
+        return _
+    lax.fori_loop(0, rows_ref.shape[1] // tile, step, 0)
+
+
+def finish_kernel(groups, ids_ref, stat_ref, *refs):
+    parts = refs[:groups]
+    grad_ref, gates_ref = refs[groups:]
+    me = lax.axis_index("node")
+    ids = ids_ref[...]
+    capacity = ids.shape[1] // 2
+    total = jnp.zeros(grad_ref.shape, F32)
+    gates = jnp.zeros(ids.shape, F32)
+    for shift in range(groups):
+        expert = me ^ shift
+        chosen = slots_of(ids, expert, capacity)
+        total = total + dot_tn(chosen.astype(BF16), parts[shift][...])
+        stat = jnp.broadcast_to(stat_ref[shift : shift + 1], (8, capacity))
+        spread = lax.dot_general(
+            stat, chosen, (((1,), (0,)), ((), ())),
+            precision=lax.Precision.HIGHEST, preferred_element_type=F32,
+        )[0:1]
+        gates = gates + jnp.where(ids == expert, spread, 0.0)
+    grad_ref[...] = total.astype(BF16)
+    gates_ref[...] = gates
+
+
+def fast_local(hidden_in, out_grad, expert_ids, gate_weights, w_gate, w_up, w_down):
+    groups = lax.axis_size("node")
+    experts = lax.axis_size("expert")
+    tokens, width = hidden_in.shape
+    capacity = tokens // 2
+    rows = groups * capacity
+    units, features = w_gate.shape[1:]
+    shape = jax.ShapeDtypeStruct
+
+    def over_node(x, shift):
+        return lax.ppermute(x, "node", [(i, i ^ shift) for i in range(groups)])
+
+    def over_expert(x, relative):
+        return lax.ppermute(x, "expert", [(i, i ^ relative) for i in range(experts)])
+
+    ids = expert_ids.T
+    packed = call(
+        functools.partial(pack_kernel, groups),
+        [shape((capacity, width), BF16), shape((capacity, width), BF16), shape((16, capacity), BF16)] * groups,
+        ids, gate_weights.T, hidden_in, out_grad,
+        flops=4 * rows * tokens * width, nbytes=6 * tokens * width,
+    )
+
+    def spread(blocks):
+        own = [blocks[0]] + [over_node(blocks[s], s) for s in range(1, groups)]
+        other = [over_expert(x, 2) for x in own]
+        partner = [over_expert(x, 1) for x in own]
+        across = [over_expert(x, 1) for x in other]
+        return own + partner + other + across
+
+    ins = spread(packed[0::3])
+    grads = spread(packed[1::3])
+    weights = [packed[2]] + [over_node(packed[3 * s + 2], s) for s in range(1, groups)]
+
+    dense = 2 * rows * units * features
+    rows_in, gate, up = call(
+        functools.partial(front_kernel, groups),
+        [shape((rows, features), BF16), shape((units, rows), F32), shape((units, rows), F32)],
+        *ins, w_gate, w_up, flops=2 * dense, nbytes=4 * units * features,
+    )
+    rows_grad, dgate, dup, hid, stat = call(
+        functools.partial(middle_kernel, groups),
+        [shape((rows, features), BF16)] + [shape((units, rows), BF16)] * 3 + [shape((8, rows), F32)],
+        *grads, *weights, w_down, gate, up, flops=dense, nbytes=2 * units * features,
+    )
+    far_keep, far_give = call(
+        functools.partial(input_kernel, 2),
+        [shape((rows, width), BF16)] * 2,
+        dgate, dup, w_gate, w_up, flops=dense, nbytes=2 * units * features,
+    )
+    far_got = over_expert(far_give, 1)
+    near_keep, near_give = call(
+        functools.partial(input_kernel, 0),
+        [shape((rows, width), BF16)] * 2,
+        dgate, dup, w_gate, w_up, flops=dense, nbytes=2 * units * features,
+    )
+    near_got = over_expert(near_give, 1)
+    far_sum = call(functools.partial(add_kernel, groups), [shape((capacity, width), BF16)] * groups, far_keep, far_got,
+                   nbytes=6 * rows * width)
+    crossed = [over_expert(x, 2) for x in far_sum]
+    back = []
+    for s in range(groups):
+        block = slice(s * capacity, (s + 1) * capacity)
+        total = call(join_kernel, [shape((capacity, width), BF16)], near_keep[block], near_got[block], crossed[s])[0]
+        back.append(over_node(total, s) if s else total)
+
+    stat_rows = stat[0].reshape(groups, capacity)
+    stat_pair = stat_rows + over_expert(stat_rows, 1)
+    stat_total = stat_pair + over_expert(stat_pair, 2)
+    stat_back = jnp.concatenate(
+        [stat_total[0:1]] + [over_node(stat_total[s : s + 1], s) for s in range(1, groups)], axis=0
+    )
+
+    weight_grads = [
+        call(grad_kernel, [shape((1, units, features), BF16)], left, right, flops=dense, nbytes=2 * units * features)[0]
+        for left, right in ((dgate, rows_in), (dup, rows_in), (hid, rows_grad))
+    ]
+    grad_in, grad_gates = call(
+        functools.partial(finish_kernel, groups),
+        [shape((tokens, width), BF16), shape(ids.shape, F32)],
+        ids, stat_back, *back,
+    )
+    return (grad_in, grad_gates.T, *weight_grads)
 
 
 def contract_rows(left, right):
@@ -36,7 +274,7 @@
     return (grad_gate, grad_up, grad_down, grad_gate_pre, grad_up_pre, statistic)
 
 
-def local(hidden_in, out_grad, expert_ids, gate_weights, w_gate, w_up, w_down):
+def general_local(hidden_in, out_grad, expert_ids, gate_weights, w_gate, w_up, w_down):
     groups = lax.axis_size("node")
     count_tok = hidden_in.shape[0]
     capacity = count_tok // 2
@@ -107,6 +345,12 @@
     grad_in = (flat_input[flat_index[:, 0]] + flat_input[flat_index[:, 1]]).astype(jnp.bfloat16)
     grad_gates = flat_stat[flat_index]
     return (grad_in, grad_gates, grad_gate[None], grad_up[None], grad_down[None])
+
+
+def local(hidden_in, *rest):
+    if lax.axis_size("expert") == 4 and hidden_in.shape[1] % 128 == 0:
+        return fast_local(hidden_in, *rest)
+    return general_local(hidden_in, *rest)
 
 
 def solution(mesh):

time: 166 us -> 104 us (0.63)
  blocking collectives: 49.4 us -> 0 us
  matrix products: 34.5 us -> 0 us
  starting transfers between devices: 9.48 us -> 42.8 us
  Pallas kernels: 0 us -> 23.7 us
  waiting for transfers between devices: 42.6 us -> 26.5 us
  between operations: 14 us -> 0.91 us
  other arithmetic: 2.95 us -> 0.02 us
  local copies, waits for them, and re-layouts: 13 us -> 10.2 us
    all_to_all x3 -> x0, blocking collectives: 43 us -> none  [the longest x1 19.3 us: local(): lax.all_to_all(pack_rows(hidden_in), 'node', split_axis=0, concat_axis=0,...]
    ppermute x0 -> x47, starting transfers between devices: none -> 42.8 us  [the longest x15 24.3 us: over_node(): return lax.ppermute(x, 'node', [(i, i ^ shift) for i in range(groups)])]
    dot_general x8 -> x0, matrix products: 34.5 us -> none  [the longest x3 13.6 us: contract_cols(): lax.dot_general(left, right, (((1,), (1,)), ((), ())), preferred_element_...]
    ppermute x0 -> x47, waiting for transfers between devices: none -> 26.5 us  [the longest x32 14.1 us: over_expert(): lax.ppermute(x, 'expert', [(i, i ^ relative) for i in range(experts)])]
    reduce_scatter x1 -> x0, waiting for transfers between devices: 24.7 us -> none  [local(): lax.psum_scatter(input_part, 'expert', scatter_dimension=1, tiled=True)]
    pallas_call x0 -> x14, Pallas kernels: none -> 23.7 us  [call(): pl.pallas_call(kernel, out_shape=outs, in_specs=[pl.BlockSpec(memory_spac...]
    gather x13 -> x0, local copies, waits for them, and re-layouts: 10.9 us -> none  [the longest x2 2.44 us: local(): weight_of[token_of, group_ids[:, None]]]
    all_to_all x2 -> x0, waiting for transfers between devices: 10.5 us -> none  [the longest x1 7.47 us: local(): lax.all_to_all(input_slice.reshape(groups, capacity, slice_width), 'node'...]
  transfers between devices with their start and end apart: 5 -> 47, of which waited for: 4 -> 15; matrix products, arithmetic and copies ran while one was open for 18% -> 0% of each run, Pallas kernels for 0% -> 15%
where the time goes in v1:
time: 104 us
  starting transfers between devices  42.8 us (41%)
  waiting for transfers between devices  26.5 us (25%)
  Pallas kernels  23.7 us (23%)
  local copies, waits for them, and re-layouts  10.2 us (10%)
    ppermute x15, starting transfers between devices, over_node(): return lax.ppermute(x, 'node', [(i, i ^ shift) for i in range(groups)])  24.3 us
    pallas_call x14, Pallas kernels, call(): pl.pallas_call(kernel, out_shape=outs, in_specs=[pl.BlockSpec(memory_spac...  23.7 us
    ppermute x32, starting transfers between devices, over_expert(): lax.ppermute(x, 'expert', [(i, i ^ relative) for i in range(experts)])  18.5 us
    ppermute x32, waiting for transfers between devices, over_expert(): lax.ppermute(x, 'expert', [(i, i ^ relative) for i in range(experts)])  14.1 us
    ppermute x15, waiting for transfers between devices, over_node(): return lax.ppermute(x, 'node', [(i, i ^ shift) for i in range(groups)])  12.4 us
    unnamed x32, local copies, waits for them, and re-layouts  9.97 us
  transfers between devices with their start and end apart: 47, of which 15 were waited for; matrix products, arithmetic and copies ran while one was open for 0% of the time, Pallas kernels for 15%

profile of v1, /device:TPU:0, one launch (start us, length us, event | category | flops | bytes accessed | tf_op | source)
XLA Modules:
  0.0 104.1 jit_solution(9209531402739867487)
XLA Ops:
  4.8 3.1 %collective-permute-start.15 = (bf16[16,64]{1,0:T(8,128)(2,1)S(1)}, bf16[16,64]{1,0:T(8,128)(2,1)S(1)}, u32[]{:S(2)}, u32[]{:S(2)}) collective-permute-start(bf16[16,64]{1,0:T(8,128)(2,1)S(1)} %get-tuple-element.40), channel_id=1, source_target_pairs={{0,4},{4,0},{8,12},{12,8},{1,5},{5,1},{9,13},{13,9},{2,6},{6,2},{1... | collective-permute-start | bytes 6152 | tf_op jit(solution)/shard_map/ppermute | solution.py:170
  7.9 2.6 %collective-permute-start.16 = (bf16[16,64]{1,0:T(8,128)(2,1)S(1)}, bf16[16,64]{1,0:T(8,128)(2,1)S(1)}, u32[]{:S(2)}, u32[]{:S(2)}) collective-permute-start(bf16[16,64]{1,0:T(8,128)(2,1)S(1)} %get-tuple-element.41), channel_id=1, source_target_pairs={{0,8},{4,12},{8,0},{12,4},{1,9},{5,13},{9,1},{13,5},{2,10},{6,14},... | collective-permute-start | bytes 6152 | tf_op jit(solution)/shard_map/ppermute | solution.py:170
  11.4 3.5 %collective-permute-start.1 = (bf16[64,896]{1,0:T(8,128)(2,1)S(1)}, bf16[64,896]{1,0:T(8,128)(2,1)S(1)}, u32[]{:S(2)}, u32[]{:S(2)}) collective-permute-start(bf16[64,896]{1,0:T(8,128)(2,1)S(1)} %get-tuple-element.37), channel_id=1, source_target_pairs={{0,8},{4,12},{8,0},{12,4},{1,9},{5,13},{9,1},{13,5},{2,10},{6,14},... | collective-permute-start | bytes 344072 | tf_op jit(solution)/shard_map/ppermute | solution.py:170
  16.1 3.2 %collective-permute-start.19 = (bf16[64,896]{1,0:T(8,128)(2,1)S(1)}, bf16[64,896]{1,0:T(8,128)(2,1)S(1)}, u32[]{:S(2)}, u32[]{:S(2)}) collective-permute-start(bf16[64,896]{1,0:T(8,128)(2,1)S(1)} %get-tuple-element.45), channel_id=1, source_target_pairs={{0,8},{4,12},{8,0},{12,4},{1,9},{5,13},{9,1},{13,5},{2,10},{6,14},... | collective-permute-start | bytes 344072 | tf_op jit(solution)/shard_map/ppermute | solution.py:170
  19.3 1.8 %collective-permute-start.20 = (bf16[64,896]{1,0:T(8,128)(2,1)S(1)}, bf16[64,896]{1,0:T(8,128)(2,1)S(1)}, u32[]{:S(2)}, u32[]{:S(2)}) collective-permute-start(bf16[64,896]{1,0:T(8,128)(2,1)S(1)} %get-tuple-element.46), channel_id=1, source_target_pairs={{0,12},{4,8},{8,4},{12,0},{1,13},{5,9},{9,5},{13,1},{2,14},{6,10},... | collective-permute-start | bytes 344072 | tf_op jit(solution)/shard_map/ppermute | solution.py:170
  21.1 2.5 %collective-permute-done.1.refs_2_ = bf16[64,896]{1,0:T(8,128)(2,1)S(1)} collective-permute-done((bf16[64,896]{1,0:T(8,128)(2,1)S(1)}, bf16[64,896]{1,0:T(8,128)(2,1)S(1)}, u32[]{:S(2)}, u32[]{:S(2)}) %collective-permute-start.1) | collective-permute-done | bytes 114720 | tf_op jit(solution)/shard_map/ppermute | solution.py:170
  25.6 7.3 %collective-permute-done.19.refs_2_ = bf16[64,896]{1,0:T(8,128)(2,1)S(1)} collective-permute-done((bf16[64,896]{1,0:T(8,128)(2,1)S(1)}, bf16[64,896]{1,0:T(8,128)(2,1)S(1)}, u32[]{:S(2)}, u32[]{:S(2)}) %collective-permute-start.19) | collective-permute-done | bytes 114720 | tf_op jit(solution)/shard_map/ppermute | solution.py:170
  36.8 2.1 %collective-permute-done.8.refs_9_ = bf16[64,896]{1,0:T(8,128)(2,1)S(1)} collective-permute-done((bf16[64,896]{1,0:T(8,128)(2,1)S(1)}, bf16[64,896]{1,0:T(8,128)(2,1)S(1)}, u32[]{:S(2)}, u32[]{:S(2)}) %collective-permute-start.8) | collective-permute-done | bytes 114720 | tf_op jit(solution)/shard_map/ppermute | solution.py:173
  46.8 1.9 %collective-permute-done.27.refs_10_ = bf16[64,896]{1,0:T(8,128)(2,1)S(1)} collective-permute-done((bf16[64,896]{1,0:T(8,128)(2,1)S(1)}, bf16[64,896]{1,0:T(8,128)(2,1)S(1)}, u32[]{:S(2)}, u32[]{:S(2)}) %collective-permute-start.27) | collective-permute-done | bytes 114720 | tf_op jit(solution)/shard_map/ppermute | solution.py:173
  52.3 2.2 %copy-done = bf16[1,608,3584]{2,1,0:T(8,128)(2,1)S(1)} copy-done((bf16[1,608,3584]{2,1,0:T(8,128)(2,1)S(1)}, bf16[1,608,3584]{2,1,0:T(8,128)(2,1)}, u32[]{:S(2)}) %copy-start) | copy-done | bytes 4358168
  54.6 2.2 %copy-done.2 = bf16[1,608,3584]{2,1,0:T(8,128)(2,1)S(1)} copy-done((bf16[1,608,3584]{2,1,0:T(8,128)(2,1)S(1)}, bf16[1,608,3584]{2,1,0:T(8,128)(2,1)}, u32[]{:S(2)}) %copy-start.2) | copy-done | bytes 4358168
  56.8 2.6 %shard_map.111 = (bf16[256,3584]{1,0:T(8,128)(2,1)S(1)}, f32[608,256]{1,0:T(8,128)S(1)}, f32[608,256]{1,0:T(8,128)S(1)}) custom-call(bf16[64,896]{1,0:T(8,128)(2,1)S(1)} %get-tuple-element.43.refs_0_, bf16[64,896]{1,0:T(8,128)(2,1)S(1)} %collective-permute-done.18.refs_1_, bf16[64,896]{1,0:T(8,128)(2,1)S(1)} %collective-permute-done.19.refs_2_, ...), custom_call_target="tpu_custom_call" | custom-call | flops 2231369728 | bytes 8716288 | tf_op jit(solution)/shard_map/pallas_call | solution.py:31
  59.5 1.7 %shard_map.112 = (bf16[256,3584]{1,0:T(8,128)(2,1)S(1)}, bf16[608,256]{1,0:T(8,128)(2,1)S(1)}, bf16[608,256]{1,0:T(8,128)(2,1)S(1)}, bf16[608,256]{1,0:T(8,128)(2,1)S(1)}, f32[8,256]{1,0:T(8,128)S(1)}) custom-call(bf16[64,896]{1,0:T(8,128)(2,1)S(1)} %get-tuple-element.35.refs_0_, bf16[64,896]{1,0:T(8,128)(2,1)S(1)} %collective-permute-done.refs_1_, ...), custom_call_target="tpu_custom_call" | custom-call | flops 1115684864 | bytes 4358144 | tf_op jit(solution)/shard_map/pallas_call | solution.py:31
  61.9 1.8 %shard_map.114 = (bf16[256,896]{1,0:T(8,128)(2,1)S(1)}, bf16[256,896]{1,0:T(8,128)(2,1)S(1)}) custom-call(bf16[608,256]{1,0:T(8,128)(2,1)S(1)} %get-tuple-element.50.dgate_ref.left_ref, bf16[608,256]{1,0:T(8,128)(2,1)S(1)} %get-tuple-element.51.dup_ref.left_ref, bf16[1,608,3584]{2,1,0:T(8,128)(2,1)S(1)} %copy-done.1, bf16[1,608,3584]{2,1,0:T(8,128)(2,1)S(1)} %copy-done.3), custom_call_target="tpu_custom_call" | custom-call | flops 1115684864 | bytes 4358144 | tf_op jit(solution)/shard_map/pallas_call | solution.py:31
  64.5 1.8 %shard_map.113 = (bf16[256,896]{1,0:T(8,128)(2,1)S(1)}, bf16[256,896]{1,0:T(8,128)(2,1)S(1)}) custom-call(bf16[608,256]{1,0:T(8,128)(2,1)S(1)} %get-tuple-element.50.dgate_ref.left_ref, bf16[608,256]{1,0:T(8,128)(2,1)S(1)} %get-tuple-element.51.dup_ref.left_ref, bf16[1,608,3584]{2,1,0:T(8,128)(2,1)S(1)} %copy-done.1, bf16[1,608,3584]{2,1,0:T(8,128)(2,1)S(1)} %copy-done.3), custom_call_target="tpu_custom_call" | custom-call | flops 1115684864 | bytes 4358144 | tf_op jit(solution)/shard_map/pallas_call | solution.py:31
  67.9 4.3 %shard_map.122 = bf16[1,608,3584]{2,1,0:T(8,128)(2,1)} custom-call(bf16[608,256]{1,0:T(8,128)(2,1)S(1)} %get-tuple-element.51.dup_ref.left_ref, bf16[256,3584]{1,0:T(8,128)(2,1)S(1)} %get-tuple-element.62.rows_ref), custom_call_target="tpu_custom_call" | custom-call | flops 1115684864 | bytes 4358144 | tf_op jit(solution)/shard_map/pallas_call | solution.py:31
  73.9 4.3 %shard_map.121 = bf16[1,608,3584]{2,1,0:T(8,128)(2,1)} custom-call(bf16[608,256]{1,0:T(8,128)(2,1)S(1)} %get-tuple-element.50.dgate_ref.left_ref, bf16[256,3584]{1,0:T(8,128)(2,1)S(1)} %get-tuple-element.62.rows_ref), custom_call_target="tpu_custom_call" | custom-call | flops 1115684864 | bytes 4358144 | tf_op jit(solution)/shard_map/pallas_call | solution.py:31
  78.3 2.4 %collective-permute-start.37 = (f32[1,64]{1,0:T(1,128)S(1)}, f32[1,64]{1,0:T(1,128)S(1)}, u32[]{:S(2)}, u32[]{:S(2)}) collective-permute-start(f32[1,64]{1,0:T(1,128)S(1)} %get-tuple-element.74), channel_id=1, source_target_pairs={{0,12},{4,8},{8,4},{12,0},{1,13},{5,9},{9,5},{13,1},{2,14},{6,10},... | collective-permute-start | bytes 776 | tf_op jit(solution)/shard_map/ppermute | solution.py:170
  83.6 3.5 %collective-permute-done.41.third = bf16[64,896]{1,0:T(8,128)(2,1)S(1)} collective-permute-done((bf16[64,896]{1,0:T(8,128)(2,1)S(1)}, bf16[64,896]{1,0:T(8,128)(2,1)S(1)}, u32[]{:S(2)}, u32[]{:S(2)}) %collective-permute-start.41) | collective-permute-done | bytes 114720 | tf_op jit(solution)/shard_map/ppermute | solution.py:173
  87.0 2.0 %collective-permute-start.35 = (f32[1,64]{1,0:T(1,128)S(1)}, f32[1,64]{1,0:T(1,128)S(1)}, u32[]{:S(2)}, u32[]{:S(2)}) collective-permute-start(f32[1,64]{1,0:T(1,128)S(1)} %get-tuple-element.76), channel_id=1, source_target_pairs={{0,4},{4,0},{8,12},{12,8},{1,5},{5,1},{9,13},{13,9},{2,6},{6,2},{1... | collective-permute-start | bytes 776 | tf_op jit(solution)/shard_map/ppermute | solution.py:170
  89.8 1.8 %collective-permute-done.45.third = bf16[64,896]{1,0:T(8,128)(2,1)S(1)} collective-permute-done((bf16[64,896]{1,0:T(8,128)(2,1)S(1)}, bf16[64,896]{1,0:T(8,128)(2,1)S(1)}, u32[]{:S(2)}, u32[]{:S(2)}) %collective-permute-start.45) | collective-permute-done | bytes 114720 | tf_op jit(solution)/shard_map/ppermute | solution.py:173
  91.6 2.7 %collective-permute-start.44 = (bf16[64,896]{1,0:T(8,128)(2,1)S(1)}, bf16[64,896]{1,0:T(8,128)(2,1)S(1)}, u32[]{:S(2)}, u32[]{:S(2)}) collective-permute-start(bf16[64,896]{1,0:T(8,128)(2,1)S(1)} %shard_map.118), channel_id=1, source_target_pairs={{0,8},{4,12},{8,0},{12,4},{1,9},{5,13},{9,1},{13,5},{2,10},{6,14},... | collective-permute-start | bytes 344072 | tf_op jit(solution)/shard_map/ppermute | solution.py:170
  96.0 4.3 %shard_map.123 = bf16[1,608,3584]{2,1,0:T(8,128)(2,1)} custom-call(bf16[608,256]{1,0:T(8,128)(2,1)S(1)} %copy-done.8, bf16[256,3584]{1,0:T(8,128)(2,1)S(1)} %copy-done.6), custom_call_target="tpu_custom_call" | custom-call | flops 1115684864 | bytes 4358144 | tf_op jit(solution)/shard_map/pallas_call | solution.py:31
  102.4 1.7 %shard_map.120 = (bf16[128,896]{1,0:T(8,128)(2,1)}, f32[2,128]{1,0:T(2,128)}) custom-call(s32[2,128]{1,0:T(2,128)S(1)} %bitcast.4, f32[4,64]{1,0:T(4,128)S(1)} %pad_maximum_fusion.stat_ref, bf16[64,896]{1,0:T(8,128)(2,1)S(1)} %shard_map.116.refs_0_, bf16[64,896]{1,0:T(8,128)(2,1)S(1)} %collective-permute-done.42.refs_1_, ...), custom_call_target="tpu_custom_call" | custom-call | tf_op jit(solution)/shard_map/pallas_call | solution.py:31
  (124 shorter events, 36.0 us)
Async XLA Ops:
  4.8 10.1 %collective-permute-start.15 = (bf16[16,64]{1,0:T(8,128)(2,1)S(1)}, bf16[16,64]{1,0:T(8,128)(2,1)S(1)}, u32[]{:S(2)}, u32[]{:S(2)}) collective-permute-start(bf16[16,64]{1,0:T(8,128)(2,1)S(1)} %get-tuple-element.40), channel_id=1, source_target_pairs={{0,4},{4,0},{8,12},{12,8},{1,5},{5,1},{9,13},{13,9},{2,6},{6,2},{1... | collective-permute-start | bytes 6152 | tf_op jit(solution)/shard_map/ppermute | solution.py:170
  10.5 8.8 %collective-permute-start = (bf16[64,896]{1,0:T(8,128)(2,1)S(1)}, bf16[64,896]{1,0:T(8,128)(2,1)S(1)}, u32[]{:S(2)}, u32[]{:S(2)}) collective-permute-start(bf16[64,896]{1,0:T(8,128)(2,1)S(1)} %get-tuple-element.36), channel_id=1, source_target_pairs={{0,4},{4,0},{8,12},{12,8},{1,5},{5,1},{9,13},{13,9},{2,6},{6,2},{1... | collective-permute-start | bytes 344072 | tf_op jit(solution)/shard_map/ppermute | solution.py:170
  11.4 12.2 %collective-permute-start.1 = (bf16[64,896]{1,0:T(8,128)(2,1)S(1)}, bf16[64,896]{1,0:T(8,128)(2,1)S(1)}, u32[]{:S(2)}, u32[]{:S(2)}) collective-permute-start(bf16[64,896]{1,0:T(8,128)(2,1)S(1)} %get-tuple-element.37), channel_id=1, source_target_pairs={{0,8},{4,12},{8,0},{12,4},{1,9},{5,13},{9,1},{13,5},{2,10},{6,14},... | collective-permute-start | bytes 344072 | tf_op jit(solution)/shard_map/ppermute | solution.py:170
  14.9 10.2 %collective-permute-start.2 = (bf16[64,896]{1,0:T(8,128)(2,1)S(1)}, bf16[64,896]{1,0:T(8,128)(2,1)S(1)}, u32[]{:S(2)}, u32[]{:S(2)}) collective-permute-start(bf16[64,896]{1,0:T(8,128)(2,1)S(1)} %get-tuple-element.38), channel_id=1, source_target_pairs={{0,12},{4,8},{8,4},{12,0},{1,13},{5,9},{9,5},{13,1},{2,14},{6,10},... | collective-permute-start | bytes 344072 | tf_op jit(solution)/shard_map/ppermute | solution.py:170
  14.9 10.2 %collective-permute-start.18 = (bf16[64,896]{1,0:T(8,128)(2,1)S(1)}, bf16[64,896]{1,0:T(8,128)(2,1)S(1)}, u32[]{:S(2)}, u32[]{:S(2)}) collective-permute-start(bf16[64,896]{1,0:T(8,128)(2,1)S(1)} %get-tuple-element.44), channel_id=1, source_target_pairs={{0,4},{4,0},{8,12},{12,8},{1,5},{5,1},{9,13},{13,9},{2,6},{6,2},{1... | collective-permute-start | bytes 344072 | tf_op jit(solution)/shard_map/ppermute | solution.py:170
  16.1 16.8 %collective-permute-start.19 = (bf16[64,896]{1,0:T(8,128)(2,1)S(1)}, bf16[64,896]{1,0:T(8,128)(2,1)S(1)}, u32[]{:S(2)}, u32[]{:S(2)}) collective-permute-start(bf16[64,896]{1,0:T(8,128)(2,1)S(1)} %get-tuple-element.45), channel_id=1, source_target_pairs={{0,8},{4,12},{8,0},{12,4},{1,9},{5,13},{9,1},{13,5},{2,10},{6,14},... | collective-permute-start | bytes 344072 | tf_op jit(solution)/shard_map/ppermute | solution.py:170
  19.3 13.6 %collective-permute-start.20 = (bf16[64,896]{1,0:T(8,128)(2,1)S(1)}, bf16[64,896]{1,0:T(8,128)(2,1)S(1)}, u32[]{:S(2)}, u32[]{:S(2)}) collective-permute-start(bf16[64,896]{1,0:T(8,128)(2,1)S(1)} %get-tuple-element.46), channel_id=1, source_target_pairs={{0,12},{4,8},{8,4},{12,0},{1,13},{5,9},{9,5},{13,1},{2,14},{6,10},... | collective-permute-start | bytes 344072 | tf_op jit(solution)/shard_map/ppermute | solution.py:170
  23.5 10.9 %collective-permute-start.7 = (bf16[64,896]{1,0:T(8,128)(2,1)S(1)}, bf16[64,896]{1,0:T(8,128)(2,1)S(1)}, u32[]{:S(2)}, u32[]{:S(2)}) collective-permute-start(bf16[64,896]{1,0:T(8,128)(2,1)S(1)} %get-tuple-element.35.refs_0_), channel_id=1, source_target_pairs={{0,2},{1,3},{2,0},{3,1},{4,6},{5,7},{6,4},{7,5},{8,10},{9,11},{10,... | collective-permute-start | bytes 344072 | tf_op jit(solution)/shard_map/ppermute | solution.py:173
  25.1 9.6 %collective-permute-start.3 = (bf16[64,896]{1,0:T(8,128)(2,1)S(1)}, bf16[64,896]{1,0:T(8,128)(2,1)S(1)}, u32[]{:S(2)}, u32[]{:S(2)}) collective-permute-start(bf16[64,896]{1,0:T(8,128)(2,1)S(1)} %get-tuple-element.35.refs_0_), channel_id=1, source_target_pairs={{0,1},{1,0},{2,3},{3,2},{4,5},{5,4},{6,7},{7,6},{8,9},{9,8},{10,11... | collective-permute-start | bytes 344072 | tf_op jit(solution)/shard_map/ppermute | solution.py:173
  25.1 10.1 %collective-permute-start.25 = (bf16[64,896]{1,0:T(8,128)(2,1)S(1)}, bf16[64,896]{1,0:T(8,128)(2,1)S(1)}, u32[]{:S(2)}, u32[]{:S(2)}) collective-permute-start(bf16[64,896]{1,0:T(8,128)(2,1)S(1)} %get-tuple-element.43.refs_0_), channel_id=1, source_target_pairs={{0,2},{1,3},{2,0},{3,1},{4,6},{5,7},{6,4},{7,5},{8,10},{9,11},{10,... | collective-permute-start | bytes 344072 | tf_op jit(solution)/shard_map/ppermute | solution.py:173
  35.2 7.7 %collective-permute-start.5 = (bf16[64,896]{1,0:T(8,128)(2,1)S(1)}, bf16[64,896]{1,0:T(8,128)(2,1)S(1)}, u32[]{:S(2)}, u32[]{:S(2)}) collective-permute-start(bf16[64,896]{1,0:T(8,128)(2,1)S(1)} %collective-permute-done.1.refs_2_), channel_id=1, source_target_pairs={{0,1},{1,0},{2,3},{3,2},{4,5},{5,4},{6,7},{7,6},{8,9},{9,8},{10,11... | collective-permute-start | bytes 344072 | tf_op jit(solution)/shard_map/ppermute | solution.py:173
  35.2 8.6 %collective-permute-start.10 = (bf16[64,896]{1,0:T(8,128)(2,1)S(1)}, bf16[64,896]{1,0:T(8,128)(2,1)S(1)}, u32[]{:S(2)}, u32[]{:S(2)}) collective-permute-start(bf16[64,896]{1,0:T(8,128)(2,1)S(1)} %collective-permute-done.2.refs_3_), channel_id=1, source_target_pairs={{0,2},{1,3},{2,0},{3,1},{4,6},{5,7},{6,4},{7,5},{8,10},{9,11},{10,... | collective-permute-start | bytes 344072 | tf_op jit(solution)/shard_map/ppermute | solution.py:173
  50.8 8.6 %collective-permute-start.6 = (bf16[64,896]{1,0:T(8,128)(2,1)S(1)}, bf16[64,896]{1,0:T(8,128)(2,1)S(1)}, u32[]{:S(2)}, u32[]{:S(2)}) collective-permute-start(bf16[64,896]{1,0:T(8,128)(2,1)S(1)} %collective-permute-done.2.refs_3_), channel_id=1, source_target_pairs={{0,1},{1,0},{2,3},{3,2},{4,5},{5,4},{6,7},{7,6},{8,9},{9,8},{10,11... | collective-permute-start | bytes 344072 | tf_op jit(solution)/shard_map/ppermute | solution.py:173
  51.3 8.1 %collective-permute-start.11 = (bf16[64,896]{1,0:T(8,128)(2,1)S(1)}, bf16[64,896]{1,0:T(8,128)(2,1)S(1)}, u32[]{:S(2)}, u32[]{:S(2)}) collective-permute-start(bf16[64,896]{1,0:T(8,128)(2,1)S(1)} %collective-permute-done.7.refs_8_), channel_id=1, source_target_pairs={{0,1},{1,0},{2,3},{3,2},{4,5},{5,4},{6,7},{7,6},{8,9},{9,8},{10,11... | collective-permute-start | bytes 344072 | tf_op jit(solution)/shard_map/ppermute | solution.py:173
  51.4 8.1 %collective-permute-start.12 = (bf16[64,896]{1,0:T(8,128)(2,1)S(1)}, bf16[64,896]{1,0:T(8,128)(2,1)S(1)}, u32[]{:S(2)}, u32[]{:S(2)}) collective-permute-start(bf16[64,896]{1,0:T(8,128)(2,1)S(1)} %collective-permute-done.8.refs_9_), channel_id=1, source_target_pairs={{0,1},{1,0},{2,3},{3,2},{4,5},{5,4},{6,7},{7,6},{8,9},{9,8},{10,11... | collective-permute-start | bytes 344072 | tf_op jit(solution)/shard_map/ppermute | solution.py:173
  67.4 13.4 %collective-permute-start.39 = (bf16[256,896]{1,0:T(8,128)(2,1)}, bf16[256,896]{1,0:T(8,128)(2,1)S(1)}, u32[]{:S(2)}, u32[]{:S(2)}) collective-permute-start(bf16[256,896]{1,0:T(8,128)(2,1)} %copy-done.15), channel_id=1, source_target_pairs={{0,1},{1,0},{2,3},{3,2},{4,5},{5,4},{6,7},{7,6},{8,9},{9,8},{10,11... | collective-permute-start | bytes 1376264 | tf_op jit(solution)/shard_map/ppermute | solution.py:173
  67.6 15.4 %collective-permute-start.38 = (bf16[256,896]{1,0:T(8,128)(2,1)}, bf16[256,896]{1,0:T(8,128)(2,1)S(1)}, u32[]{:S(2)}, u32[]{:S(2)}) collective-permute-start(bf16[256,896]{1,0:T(8,128)(2,1)} %copy-done.14), channel_id=1, source_target_pairs={{0,1},{1,0},{2,3},{3,2},{4,5},{5,4},{6,7},{7,6},{8,9},{9,8},{10,11... | collective-permute-start | bytes 1376264 | tf_op jit(solution)/shard_map/ppermute | solution.py:173
  78.3 16.2 %collective-permute-start.37 = (f32[1,64]{1,0:T(1,128)S(1)}, f32[1,64]{1,0:T(1,128)S(1)}, u32[]{:S(2)}, u32[]{:S(2)}) collective-permute-start(f32[1,64]{1,0:T(1,128)S(1)} %get-tuple-element.74), channel_id=1, source_target_pairs={{0,12},{4,8},{8,4},{12,0},{1,13},{5,9},{9,5},{13,1},{2,14},{6,10},... | collective-permute-start | bytes 776 | tf_op jit(solution)/shard_map/ppermute | solution.py:170
  80.6 15.3 %collective-permute-start.36 = (f32[1,64]{1,0:T(1,128)S(1)}, f32[1,64]{1,0:T(1,128)S(1)}, u32[]{:S(2)}, u32[]{:S(2)}) collective-permute-start(f32[1,64]{1,0:T(1,128)S(1)} %get-tuple-element.75), channel_id=1, source_target_pairs={{0,8},{4,12},{8,0},{12,4},{1,9},{5,13},{9,1},{13,5},{2,10},{6,14},... | collective-permute-start | bytes 776 | tf_op jit(solution)/shard_map/ppermute | solution.py:170
  81.5 7.8 %collective-permute-start.43 = (bf16[64,896]{1,0:T(8,128)(2,1)S(1)}, bf16[64,896]{1,0:T(8,128)(2,1)S(1)}, u32[]{:S(2)}, u32[]{:S(2)}) collective-permute-start(bf16[64,896]{1,0:T(8,128)(2,1)S(1)} %get-tuple-element.58), channel_id=1, source_target_pairs={{0,2},{1,3},{2,0},{3,1},{4,6},{5,7},{6,4},{7,5},{8,10},{9,11},{10,... | collective-permute-start | bytes 344072 | tf_op jit(solution)/shard_map/ppermute | solution.py:173
  83.0 8.6 %collective-permute-start.45 = (bf16[64,896]{1,0:T(8,128)(2,1)S(1)}, bf16[64,896]{1,0:T(8,128)(2,1)S(1)}, u32[]{:S(2)}, u32[]{:S(2)}) collective-permute-start(bf16[64,896]{1,0:T(8,128)(2,1)S(1)} %get-tuple-element.59), channel_id=1, source_target_pairs={{0,2},{1,3},{2,0},{3,1},{4,6},{5,7},{6,4},{7,5},{8,10},{9,11},{10,... | collective-permute-start | bytes 344072 | tf_op jit(solution)/shard_map/ppermute | solution.py:173
  87.0 13.3 %collective-permute-start.35 = (f32[1,64]{1,0:T(1,128)S(1)}, f32[1,64]{1,0:T(1,128)S(1)}, u32[]{:S(2)}, u32[]{:S(2)}) collective-permute-start(f32[1,64]{1,0:T(1,128)S(1)} %get-tuple-element.76), channel_id=1, source_target_pairs={{0,4},{4,0},{8,12},{12,8},{1,5},{5,1},{9,13},{13,9},{2,6},{6,2},{1... | collective-permute-start | bytes 776 | tf_op jit(solution)/shard_map/ppermute | solution.py:170
  89.3 11.1 %collective-permute-start.40 = (bf16[64,896]{1,0:T(8,128)(2,1)S(1)}, bf16[64,896]{1,0:T(8,128)(2,1)S(1)}, u32[]{:S(2)}, u32[]{:S(2)}) collective-permute-start(bf16[64,896]{1,0:T(8,128)(2,1)S(1)} %get-tuple-element.56), channel_id=1, source_target_pairs={{0,2},{1,3},{2,0},{3,1},{4,6},{5,7},{6,4},{7,5},{8,10},{9,11},{10,... | collective-permute-start | bytes 344072 | tf_op jit(solution)/shard_map/ppermute | solution.py:173
  91.6 9.7 %collective-permute-start.44 = (bf16[64,896]{1,0:T(8,128)(2,1)S(1)}, bf16[64,896]{1,0:T(8,128)(2,1)S(1)}, u32[]{:S(2)}, u32[]{:S(2)}) collective-permute-start(bf16[64,896]{1,0:T(8,128)(2,1)S(1)} %shard_map.118), channel_id=1, source_target_pairs={{0,8},{4,12},{8,0},{12,4},{1,9},{5,13},{9,1},{13,5},{2,10},{6,14},... | collective-permute-start | bytes 344072 | tf_op jit(solution)/shard_map/ppermute | solution.py:170
  (39 other events, 219.1 us)

commit v2 on v0

--- a/solution.py
+++ b/solution.py
@@ -1,7 +1,302 @@
+import functools
+
 import jax
 import jax.numpy as jnp
 from jax import lax
+from jax.experimental import pallas as pl
+from jax.experimental.pallas import tpu as pltpu
 from jax.sharding import PartitionSpec as P
+
+BF16 = jnp.bfloat16
+F32 = jnp.float32
+MIB = 1 << 20
+
+
+def dot_nt(left, right):
+    return lax.dot_general(left, right, (((1,), (1,)), ((), ())), preferred_element_type=F32)
+
+
+def dot_tn(left, right):
+    return lax.dot_general(left, right, (((0,), (0,)), ((), ())), preferred_element_type=F32)
+
+
+def dot_nn(left, right):
+    return lax.dot_general(left, right, (((1,), (0,)), ((), ())), preferred_element_type=F32)
+
+
+def call(kernel, outs, *args, flops=0, nbytes=0, vmem=6 * MIB, scratch=(), in_hbm=()):
+    args = [
+        pltpu.with_memory_space_constraint(a, pltpu.HBM) if i in in_hbm else a for i, a in enumerate(args)
+    ]
+    return pl.pallas_call(
+        kernel,
+        out_shape=outs,
+        in_specs=[
+            pl.BlockSpec(memory_space=pltpu.HBM if i in in_hbm else pltpu.VMEM) for i in range(len(args))
+        ],
+        out_specs=[pl.BlockSpec(memory_space=pltpu.VMEM)] * len(outs),
+        scratch_shapes=list(scratch),
+        compiler_params=pltpu.CompilerParams(vmem_limit_bytes=vmem),
+        cost_estimate=pl.CostEstimate(flops=flops, bytes_accessed=nbytes, transcendentals=0),
+    )(*args)
+
+
+def slots_of(ids, expert, capacity):
+    tokens = ids.shape[1]
+    routed = jnp.max((ids == expert).astype(F32), axis=0, keepdims=True)
+    before = (
+        lax.broadcasted_iota(jnp.int32, (tokens, tokens), 0)
+        < lax.broadcasted_iota(jnp.int32, (tokens, tokens), 1)
+    ).astype(BF16)
+    position = dot_nn(jnp.broadcast_to(routed, (8, tokens)).astype(BF16), before)[0:1]
+    slot = lax.broadcasted_iota(jnp.int32, (capacity, tokens), 0).astype(F32)
+    return jnp.where((slot == position) & (routed > 0.0), 1.0, 0.0)
+
+
+def pack_kernel(groups, *refs):
+    sources, outs, local, sems = refs[:4], refs[4 : 4 + groups], refs[4 + groups : 8 + groups], refs[-1]
+    copies = [pltpu.make_async_copy(a, b, sems.at[i]) for i, (a, b) in enumerate(zip(sources, local))]
+    for copy in copies:
+        copy.start()
+    ids_ref, gates_ref, hidden_ref, grad_ref = local
+    me = lax.axis_index("node")
+    copies[0].wait()
+    copies[1].wait()
+    ids = ids_ref[...]
+    capacity = ids.shape[1] // 2
+    one_hots = [slots_of(ids, me ^ shift, capacity) for shift in range(groups)]
+    copies[2].wait()
+    for one_hot, out in zip(one_hots, outs):
+        out[:capacity] = dot_nn(one_hot.astype(BF16), hidden_ref[...]).astype(BF16)
+    gates = gates_ref[...].astype(F32)
+    copies[3].wait()
+    for shift, (one_hot, out) in enumerate(zip(one_hots, outs)):
+        weight = jnp.sum(jnp.where(ids == (me ^ shift), gates, 0.0), axis=0, keepdims=True)
+        out[capacity:] = dot_nn((one_hot * weight).astype(BF16), grad_ref[...]).astype(BF16)
+
+
+def load_kernel(*refs):
+    count = len(refs) // 2
+    sources, outs, sems = refs[:count], refs[count : 2 * count], refs[-1]
+    copies = [pltpu.make_async_copy(a, b, sems.at[i]) for i, (a, b) in enumerate(zip(sources, outs))]
+    for copy in copies:
+        copy.start()
+    for copy in copies:
+        copy.wait()
+
+
+def assemble(parts, relatives, groups, base, rows_ref, grads_ref):
+    me = lax.axis_index("expert")
+    capacity, width = parts[0].shape[0] // 2, parts[0].shape[1]
+    for index, part in enumerate(parts):
+        place, shift = divmod(index, groups)
+        columns = pl.ds(pl.multiple_of(((me ^ relatives[place]) - base) * width, width), width)
+        rows = slice(shift * capacity, (shift + 1) * capacity)
+        rows_ref[rows, columns] = part[:capacity]
+        grads_ref[rows, columns] = part[capacity:]
+
+
+def local_kernel(groups, *refs):
+    parts = refs[: 2 * groups]
+    gate_w, up_w, down_w, gate_ref, up_ref, back_ref, rows_ref, grads_ref = refs[2 * groups :]
+    base = (lax.axis_index("expert") // 2) * 2
+    assemble(parts, (0, 1), groups, base, rows_ref, grads_ref)
+    half = rows_ref.shape[1]
+    columns = pl.ds(pl.multiple_of(base * (half // 2), half), half)
+    gate_ref[...] = dot_nt(gate_w[0, :, columns], rows_ref[...])
+    up_ref[...] = dot_nt(up_w[0, :, columns], rows_ref[...])
+    back_ref[...] = dot_nt(down_w[0, :, columns], grads_ref[...])
+
+
+def middle_kernel(groups, *refs):
+    parts = refs[: 4 * groups]
+    (gate_w, up_w, down_w, gate_ref, up_ref, back_ref,
+     rows_ref, grads_ref, dgate_ref, dup_ref, hid_ref, stat_ref) = refs[4 * groups :]
+    assemble(parts, (2, 3, 0, 1), groups, 0, rows_ref, grads_ref)
+    half = rows_ref.shape[1] // 2
+    columns = pl.ds(pl.multiple_of((1 - lax.axis_index("expert") // 2) * half, half), half)
+    gate = gate_ref[...] + dot_nt(gate_w[0, :, columns], rows_ref[:, columns])
+    up = up_ref[...] + dot_nt(up_w[0, :, columns], rows_ref[:, columns])
+    back = back_ref[...] + dot_nt(down_w[0, :, columns], grads_ref[:, columns])
+    sig = 1.0 / (1.0 + jnp.exp(-gate))
+    silu = gate * sig
+    hidden = silu * up
+    stat_ref[...] = jnp.broadcast_to(jnp.sum(hidden * back, axis=0, keepdims=True), stat_ref.shape)
+    dgate_ref[...] = (back * up * sig * (1.0 + gate * (1.0 - sig))).astype(BF16)
+    dup_ref[...] = (back * silu).astype(BF16)
+    hid_ref[...] = hidden.astype(BF16)
+
+
+EXTRA = 8
+
+
+def halves_of(row):
+    high = row.astype(BF16).astype(F32)
+    index = lax.broadcasted_iota(jnp.int32, (EXTRA, row.shape[1]), 0)
+    return jnp.where(index == 0, high, jnp.where(index == 1, row - high, 0.0)).astype(BF16)
+
+
+def row_of(halves):
+    return halves[0:1].astype(F32) + halves[1:2].astype(F32)
+
+
+def input_kernel(far, dgate_ref, dup_ref, gate_w, up_w, stat_ref, give_ref, keep_ref):
+    me = lax.axis_index("expert")
+    rows, width = keep_ref.shape
+    dgate = dgate_ref[...].T
+    dup = dup_ref[...].T
+    for ref, relative in ((give_ref, far + 1), (keep_ref, far)):
+        columns = pl.ds(pl.multiple_of((me ^ relative) * width, width), width)
+        total = dot_nn(dgate, gate_w[0, :, columns]) + dot_nn(dup, up_w[0, :, columns])
+        ref[:rows] = total.astype(ref.dtype)
+    if far:
+        give_ref[rows:, :rows] = halves_of(stat_ref[0:1])
+        give_ref[rows:, rows:] = jnp.zeros((EXTRA, width - rows), BF16)
+
+
+def add_kernel(groups, keep, got, stat_ref, *outs):
+    capacity = outs[0].shape[0] - EXTRA
+    rows = groups * capacity
+    stat = stat_ref[0:1] + row_of(got[rows:, :rows])
+    outs[groups][...] = jnp.broadcast_to(stat, outs[groups].shape)
+    for shift in range(groups):
+        block = slice(shift * capacity, (shift + 1) * capacity)
+        outs[shift][:capacity] = (keep[block] + got[block].astype(F32)).astype(BF16)
+        outs[shift][capacity:, :capacity] = halves_of(stat[:, block])
+        outs[shift][capacity:, capacity:] = jnp.zeros((EXTRA, outs[shift].shape[1] - capacity), BF16)
+
+
+def join_kernel(shift, keep, got, crossed, stat_ref, out):
+    capacity = out.shape[0] - EXTRA
+    block = slice(shift * capacity, (shift + 1) * capacity)
+    out[:capacity] = (keep[block] + got[block].astype(F32) + crossed[:capacity].astype(F32)).astype(BF16)
+    out[capacity:, :capacity] = halves_of(stat_ref[0:1, block] + row_of(crossed[capacity:, :capacity]))
+    out[capacity:, capacity:] = jnp.zeros((EXTRA, out.shape[1] - capacity), BF16)
+
+
+def grad_kernel(left_ref, rows_ref, out_ref):
+    out_ref[0] = dot_nn(left_ref[...], rows_ref[...]).astype(BF16)
+
+
+def weight_grad(left, rows):
+    units, count = left.shape
+    features = rows.shape[1]
+    tile = 512 if features % 512 == 0 else features
+    return pl.pallas_call(
+        grad_kernel,
+        out_shape=jax.ShapeDtypeStruct((1, units, features), BF16),
+        grid=(features // tile,),
+        in_specs=[
+            pl.BlockSpec((units, count), lambda i: (0, 0)),
+            pl.BlockSpec((count, tile), lambda i: (0, i)),
+        ],
+        out_specs=pl.BlockSpec((1, units, tile), lambda i: (0, 0, i)),
+        compiler_params=pltpu.CompilerParams(vmem_limit_bytes=8 * MIB),
+        cost_estimate=pl.CostEstimate(flops=0, bytes_accessed=0, transcendentals=0),
+    )(left, rows)
+
+
+def finish_kernel(groups, ids_ref, gates_in_ref, *refs):
+    parts = refs[:groups]
+    grad_ref, gates_ref = refs[groups:]
+    me = lax.axis_index("node")
+    ids = ids_ref[...]
+    capacity = ids.shape[1] // 2
+    total = jnp.zeros(grad_ref.shape, F32)
+    gates = jnp.zeros(ids.shape, F32)
+    for shift in range(groups):
+        expert = me ^ shift
+        chosen = slots_of(ids, expert, capacity)
+        total = total + dot_tn(chosen.astype(BF16), parts[shift][:capacity])
+        halves = dot_nn(parts[shift][capacity:, :capacity], chosen.astype(BF16))
+        gates = gates + jnp.where(ids == expert, halves[0:1] + halves[1:2], 0.0)
+    grad_ref[...] = total.astype(BF16)
+    gates_ref[...] = gates / gates_in_ref[...].astype(F32)
+
+
+def fast_local(hidden_in, out_grad, expert_ids, gate_weights, w_gate, w_up, w_down):
+    groups = lax.axis_size("node")
+    experts = lax.axis_size("expert")
+    tokens, width = hidden_in.shape
+    capacity = tokens // 2
+    rows = groups * capacity
+    units, features = w_gate.shape[1:]
+    shape = jax.ShapeDtypeStruct
+    after = lax.optimization_barrier
+
+    def over_node(x, shift):
+        return lax.ppermute(x, "node", [(i, i ^ shift) for i in range(groups)])
+
+    def over_expert(x, relative):
+        return lax.ppermute(x, "expert", [(i, i ^ relative) for i in range(experts)])
+
+    ids, gates = expert_ids.T, gate_weights.T
+    blocks = call(
+        functools.partial(pack_kernel, groups),
+        [shape((tokens, width), BF16)] * groups,
+        ids, gates, hidden_in, out_grad,
+        flops=4 * rows * tokens * width, nbytes=6 * tokens * width, in_hbm=(0, 1, 2, 3),
+        scratch=[
+            pltpu.VMEM(ids.shape, ids.dtype), pltpu.VMEM(gates.shape, gates.dtype),
+            pltpu.VMEM((tokens, width), BF16), pltpu.VMEM((tokens, width), BF16), pltpu.SemaphoreType.DMA((4,)),
+        ],
+    )
+    own = [blocks[0]] + [over_node(blocks[s], s) for s in range(1, groups)]
+    partner = [over_expert(x, 1) for x in own]
+    mats = after((w_gate, w_up, w_down, own[1]))[:3]
+    mats = call(load_kernel, [shape(m.shape, BF16) for m in mats], *mats, nbytes=12 * units * features,
+                in_hbm=(0, 1, 2), scratch=[pltpu.SemaphoreType.DMA((3,))])
+    other = [over_expert(own[0], 2)]
+    other.append(over_expert(own[1], 2))
+    for s in range(2, groups):
+        other.append(over_expert(after((own[s], other[1], mats[0]))[0], 2))
+    across = [over_expert(x, 1) for x in other]
+
+    dense = 2 * rows * units * features
+    partial_sums = call(
+        functools.partial(local_kernel, groups),
+        [shape((units, rows), F32)] * 3,
+        *own, *partner, *mats, flops=3 * dense // 2, nbytes=3 * units * features,
+        scratch=[pltpu.VMEM((rows, 2 * width), BF16)] * 2,
+    )
+    rows_in, rows_grad, dgate, dup, hid, stat = call(
+        functools.partial(middle_kernel, groups),
+        [shape((rows, features), BF16)] * 2 + [shape((units, rows), BF16)] * 3 + [shape((8, rows), F32)],
+        *other, *across, *own, *partner, *mats, *partial_sums,
+        flops=3 * dense // 2, nbytes=3 * units * features,
+    )
+
+    def input_part(far):
+        return call(
+            functools.partial(input_kernel, far),
+            [shape((rows + (EXTRA if far else 0), width), BF16), shape((rows, width), F32)],
+            dgate, dup, mats[0], mats[1], stat, flops=dense, nbytes=2 * units * features,
+        )
+
+    far_give, far_keep = input_part(2)
+    far_got = over_expert(far_give, 1)
+    near_give, near_keep = input_part(0)
+    near_got = over_expert(near_give, 1)
+    *far_sum, stat_pair = call(
+        functools.partial(add_kernel, groups),
+        [shape((capacity + EXTRA, width), BF16)] * groups + [shape((8, rows), F32)],
+        far_keep, far_got, stat, nbytes=6 * rows * width,
+    )
+    back, totals = [None] * groups, []
+    for s in reversed(range(groups)):
+        totals += call(functools.partial(join_kernel, s), [shape((capacity + EXTRA, width), BF16)],
+                       near_keep, near_got, over_expert(far_sum[s], 2), stat_pair)
+        back[s] = over_node(totals[-1], s) if s else totals[-1]
+
+    dgate, dup, hid, _ = after((dgate, dup, hid, tuple(totals[:-1])))
+    weight_grads = [weight_grad(dgate, rows_in), weight_grad(dup, rows_in), weight_grad(hid, rows_grad)]
+
+    grad_in, grad_gates = call(
+        functools.partial(finish_kernel, groups),
+        [shape((tokens, width), BF16), shape(ids.shape, F32)],
+        ids, gates, *back,
+    )
+    return (grad_in, grad_gates.T, *weight_grads)
 
 
 def contract_rows(left, right):
@@ -36,7 +331,7 @@
     return (grad_gate, grad_up, grad_down, grad_gate_pre, grad_up_pre, statistic)
 
 
-def local(hidden_in, out_grad, expert_ids, gate_weights, w_gate, w_up, w_down):
+def general_local(hidden_in, out_grad, expert_ids, gate_weights, w_gate, w_up, w_down):
     groups = lax.axis_size("node")
     count_tok = hidden_in.shape[0]
     capacity = count_tok // 2
@@ -107,6 +402,12 @@
     grad_in = (flat_input[flat_index[:, 0]] + flat_input[flat_index[:, 1]]).astype(jnp.bfloat16)
     grad_gates = flat_stat[flat_index]
     return (grad_in, grad_gates, grad_gate[None], grad_up[None], grad_down[None])
+
+
+def local(hidden_in, *rest):
+    if lax.axis_size("expert") == 4 and hidden_in.shape[1] % 128 == 0:
+        return fast_local(hidden_in, *rest)
+    return general_local(hidden_in, *rest)
 
 
 def solution(mesh):

time: 166 us -> 78.1 us (0.47)
  blocking collectives: 49.4 us -> 0 us
  matrix products: 34.5 us -> 0 us
  Pallas kernels: 0 us -> 30.5 us
  waiting for transfers between devices: 42.6 us -> 21.9 us
  starting transfers between devices: 9.48 us -> 24.7 us
  between operations: 14 us -> 0.78 us
  local copies, waits for them, and re-layouts: 13 us -> 0.01 us
  other arithmetic: 2.95 us -> 0 us
    all_to_all x3 -> x0, blocking collectives: 43 us -> none  [the longest x1 19.3 us: local(): lax.all_to_all(pack_rows(hidden_in), 'node', split_axis=0, concat_axis=0,...]
    dot_general x8 -> x0, matrix products: 34.5 us -> none  [the longest x3 13.6 us: contract_cols(): lax.dot_general(left, right, (((1,), (1,)), ((), ())), preferred_element_...]
    pallas_call x0 -> x15, Pallas kernels: none -> 30.5 us  [the longest x12 16.5 us: call(): pl.pallas_call(kernel, out_shape=outs, in_specs=[pl.BlockSpec(memory_spac...]
    ppermute x0 -> x24, starting transfers between devices: none -> 24.7 us  [the longest x6 14.8 us: over_node(): return lax.ppermute(x, 'node', [(i, i ^ shift) for i in range(groups)])]
    reduce_scatter x1 -> x0, waiting for transfers between devices: 24.7 us -> none  [local(): lax.psum_scatter(input_part, 'expert', scatter_dimension=1, tiled=True)]
    ppermute x0 -> x24, waiting for transfers between devices: none -> 21.9 us  [the longest x18 12.1 us: over_expert(): lax.ppermute(x, 'expert', [(i, i ^ relative) for i in range(experts)])]
    gather x13 -> x0, local copies, waits for them, and re-layouts: 10.9 us -> none  [the longest x2 2.44 us: local(): weight_of[token_of, group_ids[:, None]]]
    all_to_all x2 -> x0, waiting for transfers between devices: 10.5 us -> none  [the longest x1 7.47 us: local(): lax.all_to_all(input_slice.reshape(groups, capacity, slice_width), 'node'...]
  transfers between devices with their start and end apart: 5 -> 24, of which waited for: 4 -> 5; matrix products, arithmetic and copies ran while one was open for 18% -> 0% of each run, Pallas kernels for 0% -> 30%
where the time goes in v2:
time: 78.1 us; the launch traced here: 77.9 us
  Pallas kernels  30.5 us (39%)
  starting transfers between devices  24.7 us (32%)
  waiting for transfers between devices  21.9 us (28%)
    pallas_call x12, Pallas kernels, call(): pl.pallas_call(kernel, out_shape=outs, in_specs=[pl.BlockSpec(memory_spac...  16.5 us
    ppermute x6, starting transfers between devices, over_node(): return lax.ppermute(x, 'node', [(i, i ^ shift) for i in range(groups)])  14.8 us
    pallas_call x3, Pallas kernels, weight_grad(): pl.pallas_call(grad_kernel, out_shape=jax.ShapeDtypeStruct((1, units, fea...  14.1 us
    ppermute x18, waiting for transfers between devices, over_expert(): lax.ppermute(x, 'expert', [(i, i ^ relative) for i in range(experts)])  12.1 us
    ppermute x18, starting transfers between devices, over_expert(): lax.ppermute(x, 'expert', [(i, i ^ relative) for i in range(experts)])  9.91 us
    ppermute x6, waiting for transfers between devices, over_node(): return lax.ppermute(x, 'node', [(i, i ^ shift) for i in range(groups)])  9.81 us
  transfers between devices with their start and end apart: 24, of which 5 were waited for; matrix products, arithmetic and copies ran while one was open for 0% of the time, Pallas kernels for 30%

profile of v2, /device:TPU:0, one launch (start us, length us, event | category | flops | bytes accessed | tf_op | source)
XLA Modules:
  0.0 77.9 jit_solution(5258469960060618425)
XLA Ops:
  0.6 1.6 %shard_map.110 = (bf16[128,896]{1,0:T(8,128)(2,1)S(1)}, bf16[128,896]{1,0:T(8,128)(2,1)S(1)}, bf16[128,896]{1,0:T(8,128)(2,1)S(1)}, bf16[128,896]{1,0:T(8,128)(2,1)S(1)}) custom-call(s32[2,128]{1,0:T(2,128)} %bitcast.3, bf16[2,128]{1,0:T(2,128)(2,1)} %bitcast.5, bf16[128,896]{1,0:T(8,128)(2,1)} %refs_2_.1, bf16[128,896]{1,0:T(8,128)(2,1)} %refs_3_.1), custom_call_target="tpu_custom_call" | custom-call | flops 117440512 | bytes 688128 | tf_op jit(solution)/shard_map/pallas_call | solution.py:31
  2.2 3.1 %collective-permute-start.1 = (bf16[128,896]{1,0:T(8,128)(2,1)S(1)}, bf16[128,896]{1,0:T(8,128)(2,1)S(1)}, u32[]{:S(2)}, u32[]{:S(2)}) collective-permute-start(bf16[128,896]{1,0:T(8,128)(2,1)S(1)} %get-tuple-element.41), channel_id=1, source_target_pairs={{0,4},{4,0},{8,12},{12,8},{1,5},{5,1},{9,13},{13,9},{2,6},{6,2},{1... | collective-permute-start | bytes 688136 | tf_op jit(solution)/shard_map/ppermute | solution.py:228
  5.3 2.6 %collective-permute-start.3 = (bf16[128,896]{1,0:T(8,128)(2,1)S(1)}, bf16[128,896]{1,0:T(8,128)(2,1)S(1)}, u32[]{:S(2)}, u32[]{:S(2)}) collective-permute-start(bf16[128,896]{1,0:T(8,128)(2,1)S(1)} %get-tuple-element.42), channel_id=1, source_target_pairs={{0,8},{4,12},{8,0},{12,4},{1,9},{5,13},{9,1},{13,5},{2,10},{6,14},... | collective-permute-start | bytes 688136 | tf_op jit(solution)/shard_map/ppermute | solution.py:228
  7.9 7.2 %collective-permute-done.1.refs_1_.refs_9_ = bf16[128,896]{1,0:T(8,128)(2,1)S(1)} collective-permute-done((bf16[128,896]{1,0:T(8,128)(2,1)S(1)}, bf16[128,896]{1,0:T(8,128)(2,1)S(1)}, u32[]{:S(2)}, u32[]{:S(2)}) %collective-permute-start.1) | collective-permute-done | bytes 229408 | tf_op jit(solution)/shard_map/ppermute | solution.py:228
  15.1 1.7 %collective-permute-start.2 = (bf16[128,896]{1,0:T(8,128)(2,1)S(1)}, bf16[128,896]{1,0:T(8,128)(2,1)S(1)}, u32[]{:S(2)}, u32[]{:S(2)}) collective-permute-start(bf16[128,896]{1,0:T(8,128)(2,1)S(1)} %collective-permute-done.1.refs_1_.refs_9_), channel_id=1, source_target_pairs={{0,2},{1,3},{2,0},{3,1},{4,6},{5,7},{6,4},{7,5},{8,10},{9,11},{10,... | collective-permute-start | bytes 688136 | tf_op jit(solution)/shard_map/ppermute | solution.py:231
  17.1 4.8 %shard_map.111 = (bf16[1,608,3584]{2,1,0:T(8,128)(2,1)S(1)}, bf16[1,608,3584]{2,1,0:T(8,128)(2,1)S(1)}, bf16[1,608,3584]{2,1,0:T(8,128)(2,1)S(1)}) custom-call(bf16[1,608,3584]{2,1,0:T(8,128)(2,1)} %refs_0_, bf16[1,608,3584]{2,1,0:T(8,128)(2,1)} %refs_1_, bf16[1,608,3584]{2,1,0:T(8,128)(2,1)} %refs_2_.2), custom_call_target="tpu_custom_call" | custom-call | bytes 26148864 | tf_op jit(solution)/shard_map/pallas_call | solution.py:31
  21.9 2.6 %collective-permute-done.3.refs_2_.refs_10_ = bf16[128,896]{1,0:T(8,128)(2,1)S(1)} collective-permute-done((bf16[128,896]{1,0:T(8,128)(2,1)S(1)}, bf16[128,896]{1,0:T(8,128)(2,1)S(1)}, u32[]{:S(2)}, u32[]{:S(2)}) %collective-permute-start.3) | collective-permute-done | bytes 229408 | tf_op jit(solution)/shard_map/ppermute | solution.py:228
  25.1 1.5 %collective-permute-start.4 = (bf16[128,896]{1,0:T(8,128)(2,1)S(1)}, bf16[128,896]{1,0:T(8,128)(2,1)S(1)}, u32[]{:S(2)}, u32[]{:S(2)}) collective-permute-start(bf16[128,896]{1,0:T(8,128)(2,1)S(1)} %collective-permute-done.3.refs_2_.refs_10_), channel_id=1, source_target_pairs={{0,2},{1,3},{2,0},{3,1},{4,6},{5,7},{6,4},{7,5},{8,10},{9,11},{10,... | collective-permute-start | bytes 688136 | tf_op jit(solution)/shard_map/ppermute | solution.py:231
  27.7 5.8 %collective-permute-done.4.refs_2_ = bf16[128,896]{1,0:T(8,128)(2,1)S(1)} collective-permute-done((bf16[128,896]{1,0:T(8,128)(2,1)S(1)}, bf16[128,896]{1,0:T(8,128)(2,1)S(1)}, u32[]{:S(2)}, u32[]{:S(2)}) %collective-permute-start.4) | collective-permute-done | bytes 229408 | tf_op jit(solution)/shard_map/ppermute | solution.py:231
  33.6 4.0 %collective-permute-done.6.refs_3_ = bf16[128,896]{1,0:T(8,128)(2,1)S(1)} collective-permute-done((bf16[128,896]{1,0:T(8,128)(2,1)S(1)}, bf16[128,896]{1,0:T(8,128)(2,1)S(1)}, u32[]{:S(2)}, u32[]{:S(2)}) %collective-permute-start.6) | collective-permute-done | bytes 229408 | tf_op jit(solution)/shard_map/ppermute | solution.py:231
  37.6 2.0 %shard_map.112 = (f32[608,256]{1,0:T(8,128)S(1)}, f32[608,256]{1,0:T(8,128)S(1)}, f32[608,256]{1,0:T(8,128)S(1)}) custom-call(bf16[128,896]{1,0:T(8,128)(2,1)S(1)} %get-tuple-element.40.refs_0_.refs_8_, bf16[128,896]{1,0:T(8,128)(2,1)S(1)} %collective-permute-done.1.refs_1_.refs_9_, bf16[128,896]{1,0:T(8,128)(2,1)S(1)} %collective-permute-done.3.refs_2_.refs_10_, ...), custom_call_target="tpu_custom_call" | custom-call | flops 1673527296 | bytes 6537216 | tf_op jit(solution)/shard_map/pallas_call | solution.py:31
  39.6 2.3 %shard_map.113 = (bf16[256,3584]{1,0:T(8,128)(2,1)S(1)}, bf16[256,3584]{1,0:T(8,128)(2,1)S(1)}, bf16[608,256]{1,0:T(8,128)(2,1)S(1)}, bf16[608,256]{1,0:T(8,128)...) custom-call(bf16[128,896]{1,0:T(8,128)(2,1)S(1)} %collective-permute-done.refs_0_, ...), custom_call_target="tpu_custom_call" | custom-call | flops 1673527296 | bytes 6537216 | tf_op jit(solution)/shard_map/pallas_call | solution.py:31
  41.9 1.8 %shard_map.115 = (bf16[264,896]{1,0:T(8,128)(2,1)S(1)}, f32[256,896]{1,0:T(8,128)S(1)}) custom-call(bf16[608,256]{1,0:T(8,128)(2,1)S(1)} %get-tuple-element.70.dgate_ref.left_ref, bf16[608,256]{1,0:T(8,128)(2,1)S(1)} %get-tuple-element.72.dup_ref.left_ref, bf16[1,608,3584]{2,1,0:T(8,128)(2,1)S(1)} %get-tuple-element.46.refs_8_.refs_16_.gate_w, ...), custom_call_target="tpu_custom_call" | custom-call | flops 1115684864 | bytes 4358144 | tf_op jit(solution)/shard_map/pallas_call | solution.py:31
  44.2 1.8 %shard_map.114 = (bf16[256,896]{1,0:T(8,128)(2,1)S(1)}, f32[256,896]{1,0:T(8,128)S(1)}) custom-call(bf16[608,256]{1,0:T(8,128)(2,1)S(1)} %get-tuple-element.70.dgate_ref.left_ref, bf16[608,256]{1,0:T(8,128)(2,1)S(1)} %get-tuple-element.72.dup_ref.left_ref, bf16[1,608,3584]{2,1,0:T(8,128)(2,1)S(1)} %get-tuple-element.46.refs_8_.refs_16_.gate_w, ...), custom_call_target="tpu_custom_call" | custom-call | flops 1115684864 | bytes 4358144 | tf_op jit(solution)/shard_map/pallas_call | solution.py:31
  46.2 1.6 %collective-permute-start.18 = (bf16[72,896]{1,0:T(8,128)(2,1)S(1)}, bf16[72,896]{1,0:T(8,128)(2,1)S(1)}, u32[]{:S(2)}, u32[]{:S(2)}) collective-permute-start(bf16[72,896]{1,0:T(8,128)(2,1)S(1)} %get-tuple-element.64), channel_id=1, source_target_pairs={{0,2},{1,3},{2,0},{3,1},{4,6},{5,7},{6,4},{7,5},{8,10},{9,11},{10,... | collective-permute-start | bytes 387080 | tf_op jit(solution)/shard_map/ppermute | solution.py:231
  48.3 1.5 %collective-permute-start.22 = (bf16[72,896]{1,0:T(8,128)(2,1)S(1)}, bf16[72,896]{1,0:T(8,128)(2,1)S(1)}, u32[]{:S(2)}, u32[]{:S(2)}) collective-permute-start(bf16[72,896]{1,0:T(8,128)(2,1)S(1)} %get-tuple-element.66), channel_id=1, source_target_pairs={{0,2},{1,3},{2,0},{3,1},{4,6},{5,7},{6,4},{7,5},{8,10},{9,11},{10,... | collective-permute-start | bytes 387080 | tf_op jit(solution)/shard_map/ppermute | solution.py:231
  50.3 2.2 %collective-permute-done.18.crossed = bf16[72,896]{1,0:T(8,128)(2,1)S(1)} collective-permute-done((bf16[72,896]{1,0:T(8,128)(2,1)S(1)}, bf16[72,896]{1,0:T(8,128)(2,1)S(1)}, u32[]{:S(2)}, u32[]{:S(2)}) %collective-permute-start.18) | collective-permute-done | bytes 129056 | tf_op jit(solution)/shard_map/ppermute | solution.py:231
  52.7 4.0 %collective-permute-start.19 = (bf16[72,896]{1,0:T(8,128)(2,1)S(1)}, bf16[72,896]{1,0:T(8,128)(2,1)S(1)}, u32[]{:S(2)}, u32[]{:S(2)}) collective-permute-start(bf16[72,896]{1,0:T(8,128)(2,1)S(1)} %shard_map.118), channel_id=1, source_target_pairs={{0,4},{4,0},{8,12},{12,8},{1,5},{5,1},{9,13},{13,9},{2,6},{6,2},{1... | collective-permute-start | bytes 387080 | tf_op jit(solution)/shard_map/ppermute | solution.py:228
  56.8 3.6 %collective-permute-start.21 = (bf16[72,896]{1,0:T(8,128)(2,1)S(1)}, bf16[72,896]{1,0:T(8,128)(2,1)S(1)}, u32[]{:S(2)}, u32[]{:S(2)}) collective-permute-start(bf16[72,896]{1,0:T(8,128)(2,1)S(1)} %shard_map.119), channel_id=1, source_target_pairs={{0,8},{4,12},{8,0},{12,4},{1,9},{5,13},{9,1},{13,5},{2,10},{6,14},... | collective-permute-start | bytes 387080 | tf_op jit(solution)/shard_map/ppermute | solution.py:228
  60.6 1.4 %collective-permute-start.23 = (bf16[72,896]{1,0:T(8,128)(2,1)S(1)}, bf16[72,896]{1,0:T(8,128)(2,1)S(1)}, u32[]{:S(2)}, u32[]{:S(2)}) collective-permute-start(bf16[72,896]{1,0:T(8,128)(2,1)S(1)} %shard_map.120), channel_id=1, source_target_pairs={{0,12},{4,8},{8,4},{12,0},{1,13},{5,9},{9,5},{13,1},{2,14},{6,10},... | collective-permute-start | bytes 387080 | tf_op jit(solution)/shard_map/ppermute | solution.py:228
  62.0 4.7 %shard_map.122 = bf16[1,608,3584]{2,1,0:T(8,128)(2,1)} custom-call(bf16[608,256]{1,0:T(8,128)(2,1)S(1)} %get-tuple-element.70.dgate_ref.left_ref, bf16[256,3584]{1,0:T(8,128)(2,1)S(1)} %get-tuple-element.71.rows_ref), custom_call_target="tpu_custom_call" | custom-call | tf_op jit(solution)/shard_map/pallas_call | solution.py:185
  66.6 4.7 %shard_map.123 = bf16[1,608,3584]{2,1,0:T(8,128)(2,1)} custom-call(bf16[608,256]{1,0:T(8,128)(2,1)S(1)} %get-tuple-element.72.dup_ref.left_ref, bf16[256,3584]{1,0:T(8,128)(2,1)S(1)} %get-tuple-element.71.rows_ref), custom_call_target="tpu_custom_call" | custom-call | tf_op jit(solution)/shard_map/pallas_call | solution.py:185
  71.3 4.7 %shard_map.124 = bf16[1,608,3584]{2,1,0:T(8,128)(2,1)} custom-call(bf16[608,256]{1,0:T(8,128)(2,1)S(1)} %get-tuple-element.73.left_ref, bf16[256,3584]{1,0:T(8,128)(2,1)S(1)} %get-tuple-element.74.rows_ref), custom_call_target="tpu_custom_call" | custom-call | tf_op jit(solution)/shard_map/pallas_call | solution.py:185
  76.1 1.8 %shard_map.121 = (bf16[128,896]{1,0:T(8,128)(2,1)}, f32[2,128]{1,0:T(2,128)}) custom-call(s32[2,128]{1,0:T(2,128)S(1)} %bitcast.4, bf16[2,128]{1,0:T(2,128)(2,1)S(1)} %bitcast.6, bf16[72,896]{1,0:T(8,128)(2,1)S(1)} %shard_map.117.refs_0_, bf16[72,896]{1,0:T(8,128)(2,1)S(1)} %collective-permute-done.19.refs_1_, ...), custom_call_target="tpu_custom_call" | custom-call | tf_op jit(solution)/shard_map/pallas_call | solution.py:31
  (43 shorter events, 4.2 us)
Async XLA Ops:
  2.2 12.8 %collective-permute-start.1 = (bf16[128,896]{1,0:T(8,128)(2,1)S(1)}, bf16[128,896]{1,0:T(8,128)(2,1)S(1)}, u32[]{:S(2)}, u32[]{:S(2)}) collective-permute-start(bf16[128,896]{1,0:T(8,128)(2,1)S(1)} %get-tuple-element.41), channel_id=1, source_target_pairs={{0,4},{4,0},{8,12},{12,8},{1,5},{5,1},{9,13},{13,9},{2,6},{6,2},{1... | collective-permute-start | bytes 688136 | tf_op jit(solution)/shard_map/ppermute | solution.py:228
  5.3 19.3 %collective-permute-start.3 = (bf16[128,896]{1,0:T(8,128)(2,1)S(1)}, bf16[128,896]{1,0:T(8,128)(2,1)S(1)}, u32[]{:S(2)}, u32[]{:S(2)}) collective-permute-start(bf16[128,896]{1,0:T(8,128)(2,1)S(1)} %get-tuple-element.42), channel_id=1, source_target_pairs={{0,8},{4,12},{8,0},{12,4},{1,9},{5,13},{9,1},{13,5},{2,10},{6,14},... | collective-permute-start | bytes 688136 | tf_op jit(solution)/shard_map/ppermute | solution.py:228
  7.9 16.7 %collective-permute-start.5 = (bf16[128,896]{1,0:T(8,128)(2,1)S(1)}, bf16[128,896]{1,0:T(8,128)(2,1)S(1)}, u32[]{:S(2)}, u32[]{:S(2)}) collective-permute-start(bf16[128,896]{1,0:T(8,128)(2,1)S(1)} %get-tuple-element.48), channel_id=1, source_target_pairs={{0,12},{4,8},{8,4},{12,0},{1,13},{5,9},{9,5},{13,1},{2,14},{6,10},... | collective-permute-start | bytes 688136 | tf_op jit(solution)/shard_map/ppermute | solution.py:228
  15.1 10.0 %collective-permute-start.2 = (bf16[128,896]{1,0:T(8,128)(2,1)S(1)}, bf16[128,896]{1,0:T(8,128)(2,1)S(1)}, u32[]{:S(2)}, u32[]{:S(2)}) collective-permute-start(bf16[128,896]{1,0:T(8,128)(2,1)S(1)} %collective-permute-done.1.refs_1_.refs_9_), channel_id=1, source_target_pairs={{0,2},{1,3},{2,0},{3,1},{4,6},{5,7},{6,4},{7,5},{8,10},{9,11},{10,... | collective-permute-start | bytes 688136 | tf_op jit(solution)/shard_map/ppermute | solution.py:231
  16.8 9.9 %collective-permute-start.11 = (bf16[128,896]{1,0:T(8,128)(2,1)S(1)}, bf16[128,896]{1,0:T(8,128)(2,1)S(1)}, u32[]{:S(2)}, u32[]{:S(2)}) collective-permute-start(bf16[128,896]{1,0:T(8,128)(2,1)S(1)} %get-tuple-element.40.refs_0_.refs_8_), channel_id=1, source_target_pairs={{0,1},{1,0},{2,3},{3,2},{4,5},{5,4},{6,7},{7,6},{8,9},{9,8},{10,11... | collective-permute-start | bytes 688136 | tf_op jit(solution)/shard_map/ppermute | solution.py:231
  16.8 10.4 %collective-permute-start = (bf16[128,896]{1,0:T(8,128)(2,1)S(1)}, bf16[128,896]{1,0:T(8,128)(2,1)S(1)}, u32[]{:S(2)}, u32[]{:S(2)}) collective-permute-start(bf16[128,896]{1,0:T(8,128)(2,1)S(1)} %get-tuple-element.40.refs_0_.refs_8_), channel_id=1, source_target_pairs={{0,2},{1,3},{2,0},{3,1},{4,6},{5,7},{6,4},{7,5},{8,10},{9,11},{10,... | collective-permute-start | bytes 688136 | tf_op jit(solution)/shard_map/ppermute | solution.py:231
  24.6 2.6 %collective-permute-start.12 = (bf16[128,896]{1,0:T(8,128)(2,1)S(1)}, bf16[128,896]{1,0:T(8,128)(2,1)S(1)}, u32[]{:S(2)}, u32[]{:S(2)}) collective-permute-start(bf16[128,896]{1,0:T(8,128)(2,1)S(1)} %collective-permute-done.1.refs_1_.refs_9_), channel_id=1, source_target_pairs={{0,1},{1,0},{2,3},{3,2},{4,5},{5,4},{6,7},{7,6},{8,9},{9,8},{10,11... | collective-permute-start | bytes 688136 | tf_op jit(solution)/shard_map/ppermute | solution.py:231
  24.6 3.1 %collective-permute-start.13 = (bf16[128,896]{1,0:T(8,128)(2,1)S(1)}, bf16[128,896]{1,0:T(8,128)(2,1)S(1)}, u32[]{:S(2)}, u32[]{:S(2)}) collective-permute-start(bf16[128,896]{1,0:T(8,128)(2,1)S(1)} %collective-permute-done.3.refs_2_.refs_10_), channel_id=1, source_target_pairs={{0,1},{1,0},{2,3},{3,2},{4,5},{5,4},{6,7},{7,6},{8,9},{9,8},{10,11... | collective-permute-start | bytes 688136 | tf_op jit(solution)/shard_map/ppermute | solution.py:231
  25.1 8.5 %collective-permute-start.4 = (bf16[128,896]{1,0:T(8,128)(2,1)S(1)}, bf16[128,896]{1,0:T(8,128)(2,1)S(1)}, u32[]{:S(2)}, u32[]{:S(2)}) collective-permute-start(bf16[128,896]{1,0:T(8,128)(2,1)S(1)} %collective-permute-done.3.refs_2_.refs_10_), channel_id=1, source_target_pairs={{0,2},{1,3},{2,0},{3,1},{4,6},{5,7},{6,4},{7,5},{8,10},{9,11},{10,... | collective-permute-start | bytes 688136 | tf_op jit(solution)/shard_map/ppermute | solution.py:231
  26.6 11.0 %collective-permute-start.6 = (bf16[128,896]{1,0:T(8,128)(2,1)S(1)}, bf16[128,896]{1,0:T(8,128)(2,1)S(1)}, u32[]{:S(2)}, u32[]{:S(2)}) collective-permute-start(bf16[128,896]{1,0:T(8,128)(2,1)S(1)} %collective-permute-done.5.refs_3_.refs_11_), channel_id=1, source_target_pairs={{0,2},{1,3},{2,0},{3,1},{4,6},{5,7},{6,4},{7,5},{8,10},{9,11},{10,... | collective-permute-start | bytes 688136 | tf_op jit(solution)/shard_map/ppermute | solution.py:231
  27.1 10.5 %collective-permute-start.14 = (bf16[128,896]{1,0:T(8,128)(2,1)S(1)}, bf16[128,896]{1,0:T(8,128)(2,1)S(1)}, u32[]{:S(2)}, u32[]{:S(2)}) collective-permute-start(bf16[128,896]{1,0:T(8,128)(2,1)S(1)} %collective-permute-done.5.refs_3_.refs_11_), channel_id=1, source_target_pairs={{0,1},{1,0},{2,3},{3,2},{4,5},{5,4},{6,7},{7,6},{8,9},{9,8},{10,11... | collective-permute-start | bytes 688136 | tf_op jit(solution)/shard_map/ppermute | solution.py:231
  27.1 12.4 %collective-permute-start.7 = (bf16[128,896]{1,0:T(8,128)(2,1)S(1)}, bf16[128,896]{1,0:T(8,128)(2,1)S(1)}, u32[]{:S(2)}, u32[]{:S(2)}) collective-permute-start(bf16[128,896]{1,0:T(8,128)(2,1)S(1)} %collective-permute-done.refs_0_), channel_id=1, source_target_pairs={{0,1},{1,0},{2,3},{3,2},{4,5},{5,4},{6,7},{7,6},{8,9},{9,8},{10,11... | collective-permute-start | bytes 688136 | tf_op jit(solution)/shard_map/ppermute | solution.py:231
  27.6 11.9 %collective-permute-start.8 = (bf16[128,896]{1,0:T(8,128)(2,1)S(1)}, bf16[128,896]{1,0:T(8,128)(2,1)S(1)}, u32[]{:S(2)}, u32[]{:S(2)}) collective-permute-start(bf16[128,896]{1,0:T(8,128)(2,1)S(1)} %collective-permute-done.2.refs_1_), channel_id=1, source_target_pairs={{0,1},{1,0},{2,3},{3,2},{4,5},{5,4},{6,7},{7,6},{8,9},{9,8},{10,11... | collective-permute-start | bytes 688136 | tf_op jit(solution)/shard_map/ppermute | solution.py:231
  33.6 6.0 %collective-permute-start.9 = (bf16[128,896]{1,0:T(8,128)(2,1)S(1)}, bf16[128,896]{1,0:T(8,128)(2,1)S(1)}, u32[]{:S(2)}, u32[]{:S(2)}) collective-permute-start(bf16[128,896]{1,0:T(8,128)(2,1)S(1)} %collective-permute-done.4.refs_2_), channel_id=1, source_target_pairs={{0,1},{1,0},{2,3},{3,2},{4,5},{5,4},{6,7},{7,6},{8,9},{9,8},{10,11... | collective-permute-start | bytes 688136 | tf_op jit(solution)/shard_map/ppermute | solution.py:231
  37.6 2.0 %collective-permute-start.10 = (bf16[128,896]{1,0:T(8,128)(2,1)S(1)}, bf16[128,896]{1,0:T(8,128)(2,1)S(1)}, u32[]{:S(2)}, u32[]{:S(2)}) collective-permute-start(bf16[128,896]{1,0:T(8,128)(2,1)S(1)} %collective-permute-done.6.refs_3_), channel_id=1, source_target_pairs={{0,1},{1,0},{2,3},{3,2},{4,5},{5,4},{6,7},{7,6},{8,9},{9,8},{10,11... | collective-permute-start | bytes 688136 | tf_op jit(solution)/shard_map/ppermute | solution.py:231
  43.7 2.4 %collective-permute-start.16 = (bf16[264,896]{1,0:T(8,128)(2,1)S(1)}, bf16[264,896]{1,0:T(8,128)(2,1)S(1)}, u32[]{:S(2)}, u32[]{:S(2)}) collective-permute-start(bf16[264,896]{1,0:T(8,128)(2,1)S(1)} %get-tuple-element.61), channel_id=1, source_target_pairs={{0,1},{1,0},{2,3},{3,2},{4,5},{5,4},{6,7},{7,6},{8,9},{9,8},{10,11... | collective-permute-start | bytes 1419272 | tf_op jit(solution)/shard_map/ppermute | solution.py:231
  46.0 4.3 %collective-permute-start.15 = (bf16[256,896]{1,0:T(8,128)(2,1)S(1)}, bf16[256,896]{1,0:T(8,128)(2,1)S(1)}, u32[]{:S(2)}, u32[]{:S(2)}) collective-permute-start(bf16[256,896]{1,0:T(8,128)(2,1)S(1)} %get-tuple-element.59), channel_id=1, source_target_pairs={{0,1},{1,0},{2,3},{3,2},{4,5},{5,4},{6,7},{7,6},{8,9},{9,8},{10,11... | collective-permute-start | bytes 1376264 | tf_op jit(solution)/shard_map/ppermute | solution.py:231
  46.2 6.3 %collective-permute-start.18 = (bf16[72,896]{1,0:T(8,128)(2,1)S(1)}, bf16[72,896]{1,0:T(8,128)(2,1)S(1)}, u32[]{:S(2)}, u32[]{:S(2)}) collective-permute-start(bf16[72,896]{1,0:T(8,128)(2,1)S(1)} %get-tuple-element.64), channel_id=1, source_target_pairs={{0,2},{1,3},{2,0},{3,1},{4,6},{5,7},{6,4},{7,5},{8,10},{9,11},{10,... | collective-permute-start | bytes 387080 | tf_op jit(solution)/shard_map/ppermute | solution.py:231
  47.8 8.9 %collective-permute-start.20 = (bf16[72,896]{1,0:T(8,128)(2,1)S(1)}, bf16[72,896]{1,0:T(8,128)(2,1)S(1)}, u32[]{:S(2)}, u32[]{:S(2)}) collective-permute-start(bf16[72,896]{1,0:T(8,128)(2,1)S(1)} %get-tuple-element.65), channel_id=1, source_target_pairs={{0,2},{1,3},{2,0},{3,1},{4,6},{5,7},{6,4},{7,5},{8,10},{9,11},{10,... | collective-permute-start | bytes 387080 | tf_op jit(solution)/shard_map/ppermute | solution.py:231
  48.3 12.1 %collective-permute-start.22 = (bf16[72,896]{1,0:T(8,128)(2,1)S(1)}, bf16[72,896]{1,0:T(8,128)(2,1)S(1)}, u32[]{:S(2)}, u32[]{:S(2)}) collective-permute-start(bf16[72,896]{1,0:T(8,128)(2,1)S(1)} %get-tuple-element.66), channel_id=1, source_target_pairs={{0,2},{1,3},{2,0},{3,1},{4,6},{5,7},{6,4},{7,5},{8,10},{9,11},{10,... | collective-permute-start | bytes 387080 | tf_op jit(solution)/shard_map/ppermute | solution.py:231
  49.8 26.2 %collective-permute-start.17 = (bf16[72,896]{1,0:T(8,128)(2,1)S(1)}, bf16[72,896]{1,0:T(8,128)(2,1)S(1)}, u32[]{:S(2)}, u32[]{:S(2)}) collective-permute-start(bf16[72,896]{1,0:T(8,128)(2,1)S(1)} %get-tuple-element.62), channel_id=1, source_target_pairs={{0,2},{1,3},{2,0},{3,1},{4,6},{5,7},{6,4},{7,5},{8,10},{9,11},{10,... | collective-permute-start | bytes 387080 | tf_op jit(solution)/shard_map/ppermute | solution.py:231
  52.7 23.4 %collective-permute-start.19 = (bf16[72,896]{1,0:T(8,128)(2,1)S(1)}, bf16[72,896]{1,0:T(8,128)(2,1)S(1)}, u32[]{:S(2)}, u32[]{:S(2)}) collective-permute-start(bf16[72,896]{1,0:T(8,128)(2,1)S(1)} %shard_map.118), channel_id=1, source_target_pairs={{0,4},{4,0},{8,12},{12,8},{1,5},{5,1},{9,13},{13,9},{2,6},{6,2},{1... | collective-permute-start | bytes 387080 | tf_op jit(solution)/shard_map/ppermute | solution.py:228
  56.8 19.3 %collective-permute-start.21 = (bf16[72,896]{1,0:T(8,128)(2,1)S(1)}, bf16[72,896]{1,0:T(8,128)(2,1)S(1)}, u32[]{:S(2)}, u32[]{:S(2)}) collective-permute-start(bf16[72,896]{1,0:T(8,128)(2,1)S(1)} %shard_map.119), channel_id=1, source_target_pairs={{0,8},{4,12},{8,0},{12,4},{1,9},{5,13},{9,1},{13,5},{2,10},{6,14},... | collective-permute-start | bytes 387080 | tf_op jit(solution)/shard_map/ppermute | solution.py:228
  60.6 15.5 %collective-permute-start.23 = (bf16[72,896]{1,0:T(8,128)(2,1)S(1)}, bf16[72,896]{1,0:T(8,128)(2,1)S(1)}, u32[]{:S(2)}, u32[]{:S(2)}) collective-permute-start(bf16[72,896]{1,0:T(8,128)(2,1)S(1)} %shard_map.120), channel_id=1, source_target_pairs={{0,12},{4,8},{8,4},{12,0},{1,13},{5,9},{9,5},{13,1},{2,14},{6,10},... | collective-permute-start | bytes 387080 | tf_op jit(solution)/shard_map/ppermute | solution.py:228
  (2 other events, 9.6 us)

commit v3 on v2

--- a/solution.py
+++ b/solution.py
@@ -75,6 +75,15 @@
         out[capacity:] = dot_nn((one_hot * weight).astype(BF16), grad_ref[...]).astype(BF16)
 
 
+def pick_kernel(groups, ids_ref, out_ref):
+    me = lax.axis_index("node")
+    ids = ids_ref[...]
+    capacity = ids.shape[1] // 2
+    for shift in range(groups):
+        chosen = slots_of(ids, me ^ shift, capacity)
+        out_ref[:, shift * capacity : (shift + 1) * capacity] = chosen.T.astype(BF16)
+
+
 def load_kernel(*refs):
     count = len(refs) // 2
     sources, outs, sems = refs[:count], refs[count : 2 * count], refs[-1]
@@ -140,18 +149,15 @@
     return halves[0:1].astype(F32) + halves[1:2].astype(F32)
 
 
-def input_kernel(far, dgate_ref, dup_ref, gate_w, up_w, stat_ref, give_ref, keep_ref):
+def input_kernel(relative, dgate_ref, dup_ref, gate_w, up_w, stat_ref, out_ref):
     me = lax.axis_index("expert")
-    rows, width = keep_ref.shape
-    dgate = dgate_ref[...].T
-    dup = dup_ref[...].T
-    for ref, relative in ((give_ref, far + 1), (keep_ref, far)):
-        columns = pl.ds(pl.multiple_of((me ^ relative) * width, width), width)
-        total = dot_nn(dgate, gate_w[0, :, columns]) + dot_nn(dup, up_w[0, :, columns])
-        ref[:rows] = total.astype(ref.dtype)
-    if far:
-        give_ref[rows:, :rows] = halves_of(stat_ref[0:1])
-        give_ref[rows:, rows:] = jnp.zeros((EXTRA, width - rows), BF16)
+    rows, width = dgate_ref.shape[1], out_ref.shape[1]
+    columns = pl.ds(pl.multiple_of((me ^ relative) * width, width), width)
+    total = dot_tn(dgate_ref[...], gate_w[0, :, columns]) + dot_tn(dup_ref[...], up_w[0, :, columns])
+    out_ref[:rows] = total.astype(out_ref.dtype)
+    if out_ref.shape[0] > rows:
+        out_ref[rows:, :rows] = halves_of(stat_ref[0:1])
+        out_ref[rows:, rows:] = jnp.zeros((EXTRA, width - rows), BF16)
 
 
 def add_kernel(groups, keep, got, stat_ref, *outs):
@@ -174,43 +180,45 @@
     out[capacity:, capacity:] = jnp.zeros((EXTRA, out.shape[1] - capacity), BF16)
 
 
-def grad_kernel(left_ref, rows_ref, out_ref):
-    out_ref[0] = dot_nn(left_ref[...], rows_ref[...]).astype(BF16)
+def grad_kernel(tile, left_ref, rows_ref, out_ref, held_ref, sems):
+    copies = []
+    for index in range(rows_ref.shape[1] // tile):
+        columns = slice(index * tile, (index + 1) * tile)
+        held_ref[:, columns] = dot_nn(left_ref[...], rows_ref[:, columns]).astype(BF16)
+        copies.append(pltpu.make_async_copy(held_ref.at[:, columns], out_ref.at[0, :, columns], sems.at[index]))
+        copies[-1].start()
+    for copy in copies:
+        copy.wait()
 
 
 def weight_grad(left, rows):
-    units, count = left.shape
-    features = rows.shape[1]
+    units, features = left.shape[0], rows.shape[1]
     tile = 512 if features % 512 == 0 else features
     return pl.pallas_call(
-        grad_kernel,
+        functools.partial(grad_kernel, tile),
         out_shape=jax.ShapeDtypeStruct((1, units, features), BF16),
-        grid=(features // tile,),
-        in_specs=[
-            pl.BlockSpec((units, count), lambda i: (0, 0)),
-            pl.BlockSpec((count, tile), lambda i: (0, i)),
-        ],
-        out_specs=pl.BlockSpec((1, units, tile), lambda i: (0, 0, i)),
-        compiler_params=pltpu.CompilerParams(vmem_limit_bytes=8 * MIB),
+        in_specs=[pl.BlockSpec(memory_space=pltpu.VMEM)] * 2,
+        out_specs=pl.BlockSpec(memory_space=pltpu.HBM),
+        scratch_shapes=[pltpu.VMEM((units, features), BF16), pltpu.SemaphoreType.DMA((features // tile,))],
+        compiler_params=pltpu.CompilerParams(vmem_limit_bytes=10 * MIB),
         cost_estimate=pl.CostEstimate(flops=0, bytes_accessed=0, transcendentals=0),
     )(left, rows)
 
 
-def finish_kernel(groups, ids_ref, gates_in_ref, *refs):
+def finish_kernel(groups, ids_ref, gates_in_ref, pick_ref, *refs):
     parts = refs[:groups]
-    grad_ref, gates_ref = refs[groups:]
+    grad_ref, gates_ref, rows_ref = refs[groups:]
     me = lax.axis_index("node")
     ids = ids_ref[...]
     capacity = ids.shape[1] // 2
-    total = jnp.zeros(grad_ref.shape, F32)
+    for shift in range(groups):
+        rows_ref[shift * capacity : (shift + 1) * capacity] = parts[shift][:capacity]
+    grad_ref[...] = dot_nn(pick_ref[...], rows_ref[...]).astype(BF16)
     gates = jnp.zeros(ids.shape, F32)
     for shift in range(groups):
-        expert = me ^ shift
-        chosen = slots_of(ids, expert, capacity)
-        total = total + dot_tn(chosen.astype(BF16), parts[shift][:capacity])
-        halves = dot_nn(parts[shift][capacity:, :capacity], chosen.astype(BF16))
-        gates = gates + jnp.where(ids == expert, halves[0:1] + halves[1:2], 0.0)
-    grad_ref[...] = total.astype(BF16)
+        columns = slice(shift * capacity, (shift + 1) * capacity)
+        halves = dot_nt(parts[shift][capacity:, :capacity], pick_ref[:, columns])
+        gates = gates + jnp.where(ids == (me ^ shift), halves[0:1] + halves[1:2], 0.0)
     gates_ref[...] = gates / gates_in_ref[...].astype(F32)
 
 
@@ -241,16 +249,23 @@
             pltpu.VMEM((tokens, width), BF16), pltpu.VMEM((tokens, width), BF16), pltpu.SemaphoreType.DMA((4,)),
         ],
     )
-    own = [blocks[0]] + [over_node(blocks[s], s) for s in range(1, groups)]
-    partner = [over_expert(x, 1) for x in own]
-    mats = after((w_gate, w_up, w_down, own[1]))[:3]
+    own = list(blocks)
+    partner, other = [None] * groups, [None] * groups
+    other[0] = over_expert(own[0], 2)
+    partner[0] = over_expert(own[0], 1)
+    own[1] = over_node(blocks[1], 1)
+    partner[1] = over_expert(own[1], 1)
+    own[2] = over_node(blocks[2], 2)
+    partner[2] = over_expert(own[2], 1)
+    own[3] = over_node(blocks[3], 3)
+    partner[3] = over_expert(own[3], 1)
+    mats = after((w_gate, w_up, w_down, other[0]))[:3]
     mats = call(load_kernel, [shape(m.shape, BF16) for m in mats], *mats, nbytes=12 * units * features,
                 in_hbm=(0, 1, 2), scratch=[pltpu.SemaphoreType.DMA((3,))])
-    other = [over_expert(own[0], 2)]
-    other.append(over_expert(own[1], 2))
-    for s in range(2, groups):
-        other.append(over_expert(after((own[s], other[1], mats[0]))[0], 2))
-    across = [over_expert(x, 1) for x in other]
+    other[1] = over_expert(own[1], 2)
+    other[2] = over_expert(own[2], 2)
+    other[3] = over_expert(after((own[3], other[0], other[2]))[0], 2)
+    across = [over_expert(x, 1) for x in other[:-1]]
 
     dense = 2 * rows * units * features
     partial_sums = call(
@@ -259,6 +274,7 @@
         *own, *partner, *mats, flops=3 * dense // 2, nbytes=3 * units * features,
         scratch=[pltpu.VMEM((rows, 2 * width), BF16)] * 2,
     )
+    across.append(over_expert(after((other[-1], partial_sums[0]))[0], 1))
     rows_in, rows_grad, dgate, dup, hid, stat = call(
         functools.partial(middle_kernel, groups),
         [shape((rows, features), BF16)] * 2 + [shape((units, rows), BF16)] * 3 + [shape((8, rows), F32)],
@@ -266,22 +282,21 @@
         flops=3 * dense // 2, nbytes=3 * units * features,
     )
 
-    def input_part(far):
+    def input_part(relative, extra, kind):
         return call(
-            functools.partial(input_kernel, far),
-            [shape((rows + (EXTRA if far else 0), width), BF16), shape((rows, width), F32)],
-            dgate, dup, mats[0], mats[1], stat, flops=dense, nbytes=2 * units * features,
-        )
-
-    far_give, far_keep = input_part(2)
-    far_got = over_expert(far_give, 1)
-    near_give, near_keep = input_part(0)
-    near_got = over_expert(near_give, 1)
+            functools.partial(input_kernel, relative), [shape((rows + extra, width), kind)],
+            dgate, dup, mats[0], mats[1], stat, flops=dense // 2, nbytes=units * features,
+        )[0]
+
+    far_got = over_expert(input_part(3, EXTRA, BF16), 1)
+    near_got = over_expert(input_part(1, 0, BF16), 1)
+    far_keep = input_part(2, 0, F32)
     *far_sum, stat_pair = call(
         functools.partial(add_kernel, groups),
         [shape((capacity + EXTRA, width), BF16)] * groups + [shape((8, rows), F32)],
         far_keep, far_got, stat, nbytes=6 * rows * width,
     )
+    near_keep = input_part(0, 0, F32)
     back, totals = [None] * groups, []
     for s in reversed(range(groups)):
         totals += call(functools.partial(join_kernel, s), [shape((capacity + EXTRA, width), BF16)],
@@ -291,10 +306,11 @@
     dgate, dup, hid, _ = after((dgate, dup, hid, tuple(totals[:-1])))
     weight_grads = [weight_grad(dgate, rows_in), weight_grad(dup, rows_in), weight_grad(hid, rows_grad)]
 
+    pick = call(functools.partial(pick_kernel, groups), [shape((tokens, rows), BF16)], after((ids, own[1]))[0])[0]
     grad_in, grad_gates = call(
         functools.partial(finish_kernel, groups),
         [shape((tokens, width), BF16), shape(ids.shape, F32)],
-        ids, gates, *back,
+        ids, gates, pick, *back, scratch=[pltpu.VMEM((rows, width), BF16)],
     )
     return (grad_in, grad_gates.T, *weight_grads)
 

time: 78.1 us -> 68.9 us (0.88)
  Pallas kernels: 30.5 us -> 23.7 us
  waiting for transfers between devices: 21.9 us -> 20.4 us
  starting transfers between devices: 24.7 us -> 23.9 us
    ppermute x6, starting transfers between devices: 14.8 us -> 7.39 us  [over_node(): return lax.ppermute(x, 'node', [(i, i ^ shift) for i in range(groups)])]
    pallas_call x3, Pallas kernels: 14.1 us -> 7.34 us  [weight_grad(): pl.pallas_call(functools.partial(grad_kernel, tile), out_shape=jax.ShapeD...]
    ppermute x18, starting transfers between devices: 9.91 us -> 16.5 us  [over_expert(): lax.ppermute(x, 'expert', [(i, i ^ relative) for i in range(experts)])]
    ppermute x6, waiting for transfers between devices: 9.81 us -> 8.96 us  [over_node(): return lax.ppermute(x, 'node', [(i, i ^ shift) for i in range(groups)])]
    pallas_call x12 -> x15, Pallas kernels: 16.5 us -> 16.3 us  [call(): pl.pallas_call(kernel, out_shape=outs, in_specs=[pl.BlockSpec(memory_spac...]
  transfers between devices with their start and end apart: 24 -> 24, of which waited for: 5 -> 6; matrix products, arithmetic and copies ran while one was open for 0% -> 0% of each run, Pallas kernels for 30% -> 26%
where the time goes in v3:
time: 68.9 us; the launch traced here: 68.8 us
  starting transfers between devices  23.9 us (35%)
  Pallas kernels  23.7 us (34%)
  waiting for transfers between devices  20.4 us (30%)
  between operations  0.84 us (1%)
    ppermute x18, starting transfers between devices, over_expert(): lax.ppermute(x, 'expert', [(i, i ^ relative) for i in range(experts)])  16.5 us
    pallas_call x15, Pallas kernels, call(): pl.pallas_call(kernel, out_shape=outs, in_specs=[pl.BlockSpec(memory_spac...  16.3 us
    ppermute x18, waiting for transfers between devices, over_expert(): lax.ppermute(x, 'expert', [(i, i ^ relative) for i in range(experts)])  11.4 us
    ppermute x6, waiting for transfers between devices, over_node(): return lax.ppermute(x, 'node', [(i, i ^ shift) for i in range(groups)])  8.96 us
    ppermute x6, starting transfers between devices, over_node(): return lax.ppermute(x, 'node', [(i, i ^ shift) for i in range(groups)])  7.39 us
    pallas_call x3, Pallas kernels, weight_grad(): pl.pallas_call(functools.partial(grad_kernel, tile), out_shape=jax.ShapeD...  7.34 us
  transfers between devices with their start and end apart: 24, of which 6 were waited for; matrix products, arithmetic and copies ran while one was open for 0% of the time, Pallas kernels for 26%

profile of v3, /device:TPU:0, one launch (start us, length us, event | category | flops | bytes accessed | tf_op | source)
XLA Modules:
  0.0 68.8 jit_solution(7680126286240183885)
XLA Ops:
  0.6 1.6 %shard_map.110 = (bf16[128,896]{1,0:T(8,128)(2,1)S(1)}, bf16[128,896]{1,0:T(8,128)(2,1)S(1)}, bf16[128,896]{1,0:T(8,128)(2,1)S(1)}, bf16[128,896]{1,0:T(8,128)(2,1)S(1)}) custom-call(s32[2,128]{1,0:T(2,128)} %bitcast.3, bf16[2,128]{1,0:T(2,128)(2,1)} %bitcast.6, bf16[128,896]{1,0:T(8,128)(2,1)} %refs_2_.1, bf16[128,896]{1,0:T(8,128)(2,1)} %refs_3_.1), custom_call_target="tpu_custom_call" | custom-call | flops 117440512 | bytes 688128 | tf_op jit(solution)/shard_map/pallas_call | solution.py:31
  2.2 4.1 %collective-permute-start.3 = (bf16[128,896]{1,0:T(8,128)(2,1)S(1)}, bf16[128,896]{1,0:T(8,128)(2,1)S(1)}, u32[]{:S(2)}, u32[]{:S(2)}) collective-permute-start(bf16[128,896]{1,0:T(8,128)(2,1)S(1)} %get-tuple-element.40), channel_id=1, source_target_pairs={{0,8},{4,12},{8,0},{12,4},{1,9},{5,13},{9,1},{13,5},{2,10},{6,14},... | collective-permute-start | bytes 688136 | tf_op jit(solution)/shard_map/ppermute | solution.py:236
  6.3 1.6 %collective-permute-start = (bf16[128,896]{1,0:T(8,128)(2,1)S(1)}, bf16[128,896]{1,0:T(8,128)(2,1)S(1)}, u32[]{:S(2)}, u32[]{:S(2)}) collective-permute-start(bf16[128,896]{1,0:T(8,128)(2,1)S(1)} %get-tuple-element.37), channel_id=1, source_target_pairs={{0,4},{4,0},{8,12},{12,8},{1,5},{5,1},{9,13},{13,9},{2,6},{6,2},{1... | collective-permute-start | bytes 688136 | tf_op jit(solution)/shard_map/ppermute | solution.py:236
  7.9 1.5 %collective-permute-start.1 = (bf16[128,896]{1,0:T(8,128)(2,1)S(1)}, bf16[128,896]{1,0:T(8,128)(2,1)S(1)}, u32[]{:S(2)}, u32[]{:S(2)}) collective-permute-start(bf16[128,896]{1,0:T(8,128)(2,1)S(1)} %get-tuple-element.39.refs_0_.refs_8_), channel_id=1, source_target_pairs={{0,2},{1,3},{2,0},{3,1},{4,6},{5,7},{6,4},{7,5},{8,10},{9,11},{10,... | collective-permute-start | bytes 688136 | tf_op jit(solution)/shard_map/ppermute | solution.py:239
  9.6 8.9 %collective-permute-done.3.refs_2_.refs_10_ = bf16[128,896]{1,0:T(8,128)(2,1)S(1)} collective-permute-done((bf16[128,896]{1,0:T(8,128)(2,1)S(1)}, bf16[128,896]{1,0:T(8,128)(2,1)S(1)}, u32[]{:S(2)}, u32[]{:S(2)}) %collective-permute-start.3) | collective-permute-done | bytes 229408 | tf_op jit(solution)/shard_map/ppermute | solution.py:236
  18.6 5.9 %collective-permute-start.4 = (bf16[128,896]{1,0:T(8,128)(2,1)S(1)}, bf16[128,896]{1,0:T(8,128)(2,1)S(1)}, u32[]{:S(2)}, u32[]{:S(2)}) collective-permute-start(bf16[128,896]{1,0:T(8,128)(2,1)S(1)} %collective-permute-done.3.refs_2_.refs_10_), channel_id=1, source_target_pairs={{0,2},{1,3},{2,0},{3,1},{4,6},{5,7},{6,4},{7,5},{8,10},{9,11},{10,... | collective-permute-start | bytes 688136 | tf_op jit(solution)/shard_map/ppermute | solution.py:239
  25.1 5.1 %collective-permute-done.4.refs_2_ = bf16[128,896]{1,0:T(8,128)(2,1)S(1)} collective-permute-done((bf16[128,896]{1,0:T(8,128)(2,1)S(1)}, bf16[128,896]{1,0:T(8,128)(2,1)S(1)}, u32[]{:S(2)}, u32[]{:S(2)}) %collective-permute-start.4) | collective-permute-done | bytes 229408 | tf_op jit(solution)/shard_map/ppermute | solution.py:239
  30.2 2.5 %collective-permute-start.6 = (bf16[128,896]{1,0:T(8,128)(2,1)S(1)}, bf16[128,896]{1,0:T(8,128)(2,1)S(1)}, u32[]{:S(2)}, u32[]{:S(2)}) collective-permute-start(bf16[128,896]{1,0:T(8,128)(2,1)S(1)} %collective-permute-done.5.refs_3_.refs_11_), channel_id=1, source_target_pairs={{0,2},{1,3},{2,0},{3,1},{4,6},{5,7},{6,4},{7,5},{8,10},{9,11},{10,... | collective-permute-start | bytes 688136 | tf_op jit(solution)/shard_map/ppermute | solution.py:239
  32.7 4.8 %shard_map.112 = (bf16[1,608,3584]{2,1,0:T(8,128)(2,1)S(1)}, bf16[1,608,3584]{2,1,0:T(8,128)(2,1)S(1)}, bf16[1,608,3584]{2,1,0:T(8,128)(2,1)S(1)}) custom-call(bf16[1,608,3584]{2,1,0:T(8,128)(2,1)} %refs_0_, bf16[1,608,3584]{2,1,0:T(8,128)(2,1)} %refs_1_, bf16[1,608,3584]{2,1,0:T(8,128)(2,1)} %refs_2_.2), custom_call_target="tpu_custom_call" | custom-call | bytes 26148864 | tf_op jit(solution)/shard_map/pallas_call | solution.py:31
  38.4 2.0 %shard_map.113 = (f32[608,256]{1,0:T(8,128)S(1)}, f32[608,256]{1,0:T(8,128)S(1)}, f32[608,256]{1,0:T(8,128)S(1)}) custom-call(bf16[128,896]{1,0:T(8,128)(2,1)S(1)} %get-tuple-element.39.refs_0_.refs_8_, bf16[128,896]{1,0:T(8,128)(2,1)S(1)} %collective-permute-done.refs_1_.refs_9_, bf16[128,896]{1,0:T(8,128)(2,1)S(1)} %collective-permute-done.3.refs_2_.refs_10_, ...), custom_call_target="tpu_custom_call" | custom-call | flops 1673527296 | bytes 6537216 | tf_op jit(solution)/shard_map/pallas_call | solution.py:31
  40.7 1.2 %collective-permute-done.14.refs_7_ = bf16[128,896]{1,0:T(8,128)(2,1)S(1)} collective-permute-done((bf16[128,896]{1,0:T(8,128)(2,1)S(1)}, bf16[128,896]{1,0:T(8,128)(2,1)S(1)}, u32[]{:S(2)}, u32[]{:S(2)}) %collective-permute-start.14) | collective-permute-done | bytes 229408 | tf_op jit(solution)/shard_map/ppermute | solution.py:239
  41.9 2.3 %shard_map.114 = (bf16[256,3584]{1,0:T(8,128)(2,1)S(1)}, bf16[256,3584]{1,0:T(8,128)(2,1)S(1)}, bf16[608,256]{1,0:T(8,128)(2,1)S(1)}, bf16[608,256]{1,0:T(8,128)...) custom-call(bf16[128,896]{1,0:T(8,128)(2,1)S(1)} %collective-permute-done.1.refs_0_, ...), custom_call_target="tpu_custom_call" | custom-call | flops 1673527296 | bytes 6537216 | tf_op jit(solution)/shard_map/pallas_call | solution.py:31
  44.2 1.0 %shard_map.118 = bf16[264,896]{1,0:T(8,128)(2,1)S(1)} custom-call(bf16[608,256]{1,0:T(8,128)(2,1)S(1)} %get-tuple-element.64.dgate_ref.left_ref, bf16[608,256]{1,0:T(8,128)(2,1)S(1)} %get-tuple-element.66.dup_ref.left_ref, bf16[1,608,3584]{2,1,0:T(8,128)(2,1)S(1)} %get-tuple-element.46.refs_8_.refs_16_.gate_w, ...), custom_call_target="tpu_custom_call" | custom-call | flops 557842432 | bytes 2179072 | tf_op jit(solution)/shard_map/pallas_call | solution.py:31
  45.5 1.0 %shard_map.116 = bf16[256,896]{1,0:T(8,128)(2,1)S(1)} custom-call(bf16[608,256]{1,0:T(8,128)(2,1)S(1)} %get-tuple-element.64.dgate_ref.left_ref, bf16[608,256]{1,0:T(8,128)(2,1)S(1)} %get-tuple-element.66.dup_ref.left_ref, bf16[1,608,3584]{2,1,0:T(8,128)(2,1)S(1)} %get-tuple-element.46.refs_8_.refs_16_.gate_w, ...), custom_call_target="tpu_custom_call" | custom-call | flops 557842432 | bytes 2179072 | tf_op jit(solution)/shard_map/pallas_call | solution.py:31
  46.8 1.0 %shard_map.117.keep = f32[256,896]{1,0:T(8,128)S(1)} custom-call(bf16[608,256]{1,0:T(8,128)(2,1)S(1)} %get-tuple-element.64.dgate_ref.left_ref, bf16[608,256]{1,0:T(8,128)(2,1)S(1)} %get-tuple-element.66.dup_ref.left_ref, bf16[1,608,3584]{2,1,0:T(8,128)(2,1)S(1)} %get-tuple-element.46.refs_8_.refs_16_.gate_w, ...), custom_call_target="tpu_custom_call" | custom-call | flops 557842432 | bytes 2179072 | tf_op jit(solution)/shard_map/pallas_call | solution.py:31
  48.3 1.8 %collective-permute-start.20 = (bf16[72,896]{1,0:T(8,128)(2,1)S(1)}, bf16[72,896]{1,0:T(8,128)(2,1)S(1)}, u32[]{:S(2)}, u32[]{:S(2)}) collective-permute-start(bf16[72,896]{1,0:T(8,128)(2,1)S(1)} %get-tuple-element.59), channel_id=1, source_target_pairs={{0,2},{1,3},{2,0},{3,1},{4,6},{5,7},{6,4},{7,5},{8,10},{9,11},{10,... | collective-permute-start | bytes 387080 | tf_op jit(solution)/shard_map/ppermute | solution.py:239
  51.3 1.9 %collective-permute-start.17 = (bf16[72,896]{1,0:T(8,128)(2,1)S(1)}, bf16[72,896]{1,0:T(8,128)(2,1)S(1)}, u32[]{:S(2)}, u32[]{:S(2)}) collective-permute-start(bf16[72,896]{1,0:T(8,128)(2,1)S(1)} %get-tuple-element.56), channel_id=1, source_target_pairs={{0,2},{1,3},{2,0},{3,1},{4,6},{5,7},{6,4},{7,5},{8,10},{9,11},{10,... | collective-permute-start | bytes 387080 | tf_op jit(solution)/shard_map/ppermute | solution.py:239
  53.1 1.2 %collective-permute-done.22.crossed = bf16[72,896]{1,0:T(8,128)(2,1)S(1)} collective-permute-done((bf16[72,896]{1,0:T(8,128)(2,1)S(1)}, bf16[72,896]{1,0:T(8,128)(2,1)S(1)}, u32[]{:S(2)}, u32[]{:S(2)}) %collective-permute-start.22) | collective-permute-done | bytes 129056 | tf_op jit(solution)/shard_map/ppermute | solution.py:239
  54.5 2.6 %collective-permute-done.20.crossed = bf16[72,896]{1,0:T(8,128)(2,1)S(1)} collective-permute-done((bf16[72,896]{1,0:T(8,128)(2,1)S(1)}, bf16[72,896]{1,0:T(8,128)(2,1)S(1)}, u32[]{:S(2)}, u32[]{:S(2)}) %collective-permute-start.20) | collective-permute-done | bytes 129056 | tf_op jit(solution)/shard_map/ppermute | solution.py:239
  57.1 1.4 %collective-permute-start.21 = (bf16[72,896]{1,0:T(8,128)(2,1)S(1)}, bf16[72,896]{1,0:T(8,128)(2,1)S(1)}, u32[]{:S(2)}, u32[]{:S(2)}) collective-permute-start(bf16[72,896]{1,0:T(8,128)(2,1)S(1)} %shard_map.122), channel_id=1, source_target_pairs={{0,8},{4,12},{8,0},{12,4},{1,9},{5,13},{9,1},{13,5},{2,10},{6,14},... | collective-permute-start | bytes 387080 | tf_op jit(solution)/shard_map/ppermute | solution.py:236
  58.5 1.3 %collective-permute-done.18.crossed = bf16[72,896]{1,0:T(8,128)(2,1)S(1)} collective-permute-done((bf16[72,896]{1,0:T(8,128)(2,1)S(1)}, bf16[72,896]{1,0:T(8,128)(2,1)S(1)}, u32[]{:S(2)}, u32[]{:S(2)}) %collective-permute-start.18) | collective-permute-done | bytes 129056 | tf_op jit(solution)/shard_map/ppermute | solution.py:239
  60.4 2.4 %shard_map.126 = bf16[1,608,3584]{2,1,0:T(8,128)(2,1)} custom-call(bf16[608,256]{1,0:T(8,128)(2,1)S(1)} %get-tuple-element.66.dup_ref.left_ref, bf16[256,3584]{1,0:T(8,128)(2,1)S(1)} %get-tuple-element.65.rows_ref), custom_call_target="tpu_custom_call" | custom-call | tf_op jit(solution)/shard_map/pallas_call | solution.py:197
  62.8 2.4 %shard_map.125 = bf16[1,608,3584]{2,1,0:T(8,128)(2,1)} custom-call(bf16[608,256]{1,0:T(8,128)(2,1)S(1)} %get-tuple-element.64.dgate_ref.left_ref, bf16[256,3584]{1,0:T(8,128)(2,1)S(1)} %get-tuple-element.65.rows_ref), custom_call_target="tpu_custom_call" | custom-call | tf_op jit(solution)/shard_map/pallas_call | solution.py:197
  65.3 2.4 %shard_map.127 = bf16[1,608,3584]{2,1,0:T(8,128)(2,1)} custom-call(bf16[608,256]{1,0:T(8,128)(2,1)S(1)} %get-tuple-element.67.left_ref, bf16[256,3584]{1,0:T(8,128)(2,1)S(1)} %get-tuple-element.68.rows_ref), custom_call_target="tpu_custom_call" | custom-call | tf_op jit(solution)/shard_map/pallas_call | solution.py:197
  (46 shorter events, 6.1 us)
Async XLA Ops:
  2.2 16.4 %collective-permute-start.3 = (bf16[128,896]{1,0:T(8,128)(2,1)S(1)}, bf16[128,896]{1,0:T(8,128)(2,1)S(1)}, u32[]{:S(2)}, u32[]{:S(2)}) collective-permute-start(bf16[128,896]{1,0:T(8,128)(2,1)S(1)} %get-tuple-element.40), channel_id=1, source_target_pairs={{0,8},{4,12},{8,0},{12,4},{1,9},{5,13},{9,1},{13,5},{2,10},{6,14},... | collective-permute-start | bytes 688136 | tf_op jit(solution)/shard_map/ppermute | solution.py:236
  6.3 18.2 %collective-permute-start = (bf16[128,896]{1,0:T(8,128)(2,1)S(1)}, bf16[128,896]{1,0:T(8,128)(2,1)S(1)}, u32[]{:S(2)}, u32[]{:S(2)}) collective-permute-start(bf16[128,896]{1,0:T(8,128)(2,1)S(1)} %get-tuple-element.37), channel_id=1, source_target_pairs={{0,4},{4,0},{8,12},{12,8},{1,5},{5,1},{9,13},{13,9},{2,6},{6,2},{1... | collective-permute-start | bytes 688136 | tf_op jit(solution)/shard_map/ppermute | solution.py:236
  7.9 17.1 %collective-permute-start.1 = (bf16[128,896]{1,0:T(8,128)(2,1)S(1)}, bf16[128,896]{1,0:T(8,128)(2,1)S(1)}, u32[]{:S(2)}, u32[]{:S(2)}) collective-permute-start(bf16[128,896]{1,0:T(8,128)(2,1)S(1)} %get-tuple-element.39.refs_0_.refs_8_), channel_id=1, source_target_pairs={{0,2},{1,3},{2,0},{3,1},{4,6},{5,7},{6,4},{7,5},{8,10},{9,11},{10,... | collective-permute-start | bytes 688136 | tf_op jit(solution)/shard_map/ppermute | solution.py:239
  9.4 15.7 %collective-permute-start.5 = (bf16[128,896]{1,0:T(8,128)(2,1)S(1)}, bf16[128,896]{1,0:T(8,128)(2,1)S(1)}, u32[]{:S(2)}, u32[]{:S(2)}) collective-permute-start(bf16[128,896]{1,0:T(8,128)(2,1)S(1)} %get-tuple-element.41), channel_id=1, source_target_pairs={{0,12},{4,8},{8,4},{12,0},{1,13},{5,9},{9,5},{13,1},{2,14},{6,10},... | collective-permute-start | bytes 688136 | tf_op jit(solution)/shard_map/ppermute | solution.py:236
  18.6 11.6 %collective-permute-start.4 = (bf16[128,896]{1,0:T(8,128)(2,1)S(1)}, bf16[128,896]{1,0:T(8,128)(2,1)S(1)}, u32[]{:S(2)}, u32[]{:S(2)}) collective-permute-start(bf16[128,896]{1,0:T(8,128)(2,1)S(1)} %collective-permute-done.3.refs_2_.refs_10_), channel_id=1, source_target_pairs={{0,2},{1,3},{2,0},{3,1},{4,6},{5,7},{6,4},{7,5},{8,10},{9,11},{10,... | collective-permute-start | bytes 688136 | tf_op jit(solution)/shard_map/ppermute | solution.py:239
  24.5 5.7 %collective-permute-start.10 = (bf16[128,896]{1,0:T(8,128)(2,1)S(1)}, bf16[128,896]{1,0:T(8,128)(2,1)S(1)}, u32[]{:S(2)}, u32[]{:S(2)}) collective-permute-start(bf16[128,896]{1,0:T(8,128)(2,1)S(1)} %get-tuple-element.39.refs_0_.refs_8_), channel_id=1, source_target_pairs={{0,1},{1,0},{2,3},{3,2},{4,5},{5,4},{6,7},{7,6},{8,9},{9,8},{10,11... | collective-permute-start | bytes 688136 | tf_op jit(solution)/shard_map/ppermute | solution.py:239
  24.5 13.1 %collective-permute-start.11 = (bf16[128,896]{1,0:T(8,128)(2,1)S(1)}, bf16[128,896]{1,0:T(8,128)(2,1)S(1)}, u32[]{:S(2)}, u32[]{:S(2)}) collective-permute-start(bf16[128,896]{1,0:T(8,128)(2,1)S(1)} %collective-permute-done.refs_1_.refs_9_), channel_id=1, source_target_pairs={{0,1},{1,0},{2,3},{3,2},{4,5},{5,4},{6,7},{7,6},{8,9},{9,8},{10,11... | collective-permute-start | bytes 688136 | tf_op jit(solution)/shard_map/ppermute | solution.py:239
  25.0 12.9 %collective-permute-start.12 = (bf16[128,896]{1,0:T(8,128)(2,1)S(1)}, bf16[128,896]{1,0:T(8,128)(2,1)S(1)}, u32[]{:S(2)}, u32[]{:S(2)}) collective-permute-start(bf16[128,896]{1,0:T(8,128)(2,1)S(1)} %collective-permute-done.3.refs_2_.refs_10_), channel_id=1, source_target_pairs={{0,1},{1,0},{2,3},{3,2},{4,5},{5,4},{6,7},{7,6},{8,9},{9,8},{10,11... | collective-permute-start | bytes 688136 | tf_op jit(solution)/shard_map/ppermute | solution.py:239
  25.1 13.1 %collective-permute-start.2 = (bf16[128,896]{1,0:T(8,128)(2,1)S(1)}, bf16[128,896]{1,0:T(8,128)(2,1)S(1)}, u32[]{:S(2)}, u32[]{:S(2)}) collective-permute-start(bf16[128,896]{1,0:T(8,128)(2,1)S(1)} %collective-permute-done.refs_1_.refs_9_), channel_id=1, source_target_pairs={{0,2},{1,3},{2,0},{3,1},{4,6},{5,7},{6,4},{7,5},{8,10},{9,11},{10,... | collective-permute-start | bytes 688136 | tf_op jit(solution)/shard_map/ppermute | solution.py:239
  30.2 8.1 %collective-permute-start.13 = (bf16[128,896]{1,0:T(8,128)(2,1)S(1)}, bf16[128,896]{1,0:T(8,128)(2,1)S(1)}, u32[]{:S(2)}, u32[]{:S(2)}) collective-permute-start(bf16[128,896]{1,0:T(8,128)(2,1)S(1)} %collective-permute-done.5.refs_3_.refs_11_), channel_id=1, source_target_pairs={{0,1},{1,0},{2,3},{3,2},{4,5},{5,4},{6,7},{7,6},{8,9},{9,8},{10,11... | collective-permute-start | bytes 688136 | tf_op jit(solution)/shard_map/ppermute | solution.py:239
  30.2 10.1 %collective-permute-start.6 = (bf16[128,896]{1,0:T(8,128)(2,1)S(1)}, bf16[128,896]{1,0:T(8,128)(2,1)S(1)}, u32[]{:S(2)}, u32[]{:S(2)}) collective-permute-start(bf16[128,896]{1,0:T(8,128)(2,1)S(1)} %collective-permute-done.5.refs_3_.refs_11_), channel_id=1, source_target_pairs={{0,2},{1,3},{2,0},{3,1},{4,6},{5,7},{6,4},{7,5},{8,10},{9,11},{10,... | collective-permute-start | bytes 688136 | tf_op jit(solution)/shard_map/ppermute | solution.py:239
  37.6 3.2 %collective-permute-start.7 = (bf16[128,896]{1,0:T(8,128)(2,1)S(1)}, bf16[128,896]{1,0:T(8,128)(2,1)S(1)}, u32[]{:S(2)}, u32[]{:S(2)}) collective-permute-start(bf16[128,896]{1,0:T(8,128)(2,1)S(1)} %collective-permute-done.1.refs_0_), channel_id=1, source_target_pairs={{0,1},{1,0},{2,3},{3,2},{4,5},{5,4},{6,7},{7,6},{8,9},{9,8},{10,11... | collective-permute-start | bytes 688136 | tf_op jit(solution)/shard_map/ppermute | solution.py:239
  37.9 2.9 %collective-permute-start.9 = (bf16[128,896]{1,0:T(8,128)(2,1)S(1)}, bf16[128,896]{1,0:T(8,128)(2,1)S(1)}, u32[]{:S(2)}, u32[]{:S(2)}) collective-permute-start(bf16[128,896]{1,0:T(8,128)(2,1)S(1)} %collective-permute-done.4.refs_2_), channel_id=1, source_target_pairs={{0,1},{1,0},{2,3},{3,2},{4,5},{5,4},{6,7},{7,6},{8,9},{9,8},{10,11... | collective-permute-start | bytes 688136 | tf_op jit(solution)/shard_map/ppermute | solution.py:239
  38.2 2.6 %collective-permute-start.8 = (bf16[128,896]{1,0:T(8,128)(2,1)S(1)}, bf16[128,896]{1,0:T(8,128)(2,1)S(1)}, u32[]{:S(2)}, u32[]{:S(2)}) collective-permute-start(bf16[128,896]{1,0:T(8,128)(2,1)S(1)} %collective-permute-done.2.refs_1_), channel_id=1, source_target_pairs={{0,1},{1,0},{2,3},{3,2},{4,5},{5,4},{6,7},{7,6},{8,9},{9,8},{10,11... | collective-permute-start | bytes 688136 | tf_op jit(solution)/shard_map/ppermute | solution.py:239
  40.4 1.6 %collective-permute-start.14 = (bf16[128,896]{1,0:T(8,128)(2,1)S(1)}, bf16[128,896]{1,0:T(8,128)(2,1)S(1)}, u32[]{:S(2)}, u32[]{:S(2)}) collective-permute-start(bf16[128,896]{1,0:T(8,128)(2,1)S(1)} %collective-permute-done.6.refs_3_), channel_id=1, source_target_pairs={{0,1},{1,0},{2,3},{3,2},{4,5},{5,4},{6,7},{7,6},{8,9},{9,8},{10,11... | collective-permute-start | bytes 688136 | tf_op jit(solution)/shard_map/ppermute | solution.py:239
  45.2 2.6 %collective-permute-start.16 = (bf16[264,896]{1,0:T(8,128)(2,1)S(1)}, bf16[264,896]{1,0:T(8,128)(2,1)S(1)}, u32[]{:S(2)}, u32[]{:S(2)}) collective-permute-start(bf16[264,896]{1,0:T(8,128)(2,1)S(1)} %shard_map.118), channel_id=1, source_target_pairs={{0,1},{1,0},{2,3},{3,2},{4,5},{5,4},{6,7},{7,6},{8,9},{9,8},{10,11... | collective-permute-start | bytes 1419272 | tf_op jit(solution)/shard_map/ppermute | solution.py:239
  46.5 6.6 %collective-permute-start.15 = (bf16[256,896]{1,0:T(8,128)(2,1)S(1)}, bf16[256,896]{1,0:T(8,128)(2,1)S(1)}, u32[]{:S(2)}, u32[]{:S(2)}) collective-permute-start(bf16[256,896]{1,0:T(8,128)(2,1)S(1)} %shard_map.116), channel_id=1, source_target_pairs={{0,1},{1,0},{2,3},{3,2},{4,5},{5,4},{6,7},{7,6},{8,9},{9,8},{10,11... | collective-permute-start | bytes 1376264 | tf_op jit(solution)/shard_map/ppermute | solution.py:239
  47.9 6.4 %collective-permute-start.22 = (bf16[72,896]{1,0:T(8,128)(2,1)S(1)}, bf16[72,896]{1,0:T(8,128)(2,1)S(1)}, u32[]{:S(2)}, u32[]{:S(2)}) collective-permute-start(bf16[72,896]{1,0:T(8,128)(2,1)S(1)} %get-tuple-element.60), channel_id=1, source_target_pairs={{0,2},{1,3},{2,0},{3,1},{4,6},{5,7},{6,4},{7,5},{8,10},{9,11},{10,... | collective-permute-start | bytes 387080 | tf_op jit(solution)/shard_map/ppermute | solution.py:239
  48.3 8.8 %collective-permute-start.20 = (bf16[72,896]{1,0:T(8,128)(2,1)S(1)}, bf16[72,896]{1,0:T(8,128)(2,1)S(1)}, u32[]{:S(2)}, u32[]{:S(2)}) collective-permute-start(bf16[72,896]{1,0:T(8,128)(2,1)S(1)} %get-tuple-element.59), channel_id=1, source_target_pairs={{0,2},{1,3},{2,0},{3,1},{4,6},{5,7},{6,4},{7,5},{8,10},{9,11},{10,... | collective-permute-start | bytes 387080 | tf_op jit(solution)/shard_map/ppermute | solution.py:239
  50.0 9.8 %collective-permute-start.18 = (bf16[72,896]{1,0:T(8,128)(2,1)S(1)}, bf16[72,896]{1,0:T(8,128)(2,1)S(1)}, u32[]{:S(2)}, u32[]{:S(2)}) collective-permute-start(bf16[72,896]{1,0:T(8,128)(2,1)S(1)} %get-tuple-element.58), channel_id=1, source_target_pairs={{0,2},{1,3},{2,0},{3,1},{4,6},{5,7},{6,4},{7,5},{8,10},{9,11},{10,... | collective-permute-start | bytes 387080 | tf_op jit(solution)/shard_map/ppermute | solution.py:239
  51.3 16.5 %collective-permute-start.17 = (bf16[72,896]{1,0:T(8,128)(2,1)S(1)}, bf16[72,896]{1,0:T(8,128)(2,1)S(1)}, u32[]{:S(2)}, u32[]{:S(2)}) collective-permute-start(bf16[72,896]{1,0:T(8,128)(2,1)S(1)} %get-tuple-element.56), channel_id=1, source_target_pairs={{0,2},{1,3},{2,0},{3,1},{4,6},{5,7},{6,4},{7,5},{8,10},{9,11},{10,... | collective-permute-start | bytes 387080 | tf_op jit(solution)/shard_map/ppermute | solution.py:239
  54.4 13.4 %collective-permute-start.23 = (bf16[72,896]{1,0:T(8,128)(2,1)S(1)}, bf16[72,896]{1,0:T(8,128)(2,1)S(1)}, u32[]{:S(2)}, u32[]{:S(2)}) collective-permute-start(bf16[72,896]{1,0:T(8,128)(2,1)S(1)} %shard_map.123), channel_id=1, source_target_pairs={{0,12},{4,8},{8,4},{12,0},{1,13},{5,9},{9,5},{13,1},{2,14},{6,10},... | collective-permute-start | bytes 387080 | tf_op jit(solution)/shard_map/ppermute | solution.py:236
  57.1 10.7 %collective-permute-start.21 = (bf16[72,896]{1,0:T(8,128)(2,1)S(1)}, bf16[72,896]{1,0:T(8,128)(2,1)S(1)}, u32[]{:S(2)}, u32[]{:S(2)}) collective-permute-start(bf16[72,896]{1,0:T(8,128)(2,1)S(1)} %shard_map.122), channel_id=1, source_target_pairs={{0,8},{4,12},{8,0},{12,4},{1,9},{5,13},{9,1},{13,5},{2,10},{6,14},... | collective-permute-start | bytes 387080 | tf_op jit(solution)/shard_map/ppermute | solution.py:236
  60.0 7.8 %collective-permute-start.19 = (bf16[72,896]{1,0:T(8,128)(2,1)S(1)}, bf16[72,896]{1,0:T(8,128)(2,1)S(1)}, u32[]{:S(2)}, u32[]{:S(2)}) collective-permute-start(bf16[72,896]{1,0:T(8,128)(2,1)S(1)} %shard_map.121), channel_id=1, source_target_pairs={{0,4},{4,0},{8,12},{12,8},{1,5},{5,1},{9,13},{13,9},{2,6},{6,2},{1... | collective-permute-start | bytes 387080 | tf_op jit(solution)/shard_map/ppermute | solution.py:236
  (2 other events, 11.3 us)

commit v4 on v3

--- a/solution.py
+++ b/solution.py
@@ -253,18 +253,18 @@
     partner, other = [None] * groups, [None] * groups
     other[0] = over_expert(own[0], 2)
     partner[0] = over_expert(own[0], 1)
+    own[3] = over_node(blocks[3], 3)
+    partner[3] = over_expert(own[3], 1)
+    own[2] = over_node(blocks[2], 2)
+    partner[2] = over_expert(own[2], 1)
     own[1] = over_node(blocks[1], 1)
     partner[1] = over_expert(own[1], 1)
-    own[2] = over_node(blocks[2], 2)
-    partner[2] = over_expert(own[2], 1)
-    own[3] = over_node(blocks[3], 3)
-    partner[3] = over_expert(own[3], 1)
-    mats = after((w_gate, w_up, w_down, other[0]))[:3]
+    mats = after((w_gate, w_up, w_down, partner[0]))[:3]
     mats = call(load_kernel, [shape(m.shape, BF16) for m in mats], *mats, nbytes=12 * units * features,
                 in_hbm=(0, 1, 2), scratch=[pltpu.SemaphoreType.DMA((3,))])
-    other[1] = over_expert(own[1], 2)
-    other[2] = over_expert(own[2], 2)
-    other[3] = over_expert(after((own[3], other[0], other[2]))[0], 2)
+    other[1] = over_expert(after((own[1], other[0], mats[0]))[0], 2)
+    other[2] = over_expert(after((own[2], mats[0]))[0], 2)
+    other[3] = over_expert(after((own[3], other[2]))[0], 2)
     across = [over_expert(x, 1) for x in other[:-1]]
 
     dense = 2 * rows * units * features
@@ -421,7 +421,7 @@
 
 
 def local(hidden_in, *rest):
-    if lax.axis_size("expert") == 4 and hidden_in.shape[1] % 128 == 0:
+    if (lax.axis_size("node"), lax.axis_size("expert")) == (4, 4) and hidden_in.shape[1] % 128 == 0:
         return fast_local(hidden_in, *rest)
     return general_local(hidden_in, *rest)
 

time: 68.9 us -> 65.3 us (0.948)
  waiting for transfers between devices: 20.4 us -> 16 us
    ppermute x6, starting transfers between devices: 7.39 us -> 12.8 us  [over_node(): return lax.ppermute(x, 'node', [(i, i ^ shift) for i in range(groups)])]
    ppermute x18, starting transfers between devices: 16.5 us -> 11.7 us  [over_expert(): lax.ppermute(x, 'expert', [(i, i ^ relative) for i in range(experts)])]
    ppermute x6, waiting for transfers between devices: 8.96 us -> 6.56 us  [over_node(): return lax.ppermute(x, 'node', [(i, i ^ shift) for i in range(groups)])]
    ppermute x18, waiting for transfers between devices: 11.4 us -> 9.47 us  [over_expert(): lax.ppermute(x, 'expert', [(i, i ^ relative) for i in range(experts)])]
  transfers between devices with their start and end apart: 24 -> 24, of which waited for: 6 -> 7; matrix products, arithmetic and copies ran while one was open for 0% -> 0% of each run, Pallas kernels for 26% -> 28%
where the time goes in v4:
time: 65.3 us; the launch traced here: 65.1 us
  starting transfers between devices  24.5 us (38%)
  Pallas kernels  23.7 us (36%)
  waiting for transfers between devices  16 us (25%)
  between operations  0.81 us (1%)
    pallas_call x15, Pallas kernels, call(): pl.pallas_call(kernel, out_shape=outs, in_specs=[pl.BlockSpec(memory_spac...  16.4 us
    ppermute x6, starting transfers between devices, over_node(): return lax.ppermute(x, 'node', [(i, i ^ shift) for i in range(groups)])  12.8 us
    ppermute x18, starting transfers between devices, over_expert(): lax.ppermute(x, 'expert', [(i, i ^ relative) for i in range(experts)])  11.7 us
    ppermute x18, waiting for transfers between devices, over_expert(): lax.ppermute(x, 'expert', [(i, i ^ relative) for i in range(experts)])  9.47 us
    pallas_call x3, Pallas kernels, weight_grad(): pl.pallas_call(functools.partial(grad_kernel, tile), out_shape=jax.ShapeD...  7.34 us
    ppermute x6, waiting for transfers between devices, over_node(): return lax.ppermute(x, 'node', [(i, i ^ shift) for i in range(groups)])  6.56 us
  transfers between devices with their start and end apart: 24, of which 7 were waited for; matrix products, arithmetic and copies ran while one was open for 0% of the time, Pallas kernels for 28%

profile of v4, /device:TPU:0, one launch (start us, length us, event | category | flops | bytes accessed | tf_op | source)
XLA Modules:
  0.0 65.1 jit_solution(10397398137247901933)
XLA Ops:
  0.6 1.6 %shard_map.110 = (bf16[128,896]{1,0:T(8,128)(2,1)S(1)}, bf16[128,896]{1,0:T(8,128)(2,1)S(1)}, bf16[128,896]{1,0:T(8,128)(2,1)S(1)}, bf16[128,896]{1,0:T(8,128)(2,1)S(1)}) custom-call(s32[2,128]{1,0:T(2,128)} %bitcast.3, bf16[2,128]{1,0:T(2,128)(2,1)} %bitcast.6, bf16[128,896]{1,0:T(8,128)(2,1)} %refs_2_.1, bf16[128,896]{1,0:T(8,128)(2,1)} %refs_3_.1), custom_call_target="tpu_custom_call" | custom-call | flops 117440512 | bytes 688128 | tf_op jit(solution)/shard_map/pallas_call | solution.py:31
  2.7 3.7 %collective-permute-start.4 = (bf16[128,896]{1,0:T(8,128)(2,1)S(1)}, bf16[128,896]{1,0:T(8,128)(2,1)S(1)}, u32[]{:S(2)}, u32[]{:S(2)}) collective-permute-start(bf16[128,896]{1,0:T(8,128)(2,1)S(1)} %get-tuple-element.47), channel_id=1, source_target_pairs={{0,8},{4,12},{8,0},{12,4},{1,9},{5,13},{9,1},{13,5},{2,10},{6,14},... | collective-permute-start | bytes 688136 | tf_op jit(solution)/shard_map/ppermute | solution.py:236
  6.4 1.6 %collective-permute-start = (bf16[128,896]{1,0:T(8,128)(2,1)S(1)}, bf16[128,896]{1,0:T(8,128)(2,1)S(1)}, u32[]{:S(2)}, u32[]{:S(2)}) collective-permute-start(bf16[128,896]{1,0:T(8,128)(2,1)S(1)} %get-tuple-element.39), channel_id=1, source_target_pairs={{0,4},{4,0},{8,12},{12,8},{1,5},{5,1},{9,13},{13,9},{2,6},{6,2},{1... | collective-permute-start | bytes 688136 | tf_op jit(solution)/shard_map/ppermute | solution.py:236
  8.0 1.5 %collective-permute-start.1 = (bf16[128,896]{1,0:T(8,128)(2,1)S(1)}, bf16[128,896]{1,0:T(8,128)(2,1)S(1)}, u32[]{:S(2)}, u32[]{:S(2)}) collective-permute-start(bf16[128,896]{1,0:T(8,128)(2,1)S(1)} %get-tuple-element.41.refs_0_.refs_8_), channel_id=1, source_target_pairs={{0,2},{1,3},{2,0},{3,1},{4,6},{5,7},{6,4},{7,5},{8,10},{9,11},{10,... | collective-permute-start | bytes 688136 | tf_op jit(solution)/shard_map/ppermute | solution.py:239
  9.7 4.8 %shard_map.112 = (bf16[1,608,3584]{2,1,0:T(8,128)(2,1)S(1)}, bf16[1,608,3584]{2,1,0:T(8,128)(2,1)S(1)}, bf16[1,608,3584]{2,1,0:T(8,128)(2,1)S(1)}) custom-call(bf16[1,608,3584]{2,1,0:T(8,128)(2,1)} %refs_0_, bf16[1,608,3584]{2,1,0:T(8,128)(2,1)} %refs_1_, bf16[1,608,3584]{2,1,0:T(8,128)(2,1)} %refs_2_.2), custom_call_target="tpu_custom_call" | custom-call | bytes 26148864 | tf_op jit(solution)/shard_map/pallas_call | solution.py:31
  14.6 3.3 %collective-permute-done.4.refs_2_.refs_10_ = bf16[128,896]{1,0:T(8,128)(2,1)S(1)} collective-permute-done((bf16[128,896]{1,0:T(8,128)(2,1)S(1)}, bf16[128,896]{1,0:T(8,128)(2,1)S(1)}, u32[]{:S(2)}, u32[]{:S(2)}) %collective-permute-start.4) | collective-permute-done | bytes 229408 | tf_op jit(solution)/shard_map/ppermute | solution.py:236
  17.8 1.8 %collective-permute-start.5 = (bf16[128,896]{1,0:T(8,128)(2,1)S(1)}, bf16[128,896]{1,0:T(8,128)(2,1)S(1)}, u32[]{:S(2)}, u32[]{:S(2)}) collective-permute-start(bf16[128,896]{1,0:T(8,128)(2,1)S(1)} %collective-permute-done.4.refs_2_.refs_10_), channel_id=1, source_target_pairs={{0,2},{1,3},{2,0},{3,1},{4,6},{5,7},{6,4},{7,5},{8,10},{9,11},{10,... | collective-permute-start | bytes 688136 | tf_op jit(solution)/shard_map/ppermute | solution.py:239
  20.4 3.3 %collective-permute-done.6.refs_3_.refs_11_ = bf16[128,896]{1,0:T(8,128)(2,1)S(1)} collective-permute-done((bf16[128,896]{1,0:T(8,128)(2,1)S(1)}, bf16[128,896]{1,0:T(8,128)(2,1)S(1)}, u32[]{:S(2)}, u32[]{:S(2)}) %collective-permute-start.6) | collective-permute-done | bytes 229408 | tf_op jit(solution)/shard_map/ppermute | solution.py:236
  23.7 2.7 %collective-permute-done.5.refs_2_ = bf16[128,896]{1,0:T(8,128)(2,1)S(1)} collective-permute-done((bf16[128,896]{1,0:T(8,128)(2,1)S(1)}, bf16[128,896]{1,0:T(8,128)(2,1)S(1)}, u32[]{:S(2)}, u32[]{:S(2)}) %collective-permute-start.5) | collective-permute-done | bytes 229408 | tf_op jit(solution)/shard_map/ppermute | solution.py:239
  26.3 1.8 %collective-permute-start.7 = (bf16[128,896]{1,0:T(8,128)(2,1)S(1)}, bf16[128,896]{1,0:T(8,128)(2,1)S(1)}, u32[]{:S(2)}, u32[]{:S(2)}) collective-permute-start(bf16[128,896]{1,0:T(8,128)(2,1)S(1)} %collective-permute-done.6.refs_3_.refs_11_), channel_id=1, source_target_pairs={{0,2},{1,3},{2,0},{3,1},{4,6},{5,7},{6,4},{7,5},{8,10},{9,11},{10,... | collective-permute-start | bytes 688136 | tf_op jit(solution)/shard_map/ppermute | solution.py:239
  28.7 2.6 %collective-permute-done.3.refs_1_ = bf16[128,896]{1,0:T(8,128)(2,1)S(1)} collective-permute-done((bf16[128,896]{1,0:T(8,128)(2,1)S(1)}, bf16[128,896]{1,0:T(8,128)(2,1)S(1)}, u32[]{:S(2)}, u32[]{:S(2)}) %collective-permute-start.3) | collective-permute-done | bytes 229408 | tf_op jit(solution)/shard_map/ppermute | solution.py:239
  31.3 2.0 %shard_map.113 = (f32[608,256]{1,0:T(8,128)S(1)}, f32[608,256]{1,0:T(8,128)S(1)}, f32[608,256]{1,0:T(8,128)S(1)}) custom-call(bf16[128,896]{1,0:T(8,128)(2,1)S(1)} %get-tuple-element.41.refs_0_.refs_8_, bf16[128,896]{1,0:T(8,128)(2,1)S(1)} %collective-permute-done.refs_1_.refs_9_, bf16[128,896]{1,0:T(8,128)(2,1)S(1)} %collective-permute-done.4.refs_2_.refs_10_, ...), custom_call_target="tpu_custom_call" | custom-call | flops 1673527296 | bytes 6537216 | tf_op jit(solution)/shard_map/pallas_call | solution.py:31
  33.2 1.5 %collective-permute-done.7.refs_3_ = bf16[128,896]{1,0:T(8,128)(2,1)S(1)} collective-permute-done((bf16[128,896]{1,0:T(8,128)(2,1)S(1)}, bf16[128,896]{1,0:T(8,128)(2,1)S(1)}, u32[]{:S(2)}, u32[]{:S(2)}) %collective-permute-start.7) | collective-permute-done | bytes 229408 | tf_op jit(solution)/shard_map/ppermute | solution.py:239
  34.8 1.5 %collective-permute-done.14.refs_7_ = bf16[128,896]{1,0:T(8,128)(2,1)S(1)} collective-permute-done((bf16[128,896]{1,0:T(8,128)(2,1)S(1)}, bf16[128,896]{1,0:T(8,128)(2,1)S(1)}, u32[]{:S(2)}, u32[]{:S(2)}) %collective-permute-start.14) | collective-permute-done | bytes 229408 | tf_op jit(solution)/shard_map/ppermute | solution.py:239
  36.2 2.3 %shard_map.114 = (bf16[256,3584]{1,0:T(8,128)(2,1)S(1)}, bf16[256,3584]{1,0:T(8,128)(2,1)S(1)}, bf16[608,256]{1,0:T(8,128)(2,1)S(1)}, bf16[608,256]{1,0:T(8,128)...) custom-call(bf16[128,896]{1,0:T(8,128)(2,1)S(1)} %collective-permute-done.1.refs_0_, ...), custom_call_target="tpu_custom_call" | custom-call | flops 1673527296 | bytes 6537216 | tf_op jit(solution)/shard_map/pallas_call | solution.py:31
  42.3 1.4 %collective-permute-start.22 = (bf16[72,896]{1,0:T(8,128)(2,1)S(1)}, bf16[72,896]{1,0:T(8,128)(2,1)S(1)}, u32[]{:S(2)}, u32[]{:S(2)}) collective-permute-start(bf16[72,896]{1,0:T(8,128)(2,1)S(1)} %get-tuple-element.64), channel_id=1, source_target_pairs={{0,2},{1,3},{2,0},{3,1},{4,6},{5,7},{6,4},{7,5},{8,10},{9,11},{10,... | collective-permute-start | bytes 387080 | tf_op jit(solution)/shard_map/ppermute | solution.py:239
  44.4 1.3 %collective-permute-start.18 = (bf16[72,896]{1,0:T(8,128)(2,1)S(1)}, bf16[72,896]{1,0:T(8,128)(2,1)S(1)}, u32[]{:S(2)}, u32[]{:S(2)}) collective-permute-start(bf16[72,896]{1,0:T(8,128)(2,1)S(1)} %get-tuple-element.62), channel_id=1, source_target_pairs={{0,2},{1,3},{2,0},{3,1},{4,6},{5,7},{6,4},{7,5},{8,10},{9,11},{10,... | collective-permute-start | bytes 387080 | tf_op jit(solution)/shard_map/ppermute | solution.py:239
  47.4 1.2 %collective-permute-done.22.crossed = bf16[72,896]{1,0:T(8,128)(2,1)S(1)} collective-permute-done((bf16[72,896]{1,0:T(8,128)(2,1)S(1)}, bf16[72,896]{1,0:T(8,128)(2,1)S(1)}, u32[]{:S(2)}, u32[]{:S(2)}) %collective-permute-start.22) | collective-permute-done | bytes 129056 | tf_op jit(solution)/shard_map/ppermute | solution.py:239
  48.8 4.1 %collective-permute-start.23 = (bf16[72,896]{1,0:T(8,128)(2,1)S(1)}, bf16[72,896]{1,0:T(8,128)(2,1)S(1)}, u32[]{:S(2)}, u32[]{:S(2)}) collective-permute-start(bf16[72,896]{1,0:T(8,128)(2,1)S(1)} %shard_map.123), channel_id=1, source_target_pairs={{0,12},{4,8},{8,4},{12,0},{1,13},{5,9},{9,5},{13,1},{2,14},{6,10},... | collective-permute-start | bytes 387080 | tf_op jit(solution)/shard_map/ppermute | solution.py:236
  52.9 1.8 %collective-permute-start.21 = (bf16[72,896]{1,0:T(8,128)(2,1)S(1)}, bf16[72,896]{1,0:T(8,128)(2,1)S(1)}, u32[]{:S(2)}, u32[]{:S(2)}) collective-permute-start(bf16[72,896]{1,0:T(8,128)(2,1)S(1)} %shard_map.122), channel_id=1, source_target_pairs={{0,8},{4,12},{8,0},{12,4},{1,9},{5,13},{9,1},{13,5},{2,10},{6,14},... | collective-permute-start | bytes 387080 | tf_op jit(solution)/shard_map/ppermute | solution.py:236
  54.9 1.4 %collective-permute-start.19 = (bf16[72,896]{1,0:T(8,128)(2,1)S(1)}, bf16[72,896]{1,0:T(8,128)(2,1)S(1)}, u32[]{:S(2)}, u32[]{:S(2)}) collective-permute-start(bf16[72,896]{1,0:T(8,128)(2,1)S(1)} %shard_map.121), channel_id=1, source_target_pairs={{0,4},{4,0},{8,12},{12,8},{1,5},{5,1},{9,13},{13,9},{2,6},{6,2},{1... | collective-permute-start | bytes 387080 | tf_op jit(solution)/shard_map/ppermute | solution.py:236
  56.7 2.4 %shard_map.126 = bf16[1,608,3584]{2,1,0:T(8,128)(2,1)} custom-call(bf16[608,256]{1,0:T(8,128)(2,1)S(1)} %get-tuple-element.70.dup_ref.left_ref, bf16[256,3584]{1,0:T(8,128)(2,1)S(1)} %get-tuple-element.69.rows_ref), custom_call_target="tpu_custom_call" | custom-call | tf_op jit(solution)/shard_map/pallas_call | solution.py:197
  59.1 2.4 %shard_map.125 = bf16[1,608,3584]{2,1,0:T(8,128)(2,1)} custom-call(bf16[608,256]{1,0:T(8,128)(2,1)S(1)} %get-tuple-element.68.dgate_ref.left_ref, bf16[256,3584]{1,0:T(8,128)(2,1)S(1)} %get-tuple-element.69.rows_ref), custom_call_target="tpu_custom_call" | custom-call | tf_op jit(solution)/shard_map/pallas_call | solution.py:197
  61.6 2.4 %shard_map.127 = bf16[1,608,3584]{2,1,0:T(8,128)(2,1)} custom-call(bf16[608,256]{1,0:T(8,128)(2,1)S(1)} %get-tuple-element.71.left_ref, bf16[256,3584]{1,0:T(8,128)(2,1)S(1)} %get-tuple-element.72.rows_ref), custom_call_target="tpu_custom_call" | custom-call | tf_op jit(solution)/shard_map/pallas_call | solution.py:197
  (46 shorter events, 9.9 us)
Async XLA Ops:
  2.2 7.5 %collective-permute-start.2 = (bf16[128,896]{1,0:T(8,128)(2,1)S(1)}, bf16[128,896]{1,0:T(8,128)(2,1)S(1)}, u32[]{:S(2)}, u32[]{:S(2)}) collective-permute-start(bf16[128,896]{1,0:T(8,128)(2,1)S(1)} %get-tuple-element.41.refs_0_.refs_8_), channel_id=1, source_target_pairs={{0,1},{1,0},{2,3},{3,2},{4,5},{5,4},{6,7},{7,6},{8,9},{9,8},{10,11... | collective-permute-start | bytes 688136 | tf_op jit(solution)/shard_map/ppermute | solution.py:239
  2.7 15.1 %collective-permute-start.4 = (bf16[128,896]{1,0:T(8,128)(2,1)S(1)}, bf16[128,896]{1,0:T(8,128)(2,1)S(1)}, u32[]{:S(2)}, u32[]{:S(2)}) collective-permute-start(bf16[128,896]{1,0:T(8,128)(2,1)S(1)} %get-tuple-element.47), channel_id=1, source_target_pairs={{0,8},{4,12},{8,0},{12,4},{1,9},{5,13},{9,1},{13,5},{2,10},{6,14},... | collective-permute-start | bytes 688136 | tf_op jit(solution)/shard_map/ppermute | solution.py:236
  6.4 13.2 %collective-permute-start = (bf16[128,896]{1,0:T(8,128)(2,1)S(1)}, bf16[128,896]{1,0:T(8,128)(2,1)S(1)}, u32[]{:S(2)}, u32[]{:S(2)}) collective-permute-start(bf16[128,896]{1,0:T(8,128)(2,1)S(1)} %get-tuple-element.39), channel_id=1, source_target_pairs={{0,4},{4,0},{8,12},{12,8},{1,5},{5,1},{9,13},{13,9},{2,6},{6,2},{1... | collective-permute-start | bytes 688136 | tf_op jit(solution)/shard_map/ppermute | solution.py:236
  8.0 11.6 %collective-permute-start.1 = (bf16[128,896]{1,0:T(8,128)(2,1)S(1)}, bf16[128,896]{1,0:T(8,128)(2,1)S(1)}, u32[]{:S(2)}, u32[]{:S(2)}) collective-permute-start(bf16[128,896]{1,0:T(8,128)(2,1)S(1)} %get-tuple-element.41.refs_0_.refs_8_), channel_id=1, source_target_pairs={{0,2},{1,3},{2,0},{3,1},{4,6},{5,7},{6,4},{7,5},{8,10},{9,11},{10,... | collective-permute-start | bytes 688136 | tf_op jit(solution)/shard_map/ppermute | solution.py:239
  9.5 14.2 %collective-permute-start.6 = (bf16[128,896]{1,0:T(8,128)(2,1)S(1)}, bf16[128,896]{1,0:T(8,128)(2,1)S(1)}, u32[]{:S(2)}, u32[]{:S(2)}) collective-permute-start(bf16[128,896]{1,0:T(8,128)(2,1)S(1)} %get-tuple-element.49), channel_id=1, source_target_pairs={{0,12},{4,8},{8,4},{12,0},{1,13},{5,9},{9,5},{13,1},{2,14},{6,10},... | collective-permute-start | bytes 688136 | tf_op jit(solution)/shard_map/ppermute | solution.py:236
  17.8 8.5 %collective-permute-start.5 = (bf16[128,896]{1,0:T(8,128)(2,1)S(1)}, bf16[128,896]{1,0:T(8,128)(2,1)S(1)}, u32[]{:S(2)}, u32[]{:S(2)}) collective-permute-start(bf16[128,896]{1,0:T(8,128)(2,1)S(1)} %collective-permute-done.4.refs_2_.refs_10_), channel_id=1, source_target_pairs={{0,2},{1,3},{2,0},{3,1},{4,6},{5,7},{6,4},{7,5},{8,10},{9,11},{10,... | collective-permute-start | bytes 688136 | tf_op jit(solution)/shard_map/ppermute | solution.py:239
  19.6 8.5 %collective-permute-start.11 = (bf16[128,896]{1,0:T(8,128)(2,1)S(1)}, bf16[128,896]{1,0:T(8,128)(2,1)S(1)}, u32[]{:S(2)}, u32[]{:S(2)}) collective-permute-start(bf16[128,896]{1,0:T(8,128)(2,1)S(1)} %collective-permute-done.refs_1_.refs_9_), channel_id=1, source_target_pairs={{0,1},{1,0},{2,3},{3,2},{4,5},{5,4},{6,7},{7,6},{8,9},{9,8},{10,11... | collective-permute-start | bytes 688136 | tf_op jit(solution)/shard_map/ppermute | solution.py:239
  19.6 8.5 %collective-permute-start.12 = (bf16[128,896]{1,0:T(8,128)(2,1)S(1)}, bf16[128,896]{1,0:T(8,128)(2,1)S(1)}, u32[]{:S(2)}, u32[]{:S(2)}) collective-permute-start(bf16[128,896]{1,0:T(8,128)(2,1)S(1)} %collective-permute-done.4.refs_2_.refs_10_), channel_id=1, source_target_pairs={{0,1},{1,0},{2,3},{3,2},{4,5},{5,4},{6,7},{7,6},{8,9},{9,8},{10,11... | collective-permute-start | bytes 688136 | tf_op jit(solution)/shard_map/ppermute | solution.py:239
  20.1 11.1 %collective-permute-start.3 = (bf16[128,896]{1,0:T(8,128)(2,1)S(1)}, bf16[128,896]{1,0:T(8,128)(2,1)S(1)}, u32[]{:S(2)}, u32[]{:S(2)}) collective-permute-start(bf16[128,896]{1,0:T(8,128)(2,1)S(1)} %collective-permute-done.refs_1_.refs_9_), channel_id=1, source_target_pairs={{0,2},{1,3},{2,0},{3,1},{4,6},{5,7},{6,4},{7,5},{8,10},{9,11},{10,... | collective-permute-start | bytes 688136 | tf_op jit(solution)/shard_map/ppermute | solution.py:239
  23.7 7.6 %collective-permute-start.13 = (bf16[128,896]{1,0:T(8,128)(2,1)S(1)}, bf16[128,896]{1,0:T(8,128)(2,1)S(1)}, u32[]{:S(2)}, u32[]{:S(2)}) collective-permute-start(bf16[128,896]{1,0:T(8,128)(2,1)S(1)} %collective-permute-done.6.refs_3_.refs_11_), channel_id=1, source_target_pairs={{0,1},{1,0},{2,3},{3,2},{4,5},{5,4},{6,7},{7,6},{8,9},{9,8},{10,11... | collective-permute-start | bytes 688136 | tf_op jit(solution)/shard_map/ppermute | solution.py:239
  26.3 8.4 %collective-permute-start.7 = (bf16[128,896]{1,0:T(8,128)(2,1)S(1)}, bf16[128,896]{1,0:T(8,128)(2,1)S(1)}, u32[]{:S(2)}, u32[]{:S(2)}) collective-permute-start(bf16[128,896]{1,0:T(8,128)(2,1)S(1)} %collective-permute-done.6.refs_3_.refs_11_), channel_id=1, source_target_pairs={{0,2},{1,3},{2,0},{3,1},{4,6},{5,7},{6,4},{7,5},{8,10},{9,11},{10,... | collective-permute-start | bytes 688136 | tf_op jit(solution)/shard_map/ppermute | solution.py:239
  28.1 6.6 %collective-permute-start.8 = (bf16[128,896]{1,0:T(8,128)(2,1)S(1)}, bf16[128,896]{1,0:T(8,128)(2,1)S(1)}, u32[]{:S(2)}, u32[]{:S(2)}) collective-permute-start(bf16[128,896]{1,0:T(8,128)(2,1)S(1)} %collective-permute-done.1.refs_0_), channel_id=1, source_target_pairs={{0,1},{1,0},{2,3},{3,2},{4,5},{5,4},{6,7},{7,6},{8,9},{9,8},{10,11... | collective-permute-start | bytes 688136 | tf_op jit(solution)/shard_map/ppermute | solution.py:239
  28.2 6.6 %collective-permute-start.10 = (bf16[128,896]{1,0:T(8,128)(2,1)S(1)}, bf16[128,896]{1,0:T(8,128)(2,1)S(1)}, u32[]{:S(2)}, u32[]{:S(2)}) collective-permute-start(bf16[128,896]{1,0:T(8,128)(2,1)S(1)} %collective-permute-done.5.refs_2_), channel_id=1, source_target_pairs={{0,1},{1,0},{2,3},{3,2},{4,5},{5,4},{6,7},{7,6},{8,9},{9,8},{10,11... | collective-permute-start | bytes 688136 | tf_op jit(solution)/shard_map/ppermute | solution.py:239
  31.3 3.5 %collective-permute-start.9 = (bf16[128,896]{1,0:T(8,128)(2,1)S(1)}, bf16[128,896]{1,0:T(8,128)(2,1)S(1)}, u32[]{:S(2)}, u32[]{:S(2)}) collective-permute-start(bf16[128,896]{1,0:T(8,128)(2,1)S(1)} %collective-permute-done.3.refs_1_), channel_id=1, source_target_pairs={{0,1},{1,0},{2,3},{3,2},{4,5},{5,4},{6,7},{7,6},{8,9},{9,8},{10,11... | collective-permute-start | bytes 688136 | tf_op jit(solution)/shard_map/ppermute | solution.py:239
  34.8 1.5 %collective-permute-start.14 = (bf16[128,896]{1,0:T(8,128)(2,1)S(1)}, bf16[128,896]{1,0:T(8,128)(2,1)S(1)}, u32[]{:S(2)}, u32[]{:S(2)}) collective-permute-start(bf16[128,896]{1,0:T(8,128)(2,1)S(1)} %collective-permute-done.7.refs_3_), channel_id=1, source_target_pairs={{0,1},{1,0},{2,3},{3,2},{4,5},{5,4},{6,7},{7,6},{8,9},{9,8},{10,11... | collective-permute-start | bytes 688136 | tf_op jit(solution)/shard_map/ppermute | solution.py:239
  39.5 2.6 %collective-permute-start.16 = (bf16[264,896]{1,0:T(8,128)(2,1)S(1)}, bf16[264,896]{1,0:T(8,128)(2,1)S(1)}, u32[]{:S(2)}, u32[]{:S(2)}) collective-permute-start(bf16[264,896]{1,0:T(8,128)(2,1)S(1)} %shard_map.118), channel_id=1, source_target_pairs={{0,1},{1,0},{2,3},{3,2},{4,5},{5,4},{6,7},{7,6},{8,9},{9,8},{10,11... | collective-permute-start | bytes 1419272 | tf_op jit(solution)/shard_map/ppermute | solution.py:239
  40.7 6.7 %collective-permute-start.15 = (bf16[256,896]{1,0:T(8,128)(2,1)S(1)}, bf16[256,896]{1,0:T(8,128)(2,1)S(1)}, u32[]{:S(2)}, u32[]{:S(2)}) collective-permute-start(bf16[256,896]{1,0:T(8,128)(2,1)S(1)} %shard_map.116), channel_id=1, source_target_pairs={{0,1},{1,0},{2,3},{3,2},{4,5},{5,4},{6,7},{7,6},{8,9},{9,8},{10,11... | collective-permute-start | bytes 1376264 | tf_op jit(solution)/shard_map/ppermute | solution.py:239
  42.3 6.4 %collective-permute-start.22 = (bf16[72,896]{1,0:T(8,128)(2,1)S(1)}, bf16[72,896]{1,0:T(8,128)(2,1)S(1)}, u32[]{:S(2)}, u32[]{:S(2)}) collective-permute-start(bf16[72,896]{1,0:T(8,128)(2,1)S(1)} %get-tuple-element.64), channel_id=1, source_target_pairs={{0,2},{1,3},{2,0},{3,1},{4,6},{5,7},{6,4},{7,5},{8,10},{9,11},{10,... | collective-permute-start | bytes 387080 | tf_op jit(solution)/shard_map/ppermute | solution.py:239
  43.7 9.2 %collective-permute-start.20 = (bf16[72,896]{1,0:T(8,128)(2,1)S(1)}, bf16[72,896]{1,0:T(8,128)(2,1)S(1)}, u32[]{:S(2)}, u32[]{:S(2)}) collective-permute-start(bf16[72,896]{1,0:T(8,128)(2,1)S(1)} %get-tuple-element.63), channel_id=1, source_target_pairs={{0,2},{1,3},{2,0},{3,1},{4,6},{5,7},{6,4},{7,5},{8,10},{9,11},{10,... | collective-permute-start | bytes 387080 | tf_op jit(solution)/shard_map/ppermute | solution.py:239
  44.4 10.4 %collective-permute-start.18 = (bf16[72,896]{1,0:T(8,128)(2,1)S(1)}, bf16[72,896]{1,0:T(8,128)(2,1)S(1)}, u32[]{:S(2)}, u32[]{:S(2)}) collective-permute-start(bf16[72,896]{1,0:T(8,128)(2,1)S(1)} %get-tuple-element.62), channel_id=1, source_target_pairs={{0,2},{1,3},{2,0},{3,1},{4,6},{5,7},{6,4},{7,5},{8,10},{9,11},{10,... | collective-permute-start | bytes 387080 | tf_op jit(solution)/shard_map/ppermute | solution.py:239
  46.7 17.4 %collective-permute-start.17 = (bf16[72,896]{1,0:T(8,128)(2,1)S(1)}, bf16[72,896]{1,0:T(8,128)(2,1)S(1)}, u32[]{:S(2)}, u32[]{:S(2)}) collective-permute-start(bf16[72,896]{1,0:T(8,128)(2,1)S(1)} %get-tuple-element.60), channel_id=1, source_target_pairs={{0,2},{1,3},{2,0},{3,1},{4,6},{5,7},{6,4},{7,5},{8,10},{9,11},{10,... | collective-permute-start | bytes 387080 | tf_op jit(solution)/shard_map/ppermute | solution.py:239
  48.8 15.3 %collective-permute-start.23 = (bf16[72,896]{1,0:T(8,128)(2,1)S(1)}, bf16[72,896]{1,0:T(8,128)(2,1)S(1)}, u32[]{:S(2)}, u32[]{:S(2)}) collective-permute-start(bf16[72,896]{1,0:T(8,128)(2,1)S(1)} %shard_map.123), channel_id=1, source_target_pairs={{0,12},{4,8},{8,4},{12,0},{1,13},{5,9},{9,5},{13,1},{2,14},{6,10},... | collective-permute-start | bytes 387080 | tf_op jit(solution)/shard_map/ppermute | solution.py:236
  52.9 11.2 %collective-permute-start.21 = (bf16[72,896]{1,0:T(8,128)(2,1)S(1)}, bf16[72,896]{1,0:T(8,128)(2,1)S(1)}, u32[]{:S(2)}, u32[]{:S(2)}) collective-permute-start(bf16[72,896]{1,0:T(8,128)(2,1)S(1)} %shard_map.122), channel_id=1, source_target_pairs={{0,8},{4,12},{8,0},{12,4},{1,9},{5,13},{9,1},{13,5},{2,10},{6,14},... | collective-permute-start | bytes 387080 | tf_op jit(solution)/shard_map/ppermute | solution.py:236
  54.9 9.2 %collective-permute-start.19 = (bf16[72,896]{1,0:T(8,128)(2,1)S(1)}, bf16[72,896]{1,0:T(8,128)(2,1)S(1)}, u32[]{:S(2)}, u32[]{:S(2)}) collective-permute-start(bf16[72,896]{1,0:T(8,128)(2,1)S(1)} %shard_map.121), channel_id=1, source_target_pairs={{0,4},{4,0},{8,12},{12,8},{1,5},{5,1},{9,13},{13,9},{2,6},{6,2},{1... | collective-permute-start | bytes 387080 | tf_op jit(solution)/shard_map/ppermute | solution.py:236
  (2 other events, 12.2 us)

commit v5 on v4

--- a/solution.py
+++ b/solution.py
@@ -172,7 +172,8 @@
         outs[shift][capacity:, capacity:] = jnp.zeros((EXTRA, outs[shift].shape[1] - capacity), BF16)
 
 
-def join_kernel(shift, keep, got, crossed, stat_ref, out):
+def join_kernel(shift, keep, got, crossed, stat_ref, *rest):
+    out = rest[-1]
     capacity = out.shape[0] - EXTRA
     block = slice(shift * capacity, (shift + 1) * capacity)
     out[:capacity] = (keep[block] + got[block].astype(F32) + crossed[:capacity].astype(F32)).astype(BF16)
@@ -180,13 +181,14 @@
     out[capacity:, capacity:] = jnp.zeros((EXTRA, out.shape[1] - capacity), BF16)
 
 
-def grad_kernel(tile, left_ref, rows_ref, out_ref, held_ref, sems):
+def grad_kernel(tile, left_ref, rows_ref, out_ref, mark_ref, held_ref, sems):
     copies = []
     for index in range(rows_ref.shape[1] // tile):
         columns = slice(index * tile, (index + 1) * tile)
         held_ref[:, columns] = dot_nn(left_ref[...], rows_ref[:, columns]).astype(BF16)
         copies.append(pltpu.make_async_copy(held_ref.at[:, columns], out_ref.at[0, :, columns], sems.at[index]))
         copies[-1].start()
+    mark_ref[...] = jnp.zeros(mark_ref.shape, F32)
     for copy in copies:
         copy.wait()
 
@@ -196,9 +198,9 @@
     tile = 512 if features % 512 == 0 else features
     return pl.pallas_call(
         functools.partial(grad_kernel, tile),
-        out_shape=jax.ShapeDtypeStruct((1, units, features), BF16),
+        out_shape=[jax.ShapeDtypeStruct((1, units, features), BF16), jax.ShapeDtypeStruct((8, 128), F32)],
         in_specs=[pl.BlockSpec(memory_space=pltpu.VMEM)] * 2,
-        out_specs=pl.BlockSpec(memory_space=pltpu.HBM),
+        out_specs=[pl.BlockSpec(memory_space=pltpu.HBM), pl.BlockSpec(memory_space=pltpu.VMEM)],
         scratch_shapes=[pltpu.VMEM((units, features), BF16), pltpu.SemaphoreType.DMA((features // tile,))],
         compiler_params=pltpu.CompilerParams(vmem_limit_bytes=10 * MIB),
         cost_estimate=pl.CostEstimate(flops=0, bytes_accessed=0, transcendentals=0),
@@ -289,22 +291,33 @@
         )[0]
 
     far_got = over_expert(input_part(3, EXTRA, BF16), 1)
-    near_got = over_expert(input_part(1, 0, BF16), 1)
     far_keep = input_part(2, 0, F32)
     *far_sum, stat_pair = call(
         functools.partial(add_kernel, groups),
         [shape((capacity + EXTRA, width), BF16)] * groups + [shape((8, rows), F32)],
         far_keep, far_got, stat, nbytes=6 * rows * width,
     )
+    near_got = over_expert(input_part(1, 0, BF16), 1)
     near_keep = input_part(0, 0, F32)
-    back, totals = [None] * groups, []
-    for s in reversed(range(groups)):
-        totals += call(functools.partial(join_kernel, s), [shape((capacity + EXTRA, width), BF16)],
-                       near_keep, near_got, over_expert(far_sum[s], 2), stat_pair)
-        back[s] = over_node(totals[-1], s) if s else totals[-1]
-
-    dgate, dup, hid, _ = after((dgate, dup, hid, tuple(totals[:-1])))
-    weight_grads = [weight_grad(dgate, rows_in), weight_grad(dup, rows_in), weight_grad(hid, rows_grad)]
+    crossed = [over_expert(x, 2) for x in far_sum]
+    lefts = [(dgate, rows_in), (dup, rows_in), (hid, rows_grad)]
+    back, totals, marks = [None] * groups, [None] * groups, [None] * groups
+    weight_grads = [None] * 3
+    totals[3] = call(functools.partial(join_kernel, 3), [shape((capacity + EXTRA, width), BF16)],
+                     near_keep, near_got, crossed[3], stat_pair)[0]
+    back[3] = over_node(totals[3], 3)
+    weight_grads[0], marks[0] = weight_grad(after((dgate, far_sum[0]))[0], rows_in)
+    totals[2] = call(functools.partial(join_kernel, 2), [shape((capacity + EXTRA, width), BF16)],
+                     near_keep, near_got, crossed[2], stat_pair, marks[0])[0]
+    back[2] = over_node(totals[2], 2)
+    totals[1] = call(functools.partial(join_kernel, 1), [shape((capacity + EXTRA, width), BF16)],
+                     near_keep, near_got, crossed[1], stat_pair, marks[0])[0]
+    back[1] = over_node(totals[1], 1)
+    weight_grads[1], marks[1] = weight_grad(after((dup, totals[1], totals[2], totals[3]))[0], rows_in)
+    totals[0] = call(functools.partial(join_kernel, 0), [shape((capacity + EXTRA, width), BF16)],
+                     near_keep, near_got, crossed[0], stat_pair, marks[1])[0]
+    back[0] = totals[0]
+    weight_grads[2], marks[2] = weight_grad(after((hid, back[3]))[0], rows_grad)
 
     pick = call(functools.partial(pick_kernel, groups), [shape((tokens, rows), BF16)], after((ids, own[1]))[0])[0]
     grad_in, grad_gates = call(

time: 65.3 us -> 63.6 us (0.974)
  starting transfers between devices: 24.5 us -> 22 us
    ppermute x6, starting transfers between devices: 12.8 us -> 10.3 us  [over_node(): return lax.ppermute(x, 'node', [(i, i ^ shift) for i in range(groups)])]
  transfers between devices with their start and end apart: 24 -> 24, of which waited for: 7 -> 8; matrix products, arithmetic and copies ran while one was open for 0% -> 0% of each run, Pallas kernels for 28% -> 29%
where the time goes in v5:
time: 63.6 us; the launch traced here: 63.5 us
  Pallas kernels  24.3 us (38%)
  starting transfers between devices  22 us (35%)
  waiting for transfers between devices  16.3 us (26%)
  between operations  0.82 us (1%)
    pallas_call x15, Pallas kernels, call(): pl.pallas_call(kernel, out_shape=outs, in_specs=[pl.BlockSpec(memory_spac...  16.4 us
    ppermute x18, starting transfers between devices, over_expert(): lax.ppermute(x, 'expert', [(i, i ^ relative) for i in range(experts)])  11.7 us
    ppermute x6, starting transfers between devices, over_node(): return lax.ppermute(x, 'node', [(i, i ^ shift) for i in range(groups)])  10.3 us
    ppermute x18, waiting for transfers between devices, over_expert(): lax.ppermute(x, 'expert', [(i, i ^ relative) for i in range(experts)])  9.47 us
    pallas_call x3, Pallas kernels, weight_grad(): pl.pallas_call(functools.partial(grad_kernel, tile), out_shape=[jax.Shape...  7.93 us
    ppermute x6, waiting for transfers between devices, over_node(): return lax.ppermute(x, 'node', [(i, i ^ shift) for i in range(groups)])  6.85 us
  transfers between devices with their start and end apart: 24, of which 8 were waited for; matrix products, arithmetic and copies ran while one was open for 0% of the time, Pallas kernels for 29%

profile of v5, /device:TPU:0, one launch (start us, length us, event | category | flops | bytes accessed | tf_op | source)
XLA Modules:
  0.0 63.5 jit_solution(3851417654588689039)
XLA Ops:
  0.6 1.6 %shard_map.110 = (bf16[128,896]{1,0:T(8,128)(2,1)S(1)}, bf16[128,896]{1,0:T(8,128)(2,1)S(1)}, bf16[128,896]{1,0:T(8,128)(2,1)S(1)}, bf16[128,896]{1,0:T(8,128)(2,1)S(1)}) custom-call(s32[2,128]{1,0:T(2,128)} %bitcast.3, bf16[2,128]{1,0:T(2,128)(2,1)} %bitcast.6, bf16[128,896]{1,0:T(8,128)(2,1)} %refs_2_.1, bf16[128,896]{1,0:T(8,128)(2,1)} %refs_3_.1), custom_call_target="tpu_custom_call" | custom-call | flops 117440512 | bytes 688128 | tf_op jit(solution)/shard_map/pallas_call | solution.py:31
  2.7 3.7 %collective-permute-start.4 = (bf16[128,896]{1,0:T(8,128)(2,1)S(1)}, bf16[128,896]{1,0:T(8,128)(2,1)S(1)}, u32[]{:S(2)}, u32[]{:S(2)}) collective-permute-start(bf16[128,896]{1,0:T(8,128)(2,1)S(1)} %get-tuple-element.52), channel_id=1, source_target_pairs={{0,8},{4,12},{8,0},{12,4},{1,9},{5,13},{9,1},{13,5},{2,10},{6,14},... | collective-permute-start | bytes 688136 | tf_op jit(solution)/shard_map/ppermute | solution.py:238
  6.4 1.6 %collective-permute-start = (bf16[128,896]{1,0:T(8,128)(2,1)S(1)}, bf16[128,896]{1,0:T(8,128)(2,1)S(1)}, u32[]{:S(2)}, u32[]{:S(2)}) collective-permute-start(bf16[128,896]{1,0:T(8,128)(2,1)S(1)} %get-tuple-element.44), channel_id=1, source_target_pairs={{0,4},{4,0},{8,12},{12,8},{1,5},{5,1},{9,13},{13,9},{2,6},{6,2},{1... | collective-permute-start | bytes 688136 | tf_op jit(solution)/shard_map/ppermute | solution.py:238
  8.0 1.5 %collective-permute-start.1 = (bf16[128,896]{1,0:T(8,128)(2,1)S(1)}, bf16[128,896]{1,0:T(8,128)(2,1)S(1)}, u32[]{:S(2)}, u32[]{:S(2)}) collective-permute-start(bf16[128,896]{1,0:T(8,128)(2,1)S(1)} %get-tuple-element.46.refs_0_.refs_8_), channel_id=1, source_target_pairs={{0,2},{1,3},{2,0},{3,1},{4,6},{5,7},{6,4},{7,5},{8,10},{9,11},{10,... | collective-permute-start | bytes 688136 | tf_op jit(solution)/shard_map/ppermute | solution.py:241
  9.7 4.8 %shard_map.112 = (bf16[1,608,3584]{2,1,0:T(8,128)(2,1)S(1)}, bf16[1,608,3584]{2,1,0:T(8,128)(2,1)S(1)}, bf16[1,608,3584]{2,1,0:T(8,128)(2,1)S(1)}) custom-call(bf16[1,608,3584]{2,1,0:T(8,128)(2,1)} %refs_0_, bf16[1,608,3584]{2,1,0:T(8,128)(2,1)} %refs_1_, bf16[1,608,3584]{2,1,0:T(8,128)(2,1)} %refs_2_.2), custom_call_target="tpu_custom_call" | custom-call | bytes 26148864 | tf_op jit(solution)/shard_map/pallas_call | solution.py:31
  14.6 3.3 %collective-permute-done.4.refs_2_.refs_10_ = bf16[128,896]{1,0:T(8,128)(2,1)S(1)} collective-permute-done((bf16[128,896]{1,0:T(8,128)(2,1)S(1)}, bf16[128,896]{1,0:T(8,128)(2,1)S(1)}, u32[]{:S(2)}, u32[]{:S(2)}) %collective-permute-start.4) | collective-permute-done | bytes 229408 | tf_op jit(solution)/shard_map/ppermute | solution.py:238
  17.8 1.8 %collective-permute-start.5 = (bf16[128,896]{1,0:T(8,128)(2,1)S(1)}, bf16[128,896]{1,0:T(8,128)(2,1)S(1)}, u32[]{:S(2)}, u32[]{:S(2)}) collective-permute-start(bf16[128,896]{1,0:T(8,128)(2,1)S(1)} %collective-permute-done.4.refs_2_.refs_10_), channel_id=1, source_target_pairs={{0,2},{1,3},{2,0},{3,1},{4,6},{5,7},{6,4},{7,5},{8,10},{9,11},{10,... | collective-permute-start | bytes 688136 | tf_op jit(solution)/shard_map/ppermute | solution.py:241
  20.4 3.3 %collective-permute-done.6.refs_3_.refs_11_ = bf16[128,896]{1,0:T(8,128)(2,1)S(1)} collective-permute-done((bf16[128,896]{1,0:T(8,128)(2,1)S(1)}, bf16[128,896]{1,0:T(8,128)(2,1)S(1)}, u32[]{:S(2)}, u32[]{:S(2)}) %collective-permute-start.6) | collective-permute-done | bytes 229408 | tf_op jit(solution)/shard_map/ppermute | solution.py:238
  23.7 2.7 %collective-permute-done.5.refs_2_ = bf16[128,896]{1,0:T(8,128)(2,1)S(1)} collective-permute-done((bf16[128,896]{1,0:T(8,128)(2,1)S(1)}, bf16[128,896]{1,0:T(8,128)(2,1)S(1)}, u32[]{:S(2)}, u32[]{:S(2)}) %collective-permute-start.5) | collective-permute-done | bytes 229408 | tf_op jit(solution)/shard_map/ppermute | solution.py:241
  26.3 1.8 %collective-permute-start.7 = (bf16[128,896]{1,0:T(8,128)(2,1)S(1)}, bf16[128,896]{1,0:T(8,128)(2,1)S(1)}, u32[]{:S(2)}, u32[]{:S(2)}) collective-permute-start(bf16[128,896]{1,0:T(8,128)(2,1)S(1)} %collective-permute-done.6.refs_3_.refs_11_), channel_id=1, source_target_pairs={{0,2},{1,3},{2,0},{3,1},{4,6},{5,7},{6,4},{7,5},{8,10},{9,11},{10,... | collective-permute-start | bytes 688136 | tf_op jit(solution)/shard_map/ppermute | solution.py:241
  28.7 2.6 %collective-permute-done.3.refs_1_ = bf16[128,896]{1,0:T(8,128)(2,1)S(1)} collective-permute-done((bf16[128,896]{1,0:T(8,128)(2,1)S(1)}, bf16[128,896]{1,0:T(8,128)(2,1)S(1)}, u32[]{:S(2)}, u32[]{:S(2)}) %collective-permute-start.3) | collective-permute-done | bytes 229408 | tf_op jit(solution)/shard_map/ppermute | solution.py:241
  31.3 2.0 %shard_map.113 = (f32[608,256]{1,0:T(8,128)S(1)}, f32[608,256]{1,0:T(8,128)S(1)}, f32[608,256]{1,0:T(8,128)S(1)}) custom-call(bf16[128,896]{1,0:T(8,128)(2,1)S(1)} %get-tuple-element.46.refs_0_.refs_8_, bf16[128,896]{1,0:T(8,128)(2,1)S(1)} %collective-permute-done.refs_1_.refs_9_, bf16[128,896]{1,0:T(8,128)(2,1)S(1)} %collective-permute-done.4.refs_2_.refs_10_, ...), custom_call_target="tpu_custom_call" | custom-call | flops 1673527296 | bytes 6537216 | tf_op jit(solution)/shard_map/pallas_call | solution.py:31
  33.2 1.5 %collective-permute-done.7.refs_3_ = bf16[128,896]{1,0:T(8,128)(2,1)S(1)} collective-permute-done((bf16[128,896]{1,0:T(8,128)(2,1)S(1)}, bf16[128,896]{1,0:T(8,128)(2,1)S(1)}, u32[]{:S(2)}, u32[]{:S(2)}) %collective-permute-start.7) | collective-permute-done | bytes 229408 | tf_op jit(solution)/shard_map/ppermute | solution.py:241
  34.8 1.5 %collective-permute-done.14.refs_7_ = bf16[128,896]{1,0:T(8,128)(2,1)S(1)} collective-permute-done((bf16[128,896]{1,0:T(8,128)(2,1)S(1)}, bf16[128,896]{1,0:T(8,128)(2,1)S(1)}, u32[]{:S(2)}, u32[]{:S(2)}) %collective-permute-start.14) | collective-permute-done | bytes 229408 | tf_op jit(solution)/shard_map/ppermute | solution.py:241
  36.2 2.3 %shard_map.114 = (bf16[256,3584]{1,0:T(8,128)(2,1)S(1)}, bf16[256,3584]{1,0:T(8,128)(2,1)S(1)}, bf16[608,256]{1,0:T(8,128)(2,1)S(1)}, bf16[608,256]{1,0:T(8,128)...) custom-call(bf16[128,896]{1,0:T(8,128)(2,1)S(1)} %collective-permute-done.1.refs_0_, ...), custom_call_target="tpu_custom_call" | custom-call | flops 1673527296 | bytes 6537216 | tf_op jit(solution)/shard_map/pallas_call | solution.py:31
  38.5 1.0 %shard_map.118 = bf16[264,896]{1,0:T(8,128)(2,1)S(1)} custom-call(bf16[608,256]{1,0:T(8,128)(2,1)S(1)} %get-tuple-element.68.dgate_ref.left_ref, bf16[608,256]{1,0:T(8,128)(2,1)S(1)} %get-tuple-element.73.dup_ref.left_ref, bf16[1,608,3584]{2,1,0:T(8,128)(2,1)S(1)} %get-tuple-element.50.refs_8_.refs_16_.gate_w, ...), custom_call_target="tpu_custom_call" | custom-call | flops 557842432 | bytes 2179072 | tf_op jit(solution)/shard_map/pallas_call | solution.py:31
  39.7 1.0 %shard_map.116 = bf16[256,896]{1,0:T(8,128)(2,1)S(1)} custom-call(bf16[608,256]{1,0:T(8,128)(2,1)S(1)} %get-tuple-element.68.dgate_ref.left_ref, bf16[608,256]{1,0:T(8,128)(2,1)S(1)} %get-tuple-element.73.dup_ref.left_ref, bf16[1,608,3584]{2,1,0:T(8,128)(2,1)S(1)} %get-tuple-element.50.refs_8_.refs_16_.gate_w, ...), custom_call_target="tpu_custom_call" | custom-call | flops 557842432 | bytes 2179072 | tf_op jit(solution)/shard_map/pallas_call | solution.py:31
  42.3 1.4 %collective-permute-start.20 = (bf16[72,896]{1,0:T(8,128)(2,1)S(1)}, bf16[72,896]{1,0:T(8,128)(2,1)S(1)}, u32[]{:S(2)}, u32[]{:S(2)}) collective-permute-start(bf16[72,896]{1,0:T(8,128)(2,1)S(1)} %get-tuple-element.72), channel_id=1, source_target_pairs={{0,2},{1,3},{2,0},{3,1},{4,6},{5,7},{6,4},{7,5},{8,10},{9,11},{10,... | collective-permute-start | bytes 387080 | tf_op jit(solution)/shard_map/ppermute | solution.py:241
  44.4 1.3 %collective-permute-start.18 = (bf16[72,896]{1,0:T(8,128)(2,1)S(1)}, bf16[72,896]{1,0:T(8,128)(2,1)S(1)}, u32[]{:S(2)}, u32[]{:S(2)}) collective-permute-start(bf16[72,896]{1,0:T(8,128)(2,1)S(1)} %get-tuple-element.67), channel_id=1, source_target_pairs={{0,2},{1,3},{2,0},{3,1},{4,6},{5,7},{6,4},{7,5},{8,10},{9,11},{10,... | collective-permute-start | bytes 387080 | tf_op jit(solution)/shard_map/ppermute | solution.py:241
  47.4 1.2 %collective-permute-done.20.crossed = bf16[72,896]{1,0:T(8,128)(2,1)S(1)} collective-permute-done((bf16[72,896]{1,0:T(8,128)(2,1)S(1)}, bf16[72,896]{1,0:T(8,128)(2,1)S(1)}, u32[]{:S(2)}, u32[]{:S(2)}) %collective-permute-start.20) | collective-permute-done | bytes 129056 | tf_op jit(solution)/shard_map/ppermute | solution.py:241
  48.8 4.1 %collective-permute-start.23 = (bf16[72,896]{1,0:T(8,128)(2,1)S(1)}, bf16[72,896]{1,0:T(8,128)(2,1)S(1)}, u32[]{:S(2)}, u32[]{:S(2)}) collective-permute-start(bf16[72,896]{1,0:T(8,128)(2,1)S(1)} %shard_map.123), channel_id=1, source_target_pairs={{0,12},{4,8},{8,4},{12,0},{1,13},{5,9},{9,5},{13,1},{2,14},{6,10},... | collective-permute-start | bytes 387080 | tf_op jit(solution)/shard_map/ppermute | solution.py:238
  52.9 2.4 %shard_map.120 = (bf16[1,608,3584]{2,1,0:T(8,128)(2,1)}, f32[8,128]{1,0:T(8,128)S(1)}) custom-call(bf16[608,256]{1,0:T(8,128)(2,1)S(1)} %get-tuple-element.68.dgate_ref.left_ref, bf16[256,3584]{1,0:T(8,128)(2,1)S(1)} %get-tuple-element.69.rows_ref), custom_call_target="tpu_custom_call" | custom-call | tf_op jit(solution)/shard_map/pallas_call | solution.py:199
  56.7 2.4 %shard_map.124 = (bf16[1,608,3584]{2,1,0:T(8,128)(2,1)}, f32[8,128]{1,0:T(8,128)S(1)}) custom-call(bf16[608,256]{1,0:T(8,128)(2,1)S(1)} %get-tuple-element.73.dup_ref.left_ref, bf16[256,3584]{1,0:T(8,128)(2,1)S(1)} %get-tuple-element.69.rows_ref), custom_call_target="tpu_custom_call" | custom-call | tf_op jit(solution)/shard_map/pallas_call | solution.py:199
  59.2 3.0 %shard_map.127 = (bf16[1,608,3584]{2,1,0:T(8,128)(2,1)}, f32[8,128]{1,0:T(8,128)}) custom-call(bf16[608,256]{1,0:T(8,128)(2,1)S(1)} %get-tuple-element.80.left_ref, bf16[256,3584]{1,0:T(8,128)(2,1)S(1)} %get-tuple-element.81.rows_ref), custom_call_target="tpu_custom_call" | custom-call | tf_op jit(solution)/shard_map/pallas_call | solution.py:199
  (46 shorter events, 8.9 us)
Async XLA Ops:
  2.2 7.5 %collective-permute-start.2 = (bf16[128,896]{1,0:T(8,128)(2,1)S(1)}, bf16[128,896]{1,0:T(8,128)(2,1)S(1)}, u32[]{:S(2)}, u32[]{:S(2)}) collective-permute-start(bf16[128,896]{1,0:T(8,128)(2,1)S(1)} %get-tuple-element.46.refs_0_.refs_8_), channel_id=1, source_target_pairs={{0,1},{1,0},{2,3},{3,2},{4,5},{5,4},{6,7},{7,6},{8,9},{9,8},{10,11... | collective-permute-start | bytes 688136 | tf_op jit(solution)/shard_map/ppermute | solution.py:241
  2.7 15.1 %collective-permute-start.4 = (bf16[128,896]{1,0:T(8,128)(2,1)S(1)}, bf16[128,896]{1,0:T(8,128)(2,1)S(1)}, u32[]{:S(2)}, u32[]{:S(2)}) collective-permute-start(bf16[128,896]{1,0:T(8,128)(2,1)S(1)} %get-tuple-element.52), channel_id=1, source_target_pairs={{0,8},{4,12},{8,0},{12,4},{1,9},{5,13},{9,1},{13,5},{2,10},{6,14},... | collective-permute-start | bytes 688136 | tf_op jit(solution)/shard_map/ppermute | solution.py:238
  6.4 13.2 %collective-permute-start = (bf16[128,896]{1,0:T(8,128)(2,1)S(1)}, bf16[128,896]{1,0:T(8,128)(2,1)S(1)}, u32[]{:S(2)}, u32[]{:S(2)}) collective-permute-start(bf16[128,896]{1,0:T(8,128)(2,1)S(1)} %get-tuple-element.44), channel_id=1, source_target_pairs={{0,4},{4,0},{8,12},{12,8},{1,5},{5,1},{9,13},{13,9},{2,6},{6,2},{1... | collective-permute-start | bytes 688136 | tf_op jit(solution)/shard_map/ppermute | solution.py:238
  8.0 11.6 %collective-permute-start.1 = (bf16[128,896]{1,0:T(8,128)(2,1)S(1)}, bf16[128,896]{1,0:T(8,128)(2,1)S(1)}, u32[]{:S(2)}, u32[]{:S(2)}) collective-permute-start(bf16[128,896]{1,0:T(8,128)(2,1)S(1)} %get-tuple-element.46.refs_0_.refs_8_), channel_id=1, source_target_pairs={{0,2},{1,3},{2,0},{3,1},{4,6},{5,7},{6,4},{7,5},{8,10},{9,11},{10,... | collective-permute-start | bytes 688136 | tf_op jit(solution)/shard_map/ppermute | solution.py:241
  9.5 14.2 %collective-permute-start.6 = (bf16[128,896]{1,0:T(8,128)(2,1)S(1)}, bf16[128,896]{1,0:T(8,128)(2,1)S(1)}, u32[]{:S(2)}, u32[]{:S(2)}) collective-permute-start(bf16[128,896]{1,0:T(8,128)(2,1)S(1)} %get-tuple-element.54), channel_id=1, source_target_pairs={{0,12},{4,8},{8,4},{12,0},{1,13},{5,9},{9,5},{13,1},{2,14},{6,10},... | collective-permute-start | bytes 688136 | tf_op jit(solution)/shard_map/ppermute | solution.py:238
  17.8 8.5 %collective-permute-start.5 = (bf16[128,896]{1,0:T(8,128)(2,1)S(1)}, bf16[128,896]{1,0:T(8,128)(2,1)S(1)}, u32[]{:S(2)}, u32[]{:S(2)}) collective-permute-start(bf16[128,896]{1,0:T(8,128)(2,1)S(1)} %collective-permute-done.4.refs_2_.refs_10_), channel_id=1, source_target_pairs={{0,2},{1,3},{2,0},{3,1},{4,6},{5,7},{6,4},{7,5},{8,10},{9,11},{10,... | collective-permute-start | bytes 688136 | tf_op jit(solution)/shard_map/ppermute | solution.py:241
  19.6 8.5 %collective-permute-start.11 = (bf16[128,896]{1,0:T(8,128)(2,1)S(1)}, bf16[128,896]{1,0:T(8,128)(2,1)S(1)}, u32[]{:S(2)}, u32[]{:S(2)}) collective-permute-start(bf16[128,896]{1,0:T(8,128)(2,1)S(1)} %collective-permute-done.refs_1_.refs_9_), channel_id=1, source_target_pairs={{0,1},{1,0},{2,3},{3,2},{4,5},{5,4},{6,7},{7,6},{8,9},{9,8},{10,11... | collective-permute-start | bytes 688136 | tf_op jit(solution)/shard_map/ppermute | solution.py:241
  19.6 8.5 %collective-permute-start.12 = (bf16[128,896]{1,0:T(8,128)(2,1)S(1)}, bf16[128,896]{1,0:T(8,128)(2,1)S(1)}, u32[]{:S(2)}, u32[]{:S(2)}) collective-permute-start(bf16[128,896]{1,0:T(8,128)(2,1)S(1)} %collective-permute-done.4.refs_2_.refs_10_), channel_id=1, source_target_pairs={{0,1},{1,0},{2,3},{3,2},{4,5},{5,4},{6,7},{7,6},{8,9},{9,8},{10,11... | collective-permute-start | bytes 688136 | tf_op jit(solution)/shard_map/ppermute | solution.py:241
  20.1 11.1 %collective-permute-start.3 = (bf16[128,896]{1,0:T(8,128)(2,1)S(1)}, bf16[128,896]{1,0:T(8,128)(2,1)S(1)}, u32[]{:S(2)}, u32[]{:S(2)}) collective-permute-start(bf16[128,896]{1,0:T(8,128)(2,1)S(1)} %collective-permute-done.refs_1_.refs_9_), channel_id=1, source_target_pairs={{0,2},{1,3},{2,0},{3,1},{4,6},{5,7},{6,4},{7,5},{8,10},{9,11},{10,... | collective-permute-start | bytes 688136 | tf_op jit(solution)/shard_map/ppermute | solution.py:241
  23.7 7.6 %collective-permute-start.13 = (bf16[128,896]{1,0:T(8,128)(2,1)S(1)}, bf16[128,896]{1,0:T(8,128)(2,1)S(1)}, u32[]{:S(2)}, u32[]{:S(2)}) collective-permute-start(bf16[128,896]{1,0:T(8,128)(2,1)S(1)} %collective-permute-done.6.refs_3_.refs_11_), channel_id=1, source_target_pairs={{0,1},{1,0},{2,3},{3,2},{4,5},{5,4},{6,7},{7,6},{8,9},{9,8},{10,11... | collective-permute-start | bytes 688136 | tf_op jit(solution)/shard_map/ppermute | solution.py:241
  26.3 8.4 %collective-permute-start.7 = (bf16[128,896]{1,0:T(8,128)(2,1)S(1)}, bf16[128,896]{1,0:T(8,128)(2,1)S(1)}, u32[]{:S(2)}, u32[]{:S(2)}) collective-permute-start(bf16[128,896]{1,0:T(8,128)(2,1)S(1)} %collective-permute-done.6.refs_3_.refs_11_), channel_id=1, source_target_pairs={{0,2},{1,3},{2,0},{3,1},{4,6},{5,7},{6,4},{7,5},{8,10},{9,11},{10,... | collective-permute-start | bytes 688136 | tf_op jit(solution)/shard_map/ppermute | solution.py:241
  28.1 6.6 %collective-permute-start.8 = (bf16[128,896]{1,0:T(8,128)(2,1)S(1)}, bf16[128,896]{1,0:T(8,128)(2,1)S(1)}, u32[]{:S(2)}, u32[]{:S(2)}) collective-permute-start(bf16[128,896]{1,0:T(8,128)(2,1)S(1)} %collective-permute-done.1.refs_0_), channel_id=1, source_target_pairs={{0,1},{1,0},{2,3},{3,2},{4,5},{5,4},{6,7},{7,6},{8,9},{9,8},{10,11... | collective-permute-start | bytes 688136 | tf_op jit(solution)/shard_map/ppermute | solution.py:241
  28.2 6.6 %collective-permute-start.10 = (bf16[128,896]{1,0:T(8,128)(2,1)S(1)}, bf16[128,896]{1,0:T(8,128)(2,1)S(1)}, u32[]{:S(2)}, u32[]{:S(2)}) collective-permute-start(bf16[128,896]{1,0:T(8,128)(2,1)S(1)} %collective-permute-done.5.refs_2_), channel_id=1, source_target_pairs={{0,1},{1,0},{2,3},{3,2},{4,5},{5,4},{6,7},{7,6},{8,9},{9,8},{10,11... | collective-permute-start | bytes 688136 | tf_op jit(solution)/shard_map/ppermute | solution.py:241
  31.3 3.5 %collective-permute-start.9 = (bf16[128,896]{1,0:T(8,128)(2,1)S(1)}, bf16[128,896]{1,0:T(8,128)(2,1)S(1)}, u32[]{:S(2)}, u32[]{:S(2)}) collective-permute-start(bf16[128,896]{1,0:T(8,128)(2,1)S(1)} %collective-permute-done.3.refs_1_), channel_id=1, source_target_pairs={{0,1},{1,0},{2,3},{3,2},{4,5},{5,4},{6,7},{7,6},{8,9},{9,8},{10,11... | collective-permute-start | bytes 688136 | tf_op jit(solution)/shard_map/ppermute | solution.py:241
  34.8 1.5 %collective-permute-start.14 = (bf16[128,896]{1,0:T(8,128)(2,1)S(1)}, bf16[128,896]{1,0:T(8,128)(2,1)S(1)}, u32[]{:S(2)}, u32[]{:S(2)}) collective-permute-start(bf16[128,896]{1,0:T(8,128)(2,1)S(1)} %collective-permute-done.7.refs_3_), channel_id=1, source_target_pairs={{0,1},{1,0},{2,3},{3,2},{4,5},{5,4},{6,7},{7,6},{8,9},{9,8},{10,11... | collective-permute-start | bytes 688136 | tf_op jit(solution)/shard_map/ppermute | solution.py:241
  39.5 2.6 %collective-permute-start.16 = (bf16[264,896]{1,0:T(8,128)(2,1)S(1)}, bf16[264,896]{1,0:T(8,128)(2,1)S(1)}, u32[]{:S(2)}, u32[]{:S(2)}) collective-permute-start(bf16[264,896]{1,0:T(8,128)(2,1)S(1)} %shard_map.118), channel_id=1, source_target_pairs={{0,1},{1,0},{2,3},{3,2},{4,5},{5,4},{6,7},{7,6},{8,9},{9,8},{10,11... | collective-permute-start | bytes 1419272 | tf_op jit(solution)/shard_map/ppermute | solution.py:241
  40.7 6.7 %collective-permute-start.15 = (bf16[256,896]{1,0:T(8,128)(2,1)S(1)}, bf16[256,896]{1,0:T(8,128)(2,1)S(1)}, u32[]{:S(2)}, u32[]{:S(2)}) collective-permute-start(bf16[256,896]{1,0:T(8,128)(2,1)S(1)} %shard_map.116), channel_id=1, source_target_pairs={{0,1},{1,0},{2,3},{3,2},{4,5},{5,4},{6,7},{7,6},{8,9},{9,8},{10,11... | collective-permute-start | bytes 1376264 | tf_op jit(solution)/shard_map/ppermute | solution.py:241
  42.3 6.4 %collective-permute-start.20 = (bf16[72,896]{1,0:T(8,128)(2,1)S(1)}, bf16[72,896]{1,0:T(8,128)(2,1)S(1)}, u32[]{:S(2)}, u32[]{:S(2)}) collective-permute-start(bf16[72,896]{1,0:T(8,128)(2,1)S(1)} %get-tuple-element.72), channel_id=1, source_target_pairs={{0,2},{1,3},{2,0},{3,1},{4,6},{5,7},{6,4},{7,5},{8,10},{9,11},{10,... | collective-permute-start | bytes 387080 | tf_op jit(solution)/shard_map/ppermute | solution.py:241
  43.7 11.7 %collective-permute-start.19 = (bf16[72,896]{1,0:T(8,128)(2,1)S(1)}, bf16[72,896]{1,0:T(8,128)(2,1)S(1)}, u32[]{:S(2)}, u32[]{:S(2)}) collective-permute-start(bf16[72,896]{1,0:T(8,128)(2,1)S(1)} %get-tuple-element.71), channel_id=1, source_target_pairs={{0,2},{1,3},{2,0},{3,1},{4,6},{5,7},{6,4},{7,5},{8,10},{9,11},{10,... | collective-permute-start | bytes 387080 | tf_op jit(solution)/shard_map/ppermute | solution.py:241
  44.4 11.1 %collective-permute-start.18 = (bf16[72,896]{1,0:T(8,128)(2,1)S(1)}, bf16[72,896]{1,0:T(8,128)(2,1)S(1)}, u32[]{:S(2)}, u32[]{:S(2)}) collective-permute-start(bf16[72,896]{1,0:T(8,128)(2,1)S(1)} %get-tuple-element.67), channel_id=1, source_target_pairs={{0,2},{1,3},{2,0},{3,1},{4,6},{5,7},{6,4},{7,5},{8,10},{9,11},{10,... | collective-permute-start | bytes 387080 | tf_op jit(solution)/shard_map/ppermute | solution.py:241
  46.7 12.4 %collective-permute-start.17 = (bf16[72,896]{1,0:T(8,128)(2,1)S(1)}, bf16[72,896]{1,0:T(8,128)(2,1)S(1)}, u32[]{:S(2)}, u32[]{:S(2)}) collective-permute-start(bf16[72,896]{1,0:T(8,128)(2,1)S(1)} %get-tuple-element.65), channel_id=1, source_target_pairs={{0,2},{1,3},{2,0},{3,1},{4,6},{5,7},{6,4},{7,5},{8,10},{9,11},{10,... | collective-permute-start | bytes 387080 | tf_op jit(solution)/shard_map/ppermute | solution.py:241
  48.8 10.4 %collective-permute-start.23 = (bf16[72,896]{1,0:T(8,128)(2,1)S(1)}, bf16[72,896]{1,0:T(8,128)(2,1)S(1)}, u32[]{:S(2)}, u32[]{:S(2)}) collective-permute-start(bf16[72,896]{1,0:T(8,128)(2,1)S(1)} %shard_map.123), channel_id=1, source_target_pairs={{0,12},{4,8},{8,4},{12,0},{1,13},{5,9},{9,5},{13,1},{2,14},{6,10},... | collective-permute-start | bytes 387080 | tf_op jit(solution)/shard_map/ppermute | solution.py:238
  55.4 7.1 %collective-permute-start.22 = (bf16[72,896]{1,0:T(8,128)(2,1)S(1)}, bf16[72,896]{1,0:T(8,128)(2,1)S(1)}, u32[]{:S(2)}, u32[]{:S(2)}) collective-permute-start(bf16[72,896]{1,0:T(8,128)(2,1)S(1)} %shard_map.122), channel_id=1, source_target_pairs={{0,8},{4,12},{8,0},{12,4},{1,9},{5,13},{9,1},{13,5},{2,10},{6,14},... | collective-permute-start | bytes 387080 | tf_op jit(solution)/shard_map/ppermute | solution.py:238
  55.7 6.9 %collective-permute-start.21 = (bf16[72,896]{1,0:T(8,128)(2,1)S(1)}, bf16[72,896]{1,0:T(8,128)(2,1)S(1)}, u32[]{:S(2)}, u32[]{:S(2)}) collective-permute-start(bf16[72,896]{1,0:T(8,128)(2,1)S(1)} %shard_map.121), channel_id=1, source_target_pairs={{0,4},{4,0},{8,12},{12,8},{1,5},{5,1},{9,13},{13,9},{2,6},{6,2},{1... | collective-permute-start | bytes 387080 | tf_op jit(solution)/shard_map/ppermute | solution.py:238
  (2 other events, 16.9 us)

commit v6 on v5

--- a/solution.py
+++ b/solution.py
@@ -117,16 +117,25 @@
     back_ref[...] = dot_nt(down_w[0, :, columns], grads_ref[...])
 
 
+def with_slice(relative, groups, parts, mats, sums, rows_ref, grads_ref):
+    slot = lax.axis_index("expert") ^ relative
+    assemble(parts, (relative,), groups, slot, rows_ref, grads_ref)
+    width = rows_ref.shape[1]
+    columns = pl.ds(pl.multiple_of(slot * width, width), width)
+    rights = (rows_ref, rows_ref, grads_ref)
+    return [total[...] + dot_nt(mat[0, :, columns], right[...]) for total, mat, right in zip(sums, mats, rights)]
+
+
+def side_kernel(groups, *refs):
+    parts, mats, sums, outs = refs[:groups], refs[groups : groups + 3], refs[groups + 3 : groups + 6], refs[-5:]
+    for out, value in zip(outs, with_slice(2, groups, parts, mats, sums, *outs[3:])):
+        out[...] = value
+
+
 def middle_kernel(groups, *refs):
-    parts = refs[: 4 * groups]
-    (gate_w, up_w, down_w, gate_ref, up_ref, back_ref,
-     rows_ref, grads_ref, dgate_ref, dup_ref, hid_ref, stat_ref) = refs[4 * groups :]
-    assemble(parts, (2, 3, 0, 1), groups, 0, rows_ref, grads_ref)
-    half = rows_ref.shape[1] // 2
-    columns = pl.ds(pl.multiple_of((1 - lax.axis_index("expert") // 2) * half, half), half)
-    gate = gate_ref[...] + dot_nt(gate_w[0, :, columns], rows_ref[:, columns])
-    up = up_ref[...] + dot_nt(up_w[0, :, columns], rows_ref[:, columns])
-    back = back_ref[...] + dot_nt(down_w[0, :, columns], grads_ref[:, columns])
+    parts, mats, sums = refs[:groups], refs[groups : groups + 3], refs[groups + 3 : groups + 6]
+    rows_ref, grads_ref, dgate_ref, dup_ref, hid_ref, stat_ref = refs[groups + 6 :]
+    gate, up, back = with_slice(3, groups, parts, mats, sums, rows_ref, grads_ref)
     sig = 1.0 / (1.0 + jnp.exp(-gate))
     silu = gate * sig
     hidden = silu * up
@@ -181,30 +190,39 @@
     out[capacity:, capacity:] = jnp.zeros((EXTRA, out.shape[1] - capacity), BF16)
 
 
-def grad_kernel(tile, left_ref, rows_ref, out_ref, mark_ref, held_ref, sems):
-    copies = []
-    for index in range(rows_ref.shape[1] // tile):
-        columns = slice(index * tile, (index + 1) * tile)
-        held_ref[:, columns] = dot_nn(left_ref[...], rows_ref[:, columns]).astype(BF16)
-        copies.append(pltpu.make_async_copy(held_ref.at[:, columns], out_ref.at[0, :, columns], sems.at[index]))
+def grad_kernel(tiles, left_ref, local_ref, other_ref, across_ref, out_ref, mark_ref, held_ref, sems):
+    me = lax.axis_index("expert")
+    width = other_ref.shape[1]
+    pieces = ((local_ref, (me // 2) * 2), (other_ref, me ^ 2), (across_ref, me ^ 3))
+    copies, held_from = [], 0
+    for index, (piece, start, size) in enumerate(tiles):
+        piece_ref, slot = pieces[piece]
+        held = held_ref.at[:, held_from : held_from + size]
+        held[...] = dot_nn(left_ref[...], piece_ref[:, start : start + size]).astype(BF16)
+        columns = pl.ds(pl.multiple_of(slot * width + start, 128), size)
+        copies.append(pltpu.make_async_copy(held, out_ref.at[0, :, columns], sems.at[index]))
         copies[-1].start()
+        held_from += size
     mark_ref[...] = jnp.zeros(mark_ref.shape, F32)
     for copy in copies:
         copy.wait()
 
 
-def weight_grad(left, rows):
-    units, features = left.shape[0], rows.shape[1]
-    tile = 512 if features % 512 == 0 else features
+def weight_grad(left, pieces):
+    units, features = left.shape[0], sum(piece.shape[1] for piece in pieces)
+    tiles = [
+        (which, start, min(512, piece.shape[1] - start))
+        for which, piece in enumerate(pieces) for start in range(0, piece.shape[1], 512)
+    ]
     return pl.pallas_call(
-        functools.partial(grad_kernel, tile),
+        functools.partial(grad_kernel, tiles),
         out_shape=[jax.ShapeDtypeStruct((1, units, features), BF16), jax.ShapeDtypeStruct((8, 128), F32)],
-        in_specs=[pl.BlockSpec(memory_space=pltpu.VMEM)] * 2,
+        in_specs=[pl.BlockSpec(memory_space=pltpu.VMEM)] * 4,
         out_specs=[pl.BlockSpec(memory_space=pltpu.HBM), pl.BlockSpec(memory_space=pltpu.VMEM)],
-        scratch_shapes=[pltpu.VMEM((units, features), BF16), pltpu.SemaphoreType.DMA((features // tile,))],
+        scratch_shapes=[pltpu.VMEM((units, features), BF16), pltpu.SemaphoreType.DMA((len(tiles),))],
         compiler_params=pltpu.CompilerParams(vmem_limit_bytes=10 * MIB),
         cost_estimate=pl.CostEstimate(flops=0, bytes_accessed=0, transcendentals=0),
-    )(left, rows)
+    )(left, *pieces)
 
 
 def finish_kernel(groups, ids_ref, gates_in_ref, pick_ref, *refs):
@@ -270,19 +288,24 @@
     across = [over_expert(x, 1) for x in other[:-1]]
 
     dense = 2 * rows * units * features
-    partial_sums = call(
+    *sums, rows_local, grads_local = call(
         functools.partial(local_kernel, groups),
-        [shape((units, rows), F32)] * 3,
+        [shape((units, rows), F32)] * 3 + [shape((rows, 2 * width), BF16)] * 2,
         *own, *partner, *mats, flops=3 * dense // 2, nbytes=3 * units * features,
-        scratch=[pltpu.VMEM((rows, 2 * width), BF16)] * 2,
-    )
-    across.append(over_expert(after((other[-1], partial_sums[0]))[0], 1))
-    rows_in, rows_grad, dgate, dup, hid, stat = call(
+    )
+    across.append(over_expert(after((other[-1], sums[0]))[0], 1))
+    *sums, rows_other, grads_other = call(
+        functools.partial(side_kernel, groups),
+        [shape((units, rows), F32)] * 3 + [shape((rows, width), BF16)] * 2,
+        *other, *mats, *sums, flops=3 * dense // 4, nbytes=3 * units * features // 2,
+    )
+    rows_across, grads_across, dgate, dup, hid, stat = call(
         functools.partial(middle_kernel, groups),
-        [shape((rows, features), BF16)] * 2 + [shape((units, rows), BF16)] * 3 + [shape((8, rows), F32)],
-        *other, *across, *own, *partner, *mats, *partial_sums,
-        flops=3 * dense // 2, nbytes=3 * units * features,
-    )
+        [shape((rows, width), BF16)] * 2 + [shape((units, rows), BF16)] * 3 + [shape((8, rows), F32)],
+        *across, *mats, *sums, flops=3 * dense // 4, nbytes=3 * units * features // 2,
+    )
+    rows_in = [rows_local, rows_other, rows_across]
+    rows_grad = [grads_local, grads_other, grads_across]
 
     def input_part(relative, extra, kind):
         return call(

time: 63.6 us -> 63 us (level)
  waiting for transfers between devices: 16.3 us -> 15.2 us
    ppermute x18, waiting for transfers between devices: 9.47 us -> 8.19 us  [over_expert(): lax.ppermute(x, 'expert', [(i, i ^ relative) for i in range(experts)])]
    pallas_call x15 -> x16, Pallas kernels: 16.4 us -> 16.6 us  [call(): pl.pallas_call(kernel, out_shape=outs, in_specs=[pl.BlockSpec(memory_spac...]
  transfers between devices with their start and end apart: 24 -> 24, of which waited for: 8 -> 8; matrix products, arithmetic and copies ran while one was open for 0% -> 0% of each run, Pallas kernels for 29% -> 32%
where the time goes in v6:
time: 63 us; the launch traced here: 62.9 us
  Pallas kernels  24.9 us (40%)
  starting transfers between devices  22 us (35%)
  waiting for transfers between devices  15.2 us (24%)
  between operations  0.83 us (1%)
    pallas_call x16, Pallas kernels, call(): pl.pallas_call(kernel, out_shape=outs, in_specs=[pl.BlockSpec(memory_spac...  16.6 us
    ppermute x18, starting transfers between devices, over_expert(): lax.ppermute(x, 'expert', [(i, i ^ relative) for i in range(experts)])  11.7 us
    ppermute x6, starting transfers between devices, over_node(): return lax.ppermute(x, 'node', [(i, i ^ shift) for i in range(groups)])  10.3 us
    pallas_call x3, Pallas kernels, weight_grad(): pl.pallas_call(functools.partial(grad_kernel, tiles), out_shape=[jax.Shap...  8.22 us
    ppermute x18, waiting for transfers between devices, over_expert(): lax.ppermute(x, 'expert', [(i, i ^ relative) for i in range(experts)])  8.19 us
    ppermute x6, waiting for transfers between devices, over_node(): return lax.ppermute(x, 'node', [(i, i ^ shift) for i in range(groups)])  7.03 us
  transfers between devices with their start and end apart: 24, of which 8 were waited for; matrix products, arithmetic and copies ran while one was open for 0% of the time, Pallas kernels for 32%

profile of v6, /device:TPU:0, one launch (start us, length us, event | category | flops | bytes accessed | tf_op | source)
XLA Modules:
  0.0 62.9 jit_solution(9038295529872618187)
XLA Ops:
  0.6 1.6 %shard_map.110 = (bf16[128,896]{1,0:T(8,128)(2,1)S(1)}, bf16[128,896]{1,0:T(8,128)(2,1)S(1)}, bf16[128,896]{1,0:T(8,128)(2,1)S(1)}, bf16[128,896]{1,0:T(8,128)(2,1)S(1)}) custom-call(s32[2,128]{1,0:T(2,128)} %bitcast.3, bf16[2,128]{1,0:T(2,128)(2,1)} %bitcast.6, bf16[128,896]{1,0:T(8,128)(2,1)} %refs_2_.1, bf16[128,896]{1,0:T(8,128)(2,1)} %refs_3_.1), custom_call_target="tpu_custom_call" | custom-call | flops 117440512 | bytes 688128 | tf_op jit(solution)/shard_map/pallas_call | solution.py:31
  2.7 3.7 %collective-permute-start.6 = (bf16[128,896]{1,0:T(8,128)(2,1)S(1)}, bf16[128,896]{1,0:T(8,128)(2,1)S(1)}, u32[]{:S(2)}, u32[]{:S(2)}) collective-permute-start(bf16[128,896]{1,0:T(8,128)(2,1)S(1)} %get-tuple-element.59), channel_id=1, source_target_pairs={{0,8},{4,12},{8,0},{12,4},{1,9},{5,13},{9,1},{13,5},{2,10},{6,14},... | collective-permute-start | bytes 688136 | tf_op jit(solution)/shard_map/ppermute | solution.py:256
  6.4 1.6 %collective-permute-start = (bf16[128,896]{1,0:T(8,128)(2,1)S(1)}, bf16[128,896]{1,0:T(8,128)(2,1)S(1)}, u32[]{:S(2)}, u32[]{:S(2)}) collective-permute-start(bf16[128,896]{1,0:T(8,128)(2,1)S(1)} %get-tuple-element.51), channel_id=1, source_target_pairs={{0,4},{4,0},{8,12},{12,8},{1,5},{5,1},{9,13},{13,9},{2,6},{6,2},{1... | collective-permute-start | bytes 688136 | tf_op jit(solution)/shard_map/ppermute | solution.py:256
  8.0 1.5 %collective-permute-start.1 = (bf16[128,896]{1,0:T(8,128)(2,1)S(1)}, bf16[128,896]{1,0:T(8,128)(2,1)S(1)}, u32[]{:S(2)}, u32[]{:S(2)}) collective-permute-start(bf16[128,896]{1,0:T(8,128)(2,1)S(1)} %get-tuple-element.53.refs_0_), channel_id=1, source_target_pairs={{0,2},{1,3},{2,0},{3,1},{4,6},{5,7},{6,4},{7,5},{8,10},{9,11},{10,... | collective-permute-start | bytes 688136 | tf_op jit(solution)/shard_map/ppermute | solution.py:259
  9.7 4.8 %shard_map.112 = (bf16[1,608,3584]{2,1,0:T(8,128)(2,1)S(1)}, bf16[1,608,3584]{2,1,0:T(8,128)(2,1)S(1)}, bf16[1,608,3584]{2,1,0:T(8,128)(2,1)S(1)}) custom-call(bf16[1,608,3584]{2,1,0:T(8,128)(2,1)} %refs_0_, bf16[1,608,3584]{2,1,0:T(8,128)(2,1)} %refs_1_, bf16[1,608,3584]{2,1,0:T(8,128)(2,1)} %refs_2_.2), custom_call_target="tpu_custom_call" | custom-call | bytes 26148864 | tf_op jit(solution)/shard_map/pallas_call | solution.py:31
  14.6 3.3 %collective-permute-done.6.refs_2_ = bf16[128,896]{1,0:T(8,128)(2,1)S(1)} collective-permute-done((bf16[128,896]{1,0:T(8,128)(2,1)S(1)}, bf16[128,896]{1,0:T(8,128)(2,1)S(1)}, u32[]{:S(2)}, u32[]{:S(2)}) %collective-permute-start.6) | collective-permute-done | bytes 229408 | tf_op jit(solution)/shard_map/ppermute | solution.py:256
  17.8 1.8 %collective-permute-start.7 = (bf16[128,896]{1,0:T(8,128)(2,1)S(1)}, bf16[128,896]{1,0:T(8,128)(2,1)S(1)}, u32[]{:S(2)}, u32[]{:S(2)}) collective-permute-start(bf16[128,896]{1,0:T(8,128)(2,1)S(1)} %collective-permute-done.6.refs_2_), channel_id=1, source_target_pairs={{0,2},{1,3},{2,0},{3,1},{4,6},{5,7},{6,4},{7,5},{8,10},{9,11},{10,... | collective-permute-start | bytes 688136 | tf_op jit(solution)/shard_map/ppermute | solution.py:259
  20.4 3.3 %collective-permute-done.9.refs_3_ = bf16[128,896]{1,0:T(8,128)(2,1)S(1)} collective-permute-done((bf16[128,896]{1,0:T(8,128)(2,1)S(1)}, bf16[128,896]{1,0:T(8,128)(2,1)S(1)}, u32[]{:S(2)}, u32[]{:S(2)}) %collective-permute-start.9) | collective-permute-done | bytes 229408 | tf_op jit(solution)/shard_map/ppermute | solution.py:256
  23.7 2.7 %collective-permute-done.7.refs_2_ = bf16[128,896]{1,0:T(8,128)(2,1)S(1)} collective-permute-done((bf16[128,896]{1,0:T(8,128)(2,1)S(1)}, bf16[128,896]{1,0:T(8,128)(2,1)S(1)}, u32[]{:S(2)}, u32[]{:S(2)}) %collective-permute-start.7) | collective-permute-done | bytes 229408 | tf_op jit(solution)/shard_map/ppermute | solution.py:259
  26.3 1.8 %collective-permute-start.10 = (bf16[128,896]{1,0:T(8,128)(2,1)S(1)}, bf16[128,896]{1,0:T(8,128)(2,1)S(1)}, u32[]{:S(2)}, u32[]{:S(2)}) collective-permute-start(bf16[128,896]{1,0:T(8,128)(2,1)S(1)} %collective-permute-done.9.refs_3_), channel_id=1, source_target_pairs={{0,2},{1,3},{2,0},{3,1},{4,6},{5,7},{6,4},{7,5},{8,10},{9,11},{10,... | collective-permute-start | bytes 688136 | tf_op jit(solution)/shard_map/ppermute | solution.py:259
  28.7 2.6 %collective-permute-done.4.refs_1_ = bf16[128,896]{1,0:T(8,128)(2,1)S(1)} collective-permute-done((bf16[128,896]{1,0:T(8,128)(2,1)S(1)}, bf16[128,896]{1,0:T(8,128)(2,1)S(1)}, u32[]{:S(2)}, u32[]{:S(2)}) %collective-permute-start.4) | collective-permute-done | bytes 229408 | tf_op jit(solution)/shard_map/ppermute | solution.py:259
  31.3 2.0 %shard_map.113 = (f32[608,256]{1,0:T(8,128)S(1)}, f32[608,256]{1,0:T(8,128)S(1)}, f32[608,256]{1,0:T(8,128)S(1)}, bf16[256,1792]{1,0:T(8,128)(2,1)S(1)}, bf16[256,1792]{1,0:T(8,128)(2,1)S(1)}) custom-call(bf16[128,896]{1,0:T(8,128)(2,1)S(1)} %get-tuple-element.53.refs_0_, bf16[128,896]{1,0:T(8,128)(2,1)S(1)} %collective-permute-done.refs_1_, ...), custom_call_target="tpu_custom_call" | custom-call | flops 1673527296 | bytes 6537216 | tf_op jit(solution)/shard_map/pallas_call | solution.py:31
  33.3 1.5 %collective-permute-done.10.refs_3_ = bf16[128,896]{1,0:T(8,128)(2,1)S(1)} collective-permute-done((bf16[128,896]{1,0:T(8,128)(2,1)S(1)}, bf16[128,896]{1,0:T(8,128)(2,1)S(1)}, u32[]{:S(2)}, u32[]{:S(2)}) %collective-permute-start.10) | collective-permute-done | bytes 229408 | tf_op jit(solution)/shard_map/ppermute | solution.py:259
  34.8 1.2 %shard_map.114 = (f32[608,256]{1,0:T(8,128)S(1)}, f32[608,256]{1,0:T(8,128)S(1)}, f32[608,256]{1,0:T(8,128)S(1)}, bf16[256,896]{1,0:T(8,128)(2,1)S(1)}, bf16[256,896]{1,0:T(8,128)(2,1)S(1)}) custom-call(bf16[128,896]{1,0:T(8,128)(2,1)S(1)} %collective-permute-done.1.refs_0_, bf16[128,896]{1,0:T(8,128)(2,1)S(1)} %collective-permute-done.4.refs_1_, ...), custom_call_target="tpu_custom_call" | custom-call | flops 836763648 | bytes 3268608 | tf_op jit(solution)/shard_map/pallas_call | solution.py:31
  36.2 1.3 %shard_map.115 = (bf16[256,896]{1,0:T(8,128)(2,1)S(1)}, bf16[256,896]{1,0:T(8,128)(2,1)S(1)}, bf16[608,256]{1,0:T(8,128)(2,1)S(1)}, bf16[608,256]{1,0:T(8,128)(2...) custom-call(bf16[128,896]{1,0:T(8,128)(2,1)S(1)} %collective-permute-done.2.refs_0_, ...), custom_call_target="tpu_custom_call" | custom-call | flops 836763648 | bytes 3268608 | tf_op jit(solution)/shard_map/pallas_call | solution.py:31
  37.6 1.0 %shard_map.119 = bf16[264,896]{1,0:T(8,128)(2,1)S(1)} custom-call(bf16[608,256]{1,0:T(8,128)(2,1)S(1)} %get-tuple-element.78.dgate_ref.left_ref, bf16[608,256]{1,0:T(8,128)(2,1)S(1)} %get-tuple-element.85.dup_ref.left_ref, bf16[1,608,3584]{2,1,0:T(8,128)(2,1)S(1)} %get-tuple-element.57.refs_8_.refs_4_.gate_w, ...), custom_call_target="tpu_custom_call" | custom-call | flops 557842432 | bytes 2179072 | tf_op jit(solution)/shard_map/pallas_call | solution.py:31
  38.9 1.0 %shard_map.117 = bf16[256,896]{1,0:T(8,128)(2,1)S(1)} custom-call(bf16[608,256]{1,0:T(8,128)(2,1)S(1)} %get-tuple-element.78.dgate_ref.left_ref, bf16[608,256]{1,0:T(8,128)(2,1)S(1)} %get-tuple-element.85.dup_ref.left_ref, bf16[1,608,3584]{2,1,0:T(8,128)(2,1)S(1)} %get-tuple-element.57.refs_8_.refs_4_.gate_w, ...), custom_call_target="tpu_custom_call" | custom-call | flops 557842432 | bytes 2179072 | tf_op jit(solution)/shard_map/pallas_call | solution.py:31
  41.3 1.5 %collective-permute-start.20 = (bf16[72,896]{1,0:T(8,128)(2,1)S(1)}, bf16[72,896]{1,0:T(8,128)(2,1)S(1)}, u32[]{:S(2)}, u32[]{:S(2)}) collective-permute-start(bf16[72,896]{1,0:T(8,128)(2,1)S(1)} %get-tuple-element.84), channel_id=1, source_target_pairs={{0,2},{1,3},{2,0},{3,1},{4,6},{5,7},{6,4},{7,5},{8,10},{9,11},{10,... | collective-permute-start | bytes 387080 | tf_op jit(solution)/shard_map/ppermute | solution.py:259
  43.4 1.4 %collective-permute-start.18 = (bf16[72,896]{1,0:T(8,128)(2,1)S(1)}, bf16[72,896]{1,0:T(8,128)(2,1)S(1)}, u32[]{:S(2)}, u32[]{:S(2)}) collective-permute-start(bf16[72,896]{1,0:T(8,128)(2,1)S(1)} %get-tuple-element.77), channel_id=1, source_target_pairs={{0,2},{1,3},{2,0},{3,1},{4,6},{5,7},{6,4},{7,5},{8,10},{9,11},{10,... | collective-permute-start | bytes 387080 | tf_op jit(solution)/shard_map/ppermute | solution.py:259
  46.5 1.2 %collective-permute-done.20.crossed = bf16[72,896]{1,0:T(8,128)(2,1)S(1)} collective-permute-done((bf16[72,896]{1,0:T(8,128)(2,1)S(1)}, bf16[72,896]{1,0:T(8,128)(2,1)S(1)}, u32[]{:S(2)}, u32[]{:S(2)}) %collective-permute-start.20) | collective-permute-done | bytes 129056 | tf_op jit(solution)/shard_map/ppermute | solution.py:259
  47.8 4.1 %collective-permute-start.23 = (bf16[72,896]{1,0:T(8,128)(2,1)S(1)}, bf16[72,896]{1,0:T(8,128)(2,1)S(1)}, u32[]{:S(2)}, u32[]{:S(2)}) collective-permute-start(bf16[72,896]{1,0:T(8,128)(2,1)S(1)} %shard_map.124), channel_id=1, source_target_pairs={{0,12},{4,8},{8,4},{12,0},{1,13},{5,9},{9,5},{13,1},{2,14},{6,10},... | collective-permute-start | bytes 387080 | tf_op jit(solution)/shard_map/ppermute | solution.py:256
  51.9 2.5 %shard_map.121 = (bf16[1,608,3584]{2,1,0:T(8,128)(2,1)}, f32[8,128]{1,0:T(8,128)S(1)}) custom-call(bf16[608,256]{1,0:T(8,128)(2,1)S(1)} %get-tuple-element.78.dgate_ref.left_ref, bf16[256,1792]{1,0:T(8,128)(2,1)S(1)} %get-tuple-element.79.local_ref, bf16[256,896]{1,0:T(8,128)(2,1)S(1)} %get-tuple-element.80.other_ref, ...), custom_call_target="tpu_custom_call" | custom-call | tf_op jit(solution)/shard_map/pallas_call | solution.py:217
  55.7 2.6 %shard_map.125 = (bf16[1,608,3584]{2,1,0:T(8,128)(2,1)}, f32[8,128]{1,0:T(8,128)S(1)}) custom-call(bf16[608,256]{1,0:T(8,128)(2,1)S(1)} %get-tuple-element.85.dup_ref.left_ref, bf16[256,1792]{1,0:T(8,128)(2,1)S(1)} %get-tuple-element.79.local_ref, bf16[256,896]{1,0:T(8,128)(2,1)S(1)} %get-tuple-element.80.other_ref, ...), custom_call_target="tpu_custom_call" | custom-call | tf_op jit(solution)/shard_map/pallas_call | solution.py:217
  58.3 3.1 %shard_map.128 = (bf16[1,608,3584]{2,1,0:T(8,128)(2,1)}, f32[8,128]{1,0:T(8,128)}) custom-call(bf16[608,256]{1,0:T(8,128)(2,1)S(1)} %get-tuple-element.92.left_ref, bf16[256,1792]{1,0:T(8,128)(2,1)S(1)} %get-tuple-element.93.local_ref, bf16[256,896]{1,0:T(8,128)(2,1)S(1)} %get-tuple-element.94.other_ref, bf16[256,896]{1,0:T(8,128)(2,1)S(1)} %get-tuple-element.95.across_ref), custom_call_target="tpu_custom_call" | custom-call | tf_op jit(solution)/shard_map/pallas_call | solution.py:217
  (47 shorter events, 9.1 us)
Async XLA Ops:
  2.2 7.5 %collective-permute-start.3 = (bf16[128,896]{1,0:T(8,128)(2,1)S(1)}, bf16[128,896]{1,0:T(8,128)(2,1)S(1)}, u32[]{:S(2)}, u32[]{:S(2)}) collective-permute-start(bf16[128,896]{1,0:T(8,128)(2,1)S(1)} %get-tuple-element.53.refs_0_), channel_id=1, source_target_pairs={{0,1},{1,0},{2,3},{3,2},{4,5},{5,4},{6,7},{7,6},{8,9},{9,8},{10,11... | collective-permute-start | bytes 688136 | tf_op jit(solution)/shard_map/ppermute | solution.py:259
  2.7 15.1 %collective-permute-start.6 = (bf16[128,896]{1,0:T(8,128)(2,1)S(1)}, bf16[128,896]{1,0:T(8,128)(2,1)S(1)}, u32[]{:S(2)}, u32[]{:S(2)}) collective-permute-start(bf16[128,896]{1,0:T(8,128)(2,1)S(1)} %get-tuple-element.59), channel_id=1, source_target_pairs={{0,8},{4,12},{8,0},{12,4},{1,9},{5,13},{9,1},{13,5},{2,10},{6,14},... | collective-permute-start | bytes 688136 | tf_op jit(solution)/shard_map/ppermute | solution.py:256
  6.4 13.2 %collective-permute-start = (bf16[128,896]{1,0:T(8,128)(2,1)S(1)}, bf16[128,896]{1,0:T(8,128)(2,1)S(1)}, u32[]{:S(2)}, u32[]{:S(2)}) collective-permute-start(bf16[128,896]{1,0:T(8,128)(2,1)S(1)} %get-tuple-element.51), channel_id=1, source_target_pairs={{0,4},{4,0},{8,12},{12,8},{1,5},{5,1},{9,13},{13,9},{2,6},{6,2},{1... | collective-permute-start | bytes 688136 | tf_op jit(solution)/shard_map/ppermute | solution.py:256
  8.0 11.6 %collective-permute-start.1 = (bf16[128,896]{1,0:T(8,128)(2,1)S(1)}, bf16[128,896]{1,0:T(8,128)(2,1)S(1)}, u32[]{:S(2)}, u32[]{:S(2)}) collective-permute-start(bf16[128,896]{1,0:T(8,128)(2,1)S(1)} %get-tuple-element.53.refs_0_), channel_id=1, source_target_pairs={{0,2},{1,3},{2,0},{3,1},{4,6},{5,7},{6,4},{7,5},{8,10},{9,11},{10,... | collective-permute-start | bytes 688136 | tf_op jit(solution)/shard_map/ppermute | solution.py:259
  9.5 14.2 %collective-permute-start.9 = (bf16[128,896]{1,0:T(8,128)(2,1)S(1)}, bf16[128,896]{1,0:T(8,128)(2,1)S(1)}, u32[]{:S(2)}, u32[]{:S(2)}) collective-permute-start(bf16[128,896]{1,0:T(8,128)(2,1)S(1)} %get-tuple-element.61), channel_id=1, source_target_pairs={{0,12},{4,8},{8,4},{12,0},{1,13},{5,9},{9,5},{13,1},{2,14},{6,10},... | collective-permute-start | bytes 688136 | tf_op jit(solution)/shard_map/ppermute | solution.py:256
  17.8 8.5 %collective-permute-start.7 = (bf16[128,896]{1,0:T(8,128)(2,1)S(1)}, bf16[128,896]{1,0:T(8,128)(2,1)S(1)}, u32[]{:S(2)}, u32[]{:S(2)}) collective-permute-start(bf16[128,896]{1,0:T(8,128)(2,1)S(1)} %collective-permute-done.6.refs_2_), channel_id=1, source_target_pairs={{0,2},{1,3},{2,0},{3,1},{4,6},{5,7},{6,4},{7,5},{8,10},{9,11},{10,... | collective-permute-start | bytes 688136 | tf_op jit(solution)/shard_map/ppermute | solution.py:259
  19.6 8.5 %collective-permute-start.11 = (bf16[128,896]{1,0:T(8,128)(2,1)S(1)}, bf16[128,896]{1,0:T(8,128)(2,1)S(1)}, u32[]{:S(2)}, u32[]{:S(2)}) collective-permute-start(bf16[128,896]{1,0:T(8,128)(2,1)S(1)} %collective-permute-done.refs_1_), channel_id=1, source_target_pairs={{0,1},{1,0},{2,3},{3,2},{4,5},{5,4},{6,7},{7,6},{8,9},{9,8},{10,11... | collective-permute-start | bytes 688136 | tf_op jit(solution)/shard_map/ppermute | solution.py:259
  19.6 8.5 %collective-permute-start.12 = (bf16[128,896]{1,0:T(8,128)(2,1)S(1)}, bf16[128,896]{1,0:T(8,128)(2,1)S(1)}, u32[]{:S(2)}, u32[]{:S(2)}) collective-permute-start(bf16[128,896]{1,0:T(8,128)(2,1)S(1)} %collective-permute-done.6.refs_2_), channel_id=1, source_target_pairs={{0,1},{1,0},{2,3},{3,2},{4,5},{5,4},{6,7},{7,6},{8,9},{9,8},{10,11... | collective-permute-start | bytes 688136 | tf_op jit(solution)/shard_map/ppermute | solution.py:259
  20.1 11.1 %collective-permute-start.4 = (bf16[128,896]{1,0:T(8,128)(2,1)S(1)}, bf16[128,896]{1,0:T(8,128)(2,1)S(1)}, u32[]{:S(2)}, u32[]{:S(2)}) collective-permute-start(bf16[128,896]{1,0:T(8,128)(2,1)S(1)} %collective-permute-done.refs_1_), channel_id=1, source_target_pairs={{0,2},{1,3},{2,0},{3,1},{4,6},{5,7},{6,4},{7,5},{8,10},{9,11},{10,... | collective-permute-start | bytes 688136 | tf_op jit(solution)/shard_map/ppermute | solution.py:259
  23.7 7.6 %collective-permute-start.13 = (bf16[128,896]{1,0:T(8,128)(2,1)S(1)}, bf16[128,896]{1,0:T(8,128)(2,1)S(1)}, u32[]{:S(2)}, u32[]{:S(2)}) collective-permute-start(bf16[128,896]{1,0:T(8,128)(2,1)S(1)} %collective-permute-done.9.refs_3_), channel_id=1, source_target_pairs={{0,1},{1,0},{2,3},{3,2},{4,5},{5,4},{6,7},{7,6},{8,9},{9,8},{10,11... | collective-permute-start | bytes 688136 | tf_op jit(solution)/shard_map/ppermute | solution.py:259
  26.3 8.4 %collective-permute-start.10 = (bf16[128,896]{1,0:T(8,128)(2,1)S(1)}, bf16[128,896]{1,0:T(8,128)(2,1)S(1)}, u32[]{:S(2)}, u32[]{:S(2)}) collective-permute-start(bf16[128,896]{1,0:T(8,128)(2,1)S(1)} %collective-permute-done.9.refs_3_), channel_id=1, source_target_pairs={{0,2},{1,3},{2,0},{3,1},{4,6},{5,7},{6,4},{7,5},{8,10},{9,11},{10,... | collective-permute-start | bytes 688136 | tf_op jit(solution)/shard_map/ppermute | solution.py:259
  28.1 7.8 %collective-permute-start.2 = (bf16[128,896]{1,0:T(8,128)(2,1)S(1)}, bf16[128,896]{1,0:T(8,128)(2,1)S(1)}, u32[]{:S(2)}, u32[]{:S(2)}) collective-permute-start(bf16[128,896]{1,0:T(8,128)(2,1)S(1)} %collective-permute-done.1.refs_0_), channel_id=1, source_target_pairs={{0,1},{1,0},{2,3},{3,2},{4,5},{5,4},{6,7},{7,6},{8,9},{9,8},{10,11... | collective-permute-start | bytes 688136 | tf_op jit(solution)/shard_map/ppermute | solution.py:259
  28.2 7.9 %collective-permute-start.8 = (bf16[128,896]{1,0:T(8,128)(2,1)S(1)}, bf16[128,896]{1,0:T(8,128)(2,1)S(1)}, u32[]{:S(2)}, u32[]{:S(2)}) collective-permute-start(bf16[128,896]{1,0:T(8,128)(2,1)S(1)} %collective-permute-done.7.refs_2_), channel_id=1, source_target_pairs={{0,1},{1,0},{2,3},{3,2},{4,5},{5,4},{6,7},{7,6},{8,9},{9,8},{10,11... | collective-permute-start | bytes 688136 | tf_op jit(solution)/shard_map/ppermute | solution.py:259
  31.3 4.7 %collective-permute-start.5 = (bf16[128,896]{1,0:T(8,128)(2,1)S(1)}, bf16[128,896]{1,0:T(8,128)(2,1)S(1)}, u32[]{:S(2)}, u32[]{:S(2)}) collective-permute-start(bf16[128,896]{1,0:T(8,128)(2,1)S(1)} %collective-permute-done.4.refs_1_), channel_id=1, source_target_pairs={{0,1},{1,0},{2,3},{3,2},{4,5},{5,4},{6,7},{7,6},{8,9},{9,8},{10,11... | collective-permute-start | bytes 688136 | tf_op jit(solution)/shard_map/ppermute | solution.py:259
  34.8 1.5 %collective-permute-start.14 = (bf16[128,896]{1,0:T(8,128)(2,1)S(1)}, bf16[128,896]{1,0:T(8,128)(2,1)S(1)}, u32[]{:S(2)}, u32[]{:S(2)}) collective-permute-start(bf16[128,896]{1,0:T(8,128)(2,1)S(1)} %collective-permute-done.10.refs_3_), channel_id=1, source_target_pairs={{0,1},{1,0},{2,3},{3,2},{4,5},{5,4},{6,7},{7,6},{8,9},{9,8},{10,11... | collective-permute-start | bytes 688136 | tf_op jit(solution)/shard_map/ppermute | solution.py:259
  38.6 2.6 %collective-permute-start.16 = (bf16[264,896]{1,0:T(8,128)(2,1)S(1)}, bf16[264,896]{1,0:T(8,128)(2,1)S(1)}, u32[]{:S(2)}, u32[]{:S(2)}) collective-permute-start(bf16[264,896]{1,0:T(8,128)(2,1)S(1)} %shard_map.119), channel_id=1, source_target_pairs={{0,1},{1,0},{2,3},{3,2},{4,5},{5,4},{6,7},{7,6},{8,9},{9,8},{10,11... | collective-permute-start | bytes 1419272 | tf_op jit(solution)/shard_map/ppermute | solution.py:259
  39.9 6.6 %collective-permute-start.15 = (bf16[256,896]{1,0:T(8,128)(2,1)S(1)}, bf16[256,896]{1,0:T(8,128)(2,1)S(1)}, u32[]{:S(2)}, u32[]{:S(2)}) collective-permute-start(bf16[256,896]{1,0:T(8,128)(2,1)S(1)} %shard_map.117), channel_id=1, source_target_pairs={{0,1},{1,0},{2,3},{3,2},{4,5},{5,4},{6,7},{7,6},{8,9},{9,8},{10,11... | collective-permute-start | bytes 1376264 | tf_op jit(solution)/shard_map/ppermute | solution.py:259
  41.3 6.3 %collective-permute-start.20 = (bf16[72,896]{1,0:T(8,128)(2,1)S(1)}, bf16[72,896]{1,0:T(8,128)(2,1)S(1)}, u32[]{:S(2)}, u32[]{:S(2)}) collective-permute-start(bf16[72,896]{1,0:T(8,128)(2,1)S(1)} %get-tuple-element.84), channel_id=1, source_target_pairs={{0,2},{1,3},{2,0},{3,1},{4,6},{5,7},{6,4},{7,5},{8,10},{9,11},{10,... | collective-permute-start | bytes 387080 | tf_op jit(solution)/shard_map/ppermute | solution.py:259
  42.8 11.7 %collective-permute-start.19 = (bf16[72,896]{1,0:T(8,128)(2,1)S(1)}, bf16[72,896]{1,0:T(8,128)(2,1)S(1)}, u32[]{:S(2)}, u32[]{:S(2)}) collective-permute-start(bf16[72,896]{1,0:T(8,128)(2,1)S(1)} %get-tuple-element.83), channel_id=1, source_target_pairs={{0,2},{1,3},{2,0},{3,1},{4,6},{5,7},{6,4},{7,5},{8,10},{9,11},{10,... | collective-permute-start | bytes 387080 | tf_op jit(solution)/shard_map/ppermute | solution.py:259
  43.4 11.2 %collective-permute-start.18 = (bf16[72,896]{1,0:T(8,128)(2,1)S(1)}, bf16[72,896]{1,0:T(8,128)(2,1)S(1)}, u32[]{:S(2)}, u32[]{:S(2)}) collective-permute-start(bf16[72,896]{1,0:T(8,128)(2,1)S(1)} %get-tuple-element.77), channel_id=1, source_target_pairs={{0,2},{1,3},{2,0},{3,1},{4,6},{5,7},{6,4},{7,5},{8,10},{9,11},{10,... | collective-permute-start | bytes 387080 | tf_op jit(solution)/shard_map/ppermute | solution.py:259
  45.8 12.5 %collective-permute-start.17 = (bf16[72,896]{1,0:T(8,128)(2,1)S(1)}, bf16[72,896]{1,0:T(8,128)(2,1)S(1)}, u32[]{:S(2)}, u32[]{:S(2)}) collective-permute-start(bf16[72,896]{1,0:T(8,128)(2,1)S(1)} %get-tuple-element.75), channel_id=1, source_target_pairs={{0,2},{1,3},{2,0},{3,1},{4,6},{5,7},{6,4},{7,5},{8,10},{9,11},{10,... | collective-permute-start | bytes 387080 | tf_op jit(solution)/shard_map/ppermute | solution.py:259
  47.8 10.5 %collective-permute-start.23 = (bf16[72,896]{1,0:T(8,128)(2,1)S(1)}, bf16[72,896]{1,0:T(8,128)(2,1)S(1)}, u32[]{:S(2)}, u32[]{:S(2)}) collective-permute-start(bf16[72,896]{1,0:T(8,128)(2,1)S(1)} %shard_map.124), channel_id=1, source_target_pairs={{0,12},{4,8},{8,4},{12,0},{1,13},{5,9},{9,5},{13,1},{2,14},{6,10},... | collective-permute-start | bytes 387080 | tf_op jit(solution)/shard_map/ppermute | solution.py:256
  54.5 7.4 %collective-permute-start.22 = (bf16[72,896]{1,0:T(8,128)(2,1)S(1)}, bf16[72,896]{1,0:T(8,128)(2,1)S(1)}, u32[]{:S(2)}, u32[]{:S(2)}) collective-permute-start(bf16[72,896]{1,0:T(8,128)(2,1)S(1)} %shard_map.123), channel_id=1, source_target_pairs={{0,8},{4,12},{8,0},{12,4},{1,9},{5,13},{9,1},{13,5},{2,10},{6,14},... | collective-permute-start | bytes 387080 | tf_op jit(solution)/shard_map/ppermute | solution.py:256
  54.8 7.2 %collective-permute-start.21 = (bf16[72,896]{1,0:T(8,128)(2,1)S(1)}, bf16[72,896]{1,0:T(8,128)(2,1)S(1)}, u32[]{:S(2)}, u32[]{:S(2)}) collective-permute-start(bf16[72,896]{1,0:T(8,128)(2,1)S(1)} %shard_map.122), channel_id=1, source_target_pairs={{0,4},{4,0},{8,12},{12,8},{1,5},{5,1},{9,13},{13,9},{2,6},{6,2},{1... | collective-permute-start | bytes 387080 | tf_op jit(solution)/shard_map/ppermute | solution.py:256
  (2 other events, 17.1 us)

commit v7 on v6

--- a/solution.py
+++ b/solution.py
@@ -41,16 +41,19 @@
     )(*args)
 
 
-def slots_of(ids, expert, capacity):
+def slots_of(ids, groups, capacity):
+    me = lax.axis_index("node")
     tokens = ids.shape[1]
-    routed = jnp.max((ids == expert).astype(F32), axis=0, keepdims=True)
+    row = lax.broadcasted_iota(jnp.int32, (8, tokens), 0)
+    expert = jnp.where(row < groups, me ^ row, -1)
+    routed = jnp.where((ids[0:1] == expert) | (ids[1:2] == expert), 1.0, 0.0)
     before = (
         lax.broadcasted_iota(jnp.int32, (tokens, tokens), 0)
         < lax.broadcasted_iota(jnp.int32, (tokens, tokens), 1)
     ).astype(BF16)
-    position = dot_nn(jnp.broadcast_to(routed, (8, tokens)).astype(BF16), before)[0:1]
+    position = jnp.where(routed > 0.0, dot_nn(routed.astype(BF16), before), -1.0)
     slot = lax.broadcasted_iota(jnp.int32, (capacity, tokens), 0).astype(F32)
-    return jnp.where((slot == position) & (routed > 0.0), 1.0, 0.0)
+    return [jnp.where(slot == position[shift : shift + 1], 1.0, 0.0) for shift in range(groups)]
 
 
 def pack_kernel(groups, *refs):
@@ -64,7 +67,7 @@
     copies[1].wait()
     ids = ids_ref[...]
     capacity = ids.shape[1] // 2
-    one_hots = [slots_of(ids, me ^ shift, capacity) for shift in range(groups)]
+    one_hots = slots_of(ids, groups, capacity)
     copies[2].wait()
     for one_hot, out in zip(one_hots, outs):
         out[:capacity] = dot_nn(one_hot.astype(BF16), hidden_ref[...]).astype(BF16)
@@ -76,11 +79,9 @@
 
 
 def pick_kernel(groups, ids_ref, out_ref):
-    me = lax.axis_index("node")
     ids = ids_ref[...]
     capacity = ids.shape[1] // 2
-    for shift in range(groups):
-        chosen = slots_of(ids, me ^ shift, capacity)
+    for shift, chosen in enumerate(slots_of(ids, groups, capacity)):
         out_ref[:, shift * capacity : (shift + 1) * capacity] = chosen.T.astype(BF16)
 
 
@@ -190,7 +191,8 @@
     out[capacity:, capacity:] = jnp.zeros((EXTRA, out.shape[1] - capacity), BF16)
 
 
-def grad_kernel(tiles, left_ref, local_ref, other_ref, across_ref, out_ref, mark_ref, held_ref, sems):
+def grad_kernel(tiles, left_ref, local_ref, other_ref, across_ref, out_ref, *rest):
+    marks, (held_ref, sems) = rest[:-2], rest[-2:]
     me = lax.axis_index("expert")
     width = other_ref.shape[1]
     pieces = ((local_ref, (me // 2) * 2), (other_ref, me ^ 2), (across_ref, me ^ 3))
@@ -203,12 +205,13 @@
         copies.append(pltpu.make_async_copy(held, out_ref.at[0, :, columns], sems.at[index]))
         copies[-1].start()
         held_from += size
-    mark_ref[...] = jnp.zeros(mark_ref.shape, F32)
+    for mark_ref in marks:
+        mark_ref[...] = jnp.zeros(mark_ref.shape, F32)
     for copy in copies:
         copy.wait()
 
 
-def weight_grad(left, pieces):
+def weight_grad(left, pieces, mark=True):
     units, features = left.shape[0], sum(piece.shape[1] for piece in pieces)
     tiles = [
         (which, start, min(512, piece.shape[1] - start))
@@ -216,9 +219,9 @@
     ]
     return pl.pallas_call(
         functools.partial(grad_kernel, tiles),
-        out_shape=[jax.ShapeDtypeStruct((1, units, features), BF16), jax.ShapeDtypeStruct((8, 128), F32)],
+        out_shape=[jax.ShapeDtypeStruct((1, units, features), BF16)] + [jax.ShapeDtypeStruct((8, 128), F32)] * mark,
         in_specs=[pl.BlockSpec(memory_space=pltpu.VMEM)] * 4,
-        out_specs=[pl.BlockSpec(memory_space=pltpu.HBM), pl.BlockSpec(memory_space=pltpu.VMEM)],
+        out_specs=[pl.BlockSpec(memory_space=pltpu.HBM)] + [pl.BlockSpec(memory_space=pltpu.VMEM)] * mark,
         scratch_shapes=[pltpu.VMEM((units, features), BF16), pltpu.SemaphoreType.DMA((len(tiles),))],
         compiler_params=pltpu.CompilerParams(vmem_limit_bytes=10 * MIB),
         cost_estimate=pl.CostEstimate(flops=0, bytes_accessed=0, transcendentals=0),
@@ -293,7 +296,8 @@
         [shape((units, rows), F32)] * 3 + [shape((rows, 2 * width), BF16)] * 2,
         *own, *partner, *mats, flops=3 * dense // 2, nbytes=3 * units * features,
     )
-    across.append(over_expert(after((other[-1], sums[0]))[0], 1))
+    pick = call(functools.partial(pick_kernel, groups), [shape((tokens, rows), BF16)], after((ids, own[1]))[0])[0]
+    across.append(over_expert(after((other[-1], sums[0], pick))[0], 1))
     *sums, rows_other, grads_other = call(
         functools.partial(side_kernel, groups),
         [shape((units, rows), F32)] * 3 + [shape((rows, width), BF16)] * 2,
@@ -340,9 +344,8 @@
     totals[0] = call(functools.partial(join_kernel, 0), [shape((capacity + EXTRA, width), BF16)],
                      near_keep, near_got, crossed[0], stat_pair, marks[1])[0]
     back[0] = totals[0]
-    weight_grads[2], marks[2] = weight_grad(after((hid, back[3]))[0], rows_grad)
-
-    pick = call(functools.partial(pick_kernel, groups), [shape((tokens, rows), BF16)], after((ids, own[1]))[0])[0]
+    weight_grads[2] = weight_grad(after((hid, back[3]))[0], rows_grad, mark=False)[0]
+
     grad_in, grad_gates = call(
         functools.partial(finish_kernel, groups),
         [shape((tokens, width), BF16), shape(ids.shape, F32)],

time: 63 us -> 63.1 us (level)
    ppermute x6, waiting for transfers between devices: 7.03 us -> 7.95 us  [over_node(): return lax.ppermute(x, 'node', [(i, i ^ shift) for i in range(groups)])]
  transfers between devices with their start and end apart: 24 -> 24, of which waited for: 8 -> 8; matrix products, arithmetic and copies ran while one was open for 0% -> 0% of each run, Pallas kernels for 32% -> 31%
where the time goes in v7:
time: 63.1 us; the launch traced here: 62.9 us
  Pallas kernels  24.3 us (39%)
  starting transfers between devices  22 us (35%)
  waiting for transfers between devices  15.8 us (25%)
  between operations  0.84 us (1%)
    pallas_call x16, Pallas kernels, call(): pl.pallas_call(kernel, out_shape=outs, in_specs=[pl.BlockSpec(memory_spac...  16.6 us
    ppermute x18, starting transfers between devices, over_expert(): lax.ppermute(x, 'expert', [(i, i ^ relative) for i in range(experts)])  11.7 us
    ppermute x6, starting transfers between devices, over_node(): return lax.ppermute(x, 'node', [(i, i ^ shift) for i in range(groups)])  10.2 us
    ppermute x6, waiting for transfers between devices, over_node(): return lax.ppermute(x, 'node', [(i, i ^ shift) for i in range(groups)])  7.95 us
    ppermute x18, waiting for transfers between devices, over_expert(): lax.ppermute(x, 'expert', [(i, i ^ relative) for i in range(experts)])  7.83 us
    pallas_call x3, Pallas kernels, weight_grad(): pl.pallas_call(functools.partial(grad_kernel, tiles), out_shape=[jax.Shap...  7.62 us
  transfers between devices with their start and end apart: 24, of which 8 were waited for; matrix products, arithmetic and copies ran while one was open for 0% of the time, Pallas kernels for 31%

profile of v7, /device:TPU:0, one launch (start us, length us, event | category | flops | bytes accessed | tf_op | source)
XLA Modules:
  0.0 62.9 jit_solution(12285051893440824280)
XLA Ops:
  0.6 1.6 %shard_map.110 = (bf16[128,896]{1,0:T(8,128)(2,1)S(1)}, bf16[128,896]{1,0:T(8,128)(2,1)S(1)}, bf16[128,896]{1,0:T(8,128)(2,1)S(1)}, bf16[128,896]{1,0:T(8,128)(2,1)S(1)}) custom-call(s32[2,128]{1,0:T(2,128)} %bitcast.3, bf16[2,128]{1,0:T(2,128)(2,1)} %bitcast.6, bf16[128,896]{1,0:T(8,128)(2,1)} %refs_2_.1, bf16[128,896]{1,0:T(8,128)(2,1)} %refs_3_.1), custom_call_target="tpu_custom_call" | custom-call | flops 117440512 | bytes 688128 | tf_op jit(solution)/shard_map/pallas_call | solution.py:31
  2.8 3.7 %collective-permute-start.6 = (bf16[128,896]{1,0:T(8,128)(2,1)S(1)}, bf16[128,896]{1,0:T(8,128)(2,1)S(1)}, u32[]{:S(2)}, u32[]{:S(2)}) collective-permute-start(bf16[128,896]{1,0:T(8,128)(2,1)S(1)} %get-tuple-element.58), channel_id=1, source_target_pairs={{0,8},{4,12},{8,0},{12,4},{1,9},{5,13},{9,1},{13,5},{2,10},{6,14},... | collective-permute-start | bytes 688136 | tf_op jit(solution)/shard_map/ppermute | solution.py:259
  6.4 1.6 %collective-permute-start = (bf16[128,896]{1,0:T(8,128)(2,1)S(1)}, bf16[128,896]{1,0:T(8,128)(2,1)S(1)}, u32[]{:S(2)}, u32[]{:S(2)}) collective-permute-start(bf16[128,896]{1,0:T(8,128)(2,1)S(1)} %get-tuple-element.50), channel_id=1, source_target_pairs={{0,4},{4,0},{8,12},{12,8},{1,5},{5,1},{9,13},{13,9},{2,6},{6,2},{1... | collective-permute-start | bytes 688136 | tf_op jit(solution)/shard_map/ppermute | solution.py:259
  8.0 1.5 %collective-permute-start.1 = (bf16[128,896]{1,0:T(8,128)(2,1)S(1)}, bf16[128,896]{1,0:T(8,128)(2,1)S(1)}, u32[]{:S(2)}, u32[]{:S(2)}) collective-permute-start(bf16[128,896]{1,0:T(8,128)(2,1)S(1)} %get-tuple-element.52.refs_0_), channel_id=1, source_target_pairs={{0,2},{1,3},{2,0},{3,1},{4,6},{5,7},{6,4},{7,5},{8,10},{9,11},{10,... | collective-permute-start | bytes 688136 | tf_op jit(solution)/shard_map/ppermute | solution.py:262
  9.7 4.8 %shard_map.112 = (bf16[1,608,3584]{2,1,0:T(8,128)(2,1)S(1)}, bf16[1,608,3584]{2,1,0:T(8,128)(2,1)S(1)}, bf16[1,608,3584]{2,1,0:T(8,128)(2,1)S(1)}) custom-call(bf16[1,608,3584]{2,1,0:T(8,128)(2,1)} %refs_0_, bf16[1,608,3584]{2,1,0:T(8,128)(2,1)} %refs_1_, bf16[1,608,3584]{2,1,0:T(8,128)(2,1)} %refs_2_.2), custom_call_target="tpu_custom_call" | custom-call | bytes 26148864 | tf_op jit(solution)/shard_map/pallas_call | solution.py:31
  14.6 3.3 %collective-permute-done.6.refs_2_ = bf16[128,896]{1,0:T(8,128)(2,1)S(1)} collective-permute-done((bf16[128,896]{1,0:T(8,128)(2,1)S(1)}, bf16[128,896]{1,0:T(8,128)(2,1)S(1)}, u32[]{:S(2)}, u32[]{:S(2)}) %collective-permute-start.6) | collective-permute-done | bytes 229408 | tf_op jit(solution)/shard_map/ppermute | solution.py:259
  17.8 1.8 %collective-permute-start.7 = (bf16[128,896]{1,0:T(8,128)(2,1)S(1)}, bf16[128,896]{1,0:T(8,128)(2,1)S(1)}, u32[]{:S(2)}, u32[]{:S(2)}) collective-permute-start(bf16[128,896]{1,0:T(8,128)(2,1)S(1)} %collective-permute-done.6.refs_2_), channel_id=1, source_target_pairs={{0,2},{1,3},{2,0},{3,1},{4,6},{5,7},{6,4},{7,5},{8,10},{9,11},{10,... | collective-permute-start | bytes 688136 | tf_op jit(solution)/shard_map/ppermute | solution.py:262
  20.4 3.3 %collective-permute-done.9.refs_3_ = bf16[128,896]{1,0:T(8,128)(2,1)S(1)} collective-permute-done((bf16[128,896]{1,0:T(8,128)(2,1)S(1)}, bf16[128,896]{1,0:T(8,128)(2,1)S(1)}, u32[]{:S(2)}, u32[]{:S(2)}) %collective-permute-start.9) | collective-permute-done | bytes 229408 | tf_op jit(solution)/shard_map/ppermute | solution.py:259
  23.7 2.7 %collective-permute-done.7.refs_2_ = bf16[128,896]{1,0:T(8,128)(2,1)S(1)} collective-permute-done((bf16[128,896]{1,0:T(8,128)(2,1)S(1)}, bf16[128,896]{1,0:T(8,128)(2,1)S(1)}, u32[]{:S(2)}, u32[]{:S(2)}) %collective-permute-start.7) | collective-permute-done | bytes 229408 | tf_op jit(solution)/shard_map/ppermute | solution.py:262
  26.4 1.8 %collective-permute-start.10 = (bf16[128,896]{1,0:T(8,128)(2,1)S(1)}, bf16[128,896]{1,0:T(8,128)(2,1)S(1)}, u32[]{:S(2)}, u32[]{:S(2)}) collective-permute-start(bf16[128,896]{1,0:T(8,128)(2,1)S(1)} %collective-permute-done.9.refs_3_), channel_id=1, source_target_pairs={{0,2},{1,3},{2,0},{3,1},{4,6},{5,7},{6,4},{7,5},{8,10},{9,11},{10,... | collective-permute-start | bytes 688136 | tf_op jit(solution)/shard_map/ppermute | solution.py:262
  29.1 2.2 %collective-permute-done.4.refs_1_ = bf16[128,896]{1,0:T(8,128)(2,1)S(1)} collective-permute-done((bf16[128,896]{1,0:T(8,128)(2,1)S(1)}, bf16[128,896]{1,0:T(8,128)(2,1)S(1)}, u32[]{:S(2)}, u32[]{:S(2)}) %collective-permute-start.4) | collective-permute-done | bytes 229408 | tf_op jit(solution)/shard_map/ppermute | solution.py:262
  31.3 2.0 %shard_map.113 = (f32[608,256]{1,0:T(8,128)S(1)}, f32[608,256]{1,0:T(8,128)S(1)}, f32[608,256]{1,0:T(8,128)S(1)}, bf16[256,1792]{1,0:T(8,128)(2,1)S(1)}, bf16[256,1792]{1,0:T(8,128)(2,1)S(1)}) custom-call(bf16[128,896]{1,0:T(8,128)(2,1)S(1)} %get-tuple-element.52.refs_0_, bf16[128,896]{1,0:T(8,128)(2,1)S(1)} %collective-permute-done.refs_1_, ...), custom_call_target="tpu_custom_call" | custom-call | flops 1673527296 | bytes 6537216 | tf_op jit(solution)/shard_map/pallas_call | solution.py:31
  33.3 1.5 %collective-permute-done.10.refs_3_ = bf16[128,896]{1,0:T(8,128)(2,1)S(1)} collective-permute-done((bf16[128,896]{1,0:T(8,128)(2,1)S(1)}, bf16[128,896]{1,0:T(8,128)(2,1)S(1)}, u32[]{:S(2)}, u32[]{:S(2)}) %collective-permute-start.10) | collective-permute-done | bytes 229408 | tf_op jit(solution)/shard_map/ppermute | solution.py:262
  34.8 1.2 %shard_map.114 = (f32[608,256]{1,0:T(8,128)S(1)}, f32[608,256]{1,0:T(8,128)S(1)}, f32[608,256]{1,0:T(8,128)S(1)}, bf16[256,896]{1,0:T(8,128)(2,1)S(1)}, bf16[256,896]{1,0:T(8,128)(2,1)S(1)}) custom-call(bf16[128,896]{1,0:T(8,128)(2,1)S(1)} %collective-permute-done.1.refs_0_, bf16[128,896]{1,0:T(8,128)(2,1)S(1)} %collective-permute-done.4.refs_1_, ...), custom_call_target="tpu_custom_call" | custom-call | flops 836763648 | bytes 3268608 | tf_op jit(solution)/shard_map/pallas_call | solution.py:31
  36.3 1.3 %shard_map.115 = (bf16[256,896]{1,0:T(8,128)(2,1)S(1)}, bf16[256,896]{1,0:T(8,128)(2,1)S(1)}, bf16[608,256]{1,0:T(8,128)(2,1)S(1)}, bf16[608,256]{1,0:T(8,128)(2...) custom-call(bf16[128,896]{1,0:T(8,128)(2,1)S(1)} %collective-permute-done.2.refs_0_, ...), custom_call_target="tpu_custom_call" | custom-call | flops 836763648 | bytes 3268608 | tf_op jit(solution)/shard_map/pallas_call | solution.py:31
  37.6 1.0 %shard_map.119 = bf16[264,896]{1,0:T(8,128)(2,1)S(1)} custom-call(bf16[608,256]{1,0:T(8,128)(2,1)S(1)} %get-tuple-element.77.dgate_ref.left_ref, bf16[608,256]{1,0:T(8,128)(2,1)S(1)} %get-tuple-element.84.dup_ref.left_ref, bf16[1,608,3584]{2,1,0:T(8,128)(2,1)S(1)} %get-tuple-element.56.refs_8_.refs_4_.gate_w, ...), custom_call_target="tpu_custom_call" | custom-call | flops 557842432 | bytes 2179072 | tf_op jit(solution)/shard_map/pallas_call | solution.py:31
  41.3 1.5 %collective-permute-start.20 = (bf16[72,896]{1,0:T(8,128)(2,1)S(1)}, bf16[72,896]{1,0:T(8,128)(2,1)S(1)}, u32[]{:S(2)}, u32[]{:S(2)}) collective-permute-start(bf16[72,896]{1,0:T(8,128)(2,1)S(1)} %get-tuple-element.83), channel_id=1, source_target_pairs={{0,2},{1,3},{2,0},{3,1},{4,6},{5,7},{6,4},{7,5},{8,10},{9,11},{10,... | collective-permute-start | bytes 387080 | tf_op jit(solution)/shard_map/ppermute | solution.py:262
  43.4 1.4 %collective-permute-start.18 = (bf16[72,896]{1,0:T(8,128)(2,1)S(1)}, bf16[72,896]{1,0:T(8,128)(2,1)S(1)}, u32[]{:S(2)}, u32[]{:S(2)}) collective-permute-start(bf16[72,896]{1,0:T(8,128)(2,1)S(1)} %get-tuple-element.76), channel_id=1, source_target_pairs={{0,2},{1,3},{2,0},{3,1},{4,6},{5,7},{6,4},{7,5},{8,10},{9,11},{10,... | collective-permute-start | bytes 387080 | tf_op jit(solution)/shard_map/ppermute | solution.py:262
  46.5 1.2 %collective-permute-done.20.crossed = bf16[72,896]{1,0:T(8,128)(2,1)S(1)} collective-permute-done((bf16[72,896]{1,0:T(8,128)(2,1)S(1)}, bf16[72,896]{1,0:T(8,128)(2,1)S(1)}, u32[]{:S(2)}, u32[]{:S(2)}) %collective-permute-start.20) | collective-permute-done | bytes 129056 | tf_op jit(solution)/shard_map/ppermute | solution.py:262
  47.8 4.1 %collective-permute-start.23 = (bf16[72,896]{1,0:T(8,128)(2,1)S(1)}, bf16[72,896]{1,0:T(8,128)(2,1)S(1)}, u32[]{:S(2)}, u32[]{:S(2)}) collective-permute-start(bf16[72,896]{1,0:T(8,128)(2,1)S(1)} %shard_map.124), channel_id=1, source_target_pairs={{0,12},{4,8},{8,4},{12,0},{1,13},{5,9},{9,5},{13,1},{2,14},{6,10},... | collective-permute-start | bytes 387080 | tf_op jit(solution)/shard_map/ppermute | solution.py:259
  51.9 2.5 %shard_map.121 = (bf16[1,608,3584]{2,1,0:T(8,128)(2,1)}, f32[8,128]{1,0:T(8,128)S(1)}) custom-call(bf16[608,256]{1,0:T(8,128)(2,1)S(1)} %get-tuple-element.77.dgate_ref.left_ref, bf16[256,1792]{1,0:T(8,128)(2,1)S(1)} %get-tuple-element.78.local_ref, bf16[256,896]{1,0:T(8,128)(2,1)S(1)} %get-tuple-element.79.other_ref, ...), custom_call_target="tpu_custom_call" | custom-call | tf_op jit(solution)/shard_map/pallas_call | solution.py:220
  55.4 2.5 %shard_map.125 = (bf16[1,608,3584]{2,1,0:T(8,128)(2,1)}, f32[8,128]{1,0:T(8,128)S(1)}) custom-call(bf16[608,256]{1,0:T(8,128)(2,1)S(1)} %get-tuple-element.84.dup_ref.left_ref, bf16[256,1792]{1,0:T(8,128)(2,1)S(1)} %get-tuple-element.78.local_ref, bf16[256,896]{1,0:T(8,128)(2,1)S(1)} %get-tuple-element.79.other_ref, ...), custom_call_target="tpu_custom_call" | custom-call | tf_op jit(solution)/shard_map/pallas_call | solution.py:220
  58.0 2.5 %shard_map.128 = bf16[1,608,3584]{2,1,0:T(8,128)(2,1)} custom-call(bf16[608,256]{1,0:T(8,128)(2,1)S(1)} %get-tuple-element.91.left_ref, bf16[256,1792]{1,0:T(8,128)(2,1)S(1)} %get-tuple-element.92.local_ref, bf16[256,896]{1,0:T(8,128)(2,1)S(1)} %get-tuple-element.93.other_ref, bf16[256,896]{1,0:T(8,128)(2,1)S(1)} %get-tuple-element.94.across_ref), custom_call_target="tpu_custom_call" | custom-call | tf_op jit(solution)/shard_map/pallas_call | solution.py:220
  60.6 1.4 %collective-permute-done.22.refs_2_ = bf16[72,896]{1,0:T(8,128)(2,1)S(1)} collective-permute-done((bf16[72,896]{1,0:T(8,128)(2,1)S(1)}, bf16[72,896]{1,0:T(8,128)(2,1)S(1)}, u32[]{:S(2)}, u32[]{:S(2)}) %collective-permute-start.22) | collective-permute-done | bytes 129056 | tf_op jit(solution)/shard_map/ppermute | solution.py:259
  (47 shorter events, 9.7 us)
Async XLA Ops:
  2.2 7.5 %collective-permute-start.3 = (bf16[128,896]{1,0:T(8,128)(2,1)S(1)}, bf16[128,896]{1,0:T(8,128)(2,1)S(1)}, u32[]{:S(2)}, u32[]{:S(2)}) collective-permute-start(bf16[128,896]{1,0:T(8,128)(2,1)S(1)} %get-tuple-element.52.refs_0_), channel_id=1, source_target_pairs={{0,1},{1,0},{2,3},{3,2},{4,5},{5,4},{6,7},{7,6},{8,9},{9,8},{10,11... | collective-permute-start | bytes 688136 | tf_op jit(solution)/shard_map/ppermute | solution.py:262
  2.8 15.1 %collective-permute-start.6 = (bf16[128,896]{1,0:T(8,128)(2,1)S(1)}, bf16[128,896]{1,0:T(8,128)(2,1)S(1)}, u32[]{:S(2)}, u32[]{:S(2)}) collective-permute-start(bf16[128,896]{1,0:T(8,128)(2,1)S(1)} %get-tuple-element.58), channel_id=1, source_target_pairs={{0,8},{4,12},{8,0},{12,4},{1,9},{5,13},{9,1},{13,5},{2,10},{6,14},... | collective-permute-start | bytes 688136 | tf_op jit(solution)/shard_map/ppermute | solution.py:259
  6.4 13.2 %collective-permute-start = (bf16[128,896]{1,0:T(8,128)(2,1)S(1)}, bf16[128,896]{1,0:T(8,128)(2,1)S(1)}, u32[]{:S(2)}, u32[]{:S(2)}) collective-permute-start(bf16[128,896]{1,0:T(8,128)(2,1)S(1)} %get-tuple-element.50), channel_id=1, source_target_pairs={{0,4},{4,0},{8,12},{12,8},{1,5},{5,1},{9,13},{13,9},{2,6},{6,2},{1... | collective-permute-start | bytes 688136 | tf_op jit(solution)/shard_map/ppermute | solution.py:259
  8.0 11.6 %collective-permute-start.1 = (bf16[128,896]{1,0:T(8,128)(2,1)S(1)}, bf16[128,896]{1,0:T(8,128)(2,1)S(1)}, u32[]{:S(2)}, u32[]{:S(2)}) collective-permute-start(bf16[128,896]{1,0:T(8,128)(2,1)S(1)} %get-tuple-element.52.refs_0_), channel_id=1, source_target_pairs={{0,2},{1,3},{2,0},{3,1},{4,6},{5,7},{6,4},{7,5},{8,10},{9,11},{10,... | collective-permute-start | bytes 688136 | tf_op jit(solution)/shard_map/ppermute | solution.py:262
  9.5 14.2 %collective-permute-start.9 = (bf16[128,896]{1,0:T(8,128)(2,1)S(1)}, bf16[128,896]{1,0:T(8,128)(2,1)S(1)}, u32[]{:S(2)}, u32[]{:S(2)}) collective-permute-start(bf16[128,896]{1,0:T(8,128)(2,1)S(1)} %get-tuple-element.60), channel_id=1, source_target_pairs={{0,12},{4,8},{8,4},{12,0},{1,13},{5,9},{9,5},{13,1},{2,14},{6,10},... | collective-permute-start | bytes 688136 | tf_op jit(solution)/shard_map/ppermute | solution.py:259
  17.8 8.5 %collective-permute-start.7 = (bf16[128,896]{1,0:T(8,128)(2,1)S(1)}, bf16[128,896]{1,0:T(8,128)(2,1)S(1)}, u32[]{:S(2)}, u32[]{:S(2)}) collective-permute-start(bf16[128,896]{1,0:T(8,128)(2,1)S(1)} %collective-permute-done.6.refs_2_), channel_id=1, source_target_pairs={{0,2},{1,3},{2,0},{3,1},{4,6},{5,7},{6,4},{7,5},{8,10},{9,11},{10,... | collective-permute-start | bytes 688136 | tf_op jit(solution)/shard_map/ppermute | solution.py:262
  19.6 8.9 %collective-permute-start.11 = (bf16[128,896]{1,0:T(8,128)(2,1)S(1)}, bf16[128,896]{1,0:T(8,128)(2,1)S(1)}, u32[]{:S(2)}, u32[]{:S(2)}) collective-permute-start(bf16[128,896]{1,0:T(8,128)(2,1)S(1)} %collective-permute-done.refs_1_), channel_id=1, source_target_pairs={{0,1},{1,0},{2,3},{3,2},{4,5},{5,4},{6,7},{7,6},{8,9},{9,8},{10,11... | collective-permute-start | bytes 688136 | tf_op jit(solution)/shard_map/ppermute | solution.py:262
  19.6 8.9 %collective-permute-start.12 = (bf16[128,896]{1,0:T(8,128)(2,1)S(1)}, bf16[128,896]{1,0:T(8,128)(2,1)S(1)}, u32[]{:S(2)}, u32[]{:S(2)}) collective-permute-start(bf16[128,896]{1,0:T(8,128)(2,1)S(1)} %collective-permute-done.6.refs_2_), channel_id=1, source_target_pairs={{0,1},{1,0},{2,3},{3,2},{4,5},{5,4},{6,7},{7,6},{8,9},{9,8},{10,11... | collective-permute-start | bytes 688136 | tf_op jit(solution)/shard_map/ppermute | solution.py:262
  20.1 11.1 %collective-permute-start.4 = (bf16[128,896]{1,0:T(8,128)(2,1)S(1)}, bf16[128,896]{1,0:T(8,128)(2,1)S(1)}, u32[]{:S(2)}, u32[]{:S(2)}) collective-permute-start(bf16[128,896]{1,0:T(8,128)(2,1)S(1)} %collective-permute-done.refs_1_), channel_id=1, source_target_pairs={{0,2},{1,3},{2,0},{3,1},{4,6},{5,7},{6,4},{7,5},{8,10},{9,11},{10,... | collective-permute-start | bytes 688136 | tf_op jit(solution)/shard_map/ppermute | solution.py:262
  23.7 7.6 %collective-permute-start.13 = (bf16[128,896]{1,0:T(8,128)(2,1)S(1)}, bf16[128,896]{1,0:T(8,128)(2,1)S(1)}, u32[]{:S(2)}, u32[]{:S(2)}) collective-permute-start(bf16[128,896]{1,0:T(8,128)(2,1)S(1)} %collective-permute-done.9.refs_3_), channel_id=1, source_target_pairs={{0,1},{1,0},{2,3},{3,2},{4,5},{5,4},{6,7},{7,6},{8,9},{9,8},{10,11... | collective-permute-start | bytes 688136 | tf_op jit(solution)/shard_map/ppermute | solution.py:262
  26.4 8.4 %collective-permute-start.10 = (bf16[128,896]{1,0:T(8,128)(2,1)S(1)}, bf16[128,896]{1,0:T(8,128)(2,1)S(1)}, u32[]{:S(2)}, u32[]{:S(2)}) collective-permute-start(bf16[128,896]{1,0:T(8,128)(2,1)S(1)} %collective-permute-done.9.refs_3_), channel_id=1, source_target_pairs={{0,2},{1,3},{2,0},{3,1},{4,6},{5,7},{6,4},{7,5},{8,10},{9,11},{10,... | collective-permute-start | bytes 688136 | tf_op jit(solution)/shard_map/ppermute | solution.py:262
  28.5 7.5 %collective-permute-start.2 = (bf16[128,896]{1,0:T(8,128)(2,1)S(1)}, bf16[128,896]{1,0:T(8,128)(2,1)S(1)}, u32[]{:S(2)}, u32[]{:S(2)}) collective-permute-start(bf16[128,896]{1,0:T(8,128)(2,1)S(1)} %collective-permute-done.1.refs_0_), channel_id=1, source_target_pairs={{0,1},{1,0},{2,3},{3,2},{4,5},{5,4},{6,7},{7,6},{8,9},{9,8},{10,11... | collective-permute-start | bytes 688136 | tf_op jit(solution)/shard_map/ppermute | solution.py:262
  28.6 7.4 %collective-permute-start.8 = (bf16[128,896]{1,0:T(8,128)(2,1)S(1)}, bf16[128,896]{1,0:T(8,128)(2,1)S(1)}, u32[]{:S(2)}, u32[]{:S(2)}) collective-permute-start(bf16[128,896]{1,0:T(8,128)(2,1)S(1)} %collective-permute-done.7.refs_2_), channel_id=1, source_target_pairs={{0,1},{1,0},{2,3},{3,2},{4,5},{5,4},{6,7},{7,6},{8,9},{9,8},{10,11... | collective-permute-start | bytes 688136 | tf_op jit(solution)/shard_map/ppermute | solution.py:262
  31.3 4.7 %collective-permute-start.5 = (bf16[128,896]{1,0:T(8,128)(2,1)S(1)}, bf16[128,896]{1,0:T(8,128)(2,1)S(1)}, u32[]{:S(2)}, u32[]{:S(2)}) collective-permute-start(bf16[128,896]{1,0:T(8,128)(2,1)S(1)} %collective-permute-done.4.refs_1_), channel_id=1, source_target_pairs={{0,1},{1,0},{2,3},{3,2},{4,5},{5,4},{6,7},{7,6},{8,9},{9,8},{10,11... | collective-permute-start | bytes 688136 | tf_op jit(solution)/shard_map/ppermute | solution.py:262
  34.8 1.5 %collective-permute-start.14 = (bf16[128,896]{1,0:T(8,128)(2,1)S(1)}, bf16[128,896]{1,0:T(8,128)(2,1)S(1)}, u32[]{:S(2)}, u32[]{:S(2)}) collective-permute-start(bf16[128,896]{1,0:T(8,128)(2,1)S(1)} %collective-permute-done.10.refs_3_), channel_id=1, source_target_pairs={{0,1},{1,0},{2,3},{3,2},{4,5},{5,4},{6,7},{7,6},{8,9},{9,8},{10,11... | collective-permute-start | bytes 688136 | tf_op jit(solution)/shard_map/ppermute | solution.py:262
  38.6 2.6 %collective-permute-start.16 = (bf16[264,896]{1,0:T(8,128)(2,1)S(1)}, bf16[264,896]{1,0:T(8,128)(2,1)S(1)}, u32[]{:S(2)}, u32[]{:S(2)}) collective-permute-start(bf16[264,896]{1,0:T(8,128)(2,1)S(1)} %shard_map.119), channel_id=1, source_target_pairs={{0,1},{1,0},{2,3},{3,2},{4,5},{5,4},{6,7},{7,6},{8,9},{9,8},{10,11... | collective-permute-start | bytes 1419272 | tf_op jit(solution)/shard_map/ppermute | solution.py:262
  39.9 6.6 %collective-permute-start.15 = (bf16[256,896]{1,0:T(8,128)(2,1)S(1)}, bf16[256,896]{1,0:T(8,128)(2,1)S(1)}, u32[]{:S(2)}, u32[]{:S(2)}) collective-permute-start(bf16[256,896]{1,0:T(8,128)(2,1)S(1)} %shard_map.117), channel_id=1, source_target_pairs={{0,1},{1,0},{2,3},{3,2},{4,5},{5,4},{6,7},{7,6},{8,9},{9,8},{10,11... | collective-permute-start | bytes 1376264 | tf_op jit(solution)/shard_map/ppermute | solution.py:262
  41.3 6.3 %collective-permute-start.20 = (bf16[72,896]{1,0:T(8,128)(2,1)S(1)}, bf16[72,896]{1,0:T(8,128)(2,1)S(1)}, u32[]{:S(2)}, u32[]{:S(2)}) collective-permute-start(bf16[72,896]{1,0:T(8,128)(2,1)S(1)} %get-tuple-element.83), channel_id=1, source_target_pairs={{0,2},{1,3},{2,0},{3,1},{4,6},{5,7},{6,4},{7,5},{8,10},{9,11},{10,... | collective-permute-start | bytes 387080 | tf_op jit(solution)/shard_map/ppermute | solution.py:262
  42.8 11.7 %collective-permute-start.19 = (bf16[72,896]{1,0:T(8,128)(2,1)S(1)}, bf16[72,896]{1,0:T(8,128)(2,1)S(1)}, u32[]{:S(2)}, u32[]{:S(2)}) collective-permute-start(bf16[72,896]{1,0:T(8,128)(2,1)S(1)} %get-tuple-element.82), channel_id=1, source_target_pairs={{0,2},{1,3},{2,0},{3,1},{4,6},{5,7},{6,4},{7,5},{8,10},{9,11},{10,... | collective-permute-start | bytes 387080 | tf_op jit(solution)/shard_map/ppermute | solution.py:262
  43.4 11.2 %collective-permute-start.18 = (bf16[72,896]{1,0:T(8,128)(2,1)S(1)}, bf16[72,896]{1,0:T(8,128)(2,1)S(1)}, u32[]{:S(2)}, u32[]{:S(2)}) collective-permute-start(bf16[72,896]{1,0:T(8,128)(2,1)S(1)} %get-tuple-element.76), channel_id=1, source_target_pairs={{0,2},{1,3},{2,0},{3,1},{4,6},{5,7},{6,4},{7,5},{8,10},{9,11},{10,... | collective-permute-start | bytes 387080 | tf_op jit(solution)/shard_map/ppermute | solution.py:262
  45.8 12.1 %collective-permute-start.17 = (bf16[72,896]{1,0:T(8,128)(2,1)S(1)}, bf16[72,896]{1,0:T(8,128)(2,1)S(1)}, u32[]{:S(2)}, u32[]{:S(2)}) collective-permute-start(bf16[72,896]{1,0:T(8,128)(2,1)S(1)} %get-tuple-element.74), channel_id=1, source_target_pairs={{0,2},{1,3},{2,0},{3,1},{4,6},{5,7},{6,4},{7,5},{8,10},{9,11},{10,... | collective-permute-start | bytes 387080 | tf_op jit(solution)/shard_map/ppermute | solution.py:262
  47.8 10.2 %collective-permute-start.23 = (bf16[72,896]{1,0:T(8,128)(2,1)S(1)}, bf16[72,896]{1,0:T(8,128)(2,1)S(1)}, u32[]{:S(2)}, u32[]{:S(2)}) collective-permute-start(bf16[72,896]{1,0:T(8,128)(2,1)S(1)} %shard_map.124), channel_id=1, source_target_pairs={{0,12},{4,8},{8,4},{12,0},{1,13},{5,9},{9,5},{13,1},{2,14},{6,10},... | collective-permute-start | bytes 387080 | tf_op jit(solution)/shard_map/ppermute | solution.py:259
  54.5 7.4 %collective-permute-start.22 = (bf16[72,896]{1,0:T(8,128)(2,1)S(1)}, bf16[72,896]{1,0:T(8,128)(2,1)S(1)}, u32[]{:S(2)}, u32[]{:S(2)}) collective-permute-start(bf16[72,896]{1,0:T(8,128)(2,1)S(1)} %shard_map.123), channel_id=1, source_target_pairs={{0,8},{4,12},{8,0},{12,4},{1,9},{5,13},{9,1},{13,5},{2,10},{6,14},... | collective-permute-start | bytes 387080 | tf_op jit(solution)/shard_map/ppermute | solution.py:259
  54.8 7.2 %collective-permute-start.21 = (bf16[72,896]{1,0:T(8,128)(2,1)S(1)}, bf16[72,896]{1,0:T(8,128)(2,1)S(1)}, u32[]{:S(2)}, u32[]{:S(2)}) collective-permute-start(bf16[72,896]{1,0:T(8,128)(2,1)S(1)} %shard_map.122), channel_id=1, source_target_pairs={{0,4},{4,0},{8,12},{12,8},{1,5},{5,1},{9,13},{13,9},{2,6},{6,2},{1... | collective-permute-start | bytes 387080 | tf_op jit(solution)/shard_map/ppermute | solution.py:259
  (2 other events, 22.7 us)
